TPU v7x, 256 devices: a whole 4x4x8 slice. The times are simulated.
256 devices in a mesh: dp: 4 (over y_hi, core), space: 64 (over y_lo, z, x).
Axes of the slice: x: 4, y: 4 (y_hi: 2, y_lo: 2; y = y_hi * 2 + y_lo), z: 8, core: 2. Of those that a mesh axis runs over, the one named last changes fastest.
Arguments:
- field: bfloat16 [4, 128, 64, 128, 128], P('dp', 'space'), may hold values from -6 to 6
- cotangent: bfloat16 [4, 128, 64, 128, 128], P('dp', 'space'), may hold values from -6 to 6
- mode_weight: bfloat16 [256, 16, 64, 64], P('space'), may hold values from -3 to 3
- point_weight: bfloat16 [64, 64], replicated, may hold values from -0.75 to 0.75
- point_bias: float32 [64], replicated, may hold values from -3 to 3
Outputs:
- field_grad: bfloat16 [4, 128, 64, 128, 128], P('dp', 'space')
- mode_grad: float32 [256, 16, 64, 64], P('space', 'dp')
All inputs are finite; a program needn't handle non-finite values.
Results may differ from a plain program's by a relative error of at most 0.012.
Values may be sent and summed in bfloat16 or wider, within the bound.
No kernel may reach another device: no remote copies, remote signals or barrier semaphores. Data moves between devices by JAX's collectives and lax.ppermute only.
A program may use at most 128 MiB of HBM per device.

v0:
```python
import math

import jax
import jax.numpy as jnp
import numpy as np
from jax import lax
from jax.experimental import pallas as pl
from jax.experimental.pallas import tpu as pltpu
from jax.sharding import PartitionSpec as P

BF = jnp.bfloat16
F32 = jnp.float32

C = 64
M = 16
N = 128
XL = 2
XC = XL * C
PAIRS = M * M
OWN = 4
GROUPS = 64
G = 16


def basis(length, count):
    points = np.arange(length)[:, None]
    order = np.arange(count)[None, :]
    freq = (order + 1) // 2
    phase = (points * freq % length).astype(np.float32) * np.float32(2.0 * math.pi / length)
    cosine = np.logical_or(order % 2 == 1, order == 0)
    table = np.where(cosine, np.cos(phase), np.sin(phase)) * np.float32(math.sqrt(2.0 / length))
    return table.astype(np.float32)


def split(table):
    high = table.astype(BF)
    return high, (table - high.astype(np.float32)).astype(BF)


def tables():
    base = basis(N, M)
    table_z = base.astype(BF)
    forward_y = np.concatenate([np.kron(np.eye(2, dtype=np.float32), part.astype(np.float32).T) for part in split(base)])
    back_y = np.concatenate(split(base), axis=1)
    by_plane = base.reshape(GROUPS, XL, M)
    along_x = np.einsum("sxm,pq->xpmsq", by_plane, np.eye(OWN, dtype=np.float32)).reshape(XL * OWN * M, GROUPS * OWN)
    back_z = np.kron(np.eye(M, dtype=np.float32), table_z.astype(np.float32).T)
    return dict(
        forward_y=forward_y.astype(BF),
        back_y=back_y.astype(BF),
        forward_z=np.ascontiguousarray(table_z.T),
        back_z=back_z.astype(BF),
        along_x=along_x,
        back_x=np.ascontiguousarray(along_x.T),
    )


def y_modes(group, forward_y, scratch, row):
    block = jnp.concatenate(
        [jnp.concatenate(group[0:2], axis=0), jnp.concatenate(group[2:4], axis=0)], axis=1
    )
    both = jnp.dot(forward_y, block, preferred_element_type=F32)
    modes = both[: 2 * M] + both[2 * M :]
    scratch[pl.ds(row, 2 * M), :] = modes[:, :N]
    scratch[pl.ds(row + 2 * M, 2 * M), :] = modes[:, N:]


def z_modes(scratch, forward_z, out_ref):
    for a in range(M):
        part = scratch[pl.ds(a, XC, stride=M), :].astype(BF)
        out_ref[M * a : M * (a + 1), :] = lax.dot_general(
            forward_z, part, (((1,), (1,)), ((), ())), preferred_element_type=F32
        ).astype(out_ref.dtype)


def from_z_modes(modes, back_z, scratch):
    wide = lax.dot_general(modes, back_z, (((0,), (0,)), ((), ())), preferred_element_type=F32)
    for a in range(M):
        scratch[pl.ds(a, XC, stride=M), :] = wide[:, N * a : N * (a + 1)]


def from_y_modes(scratch, back_y, row):
    pair = jnp.concatenate(
        [scratch[pl.ds(row, M), :].astype(BF), scratch[pl.ds(row + M, M), :].astype(BF)], axis=1
    )
    return jnp.dot(back_y, jnp.concatenate([pair, pair], axis=0), preferred_element_type=F32)


def to_modes_kernel(field_ref, forward_y_ref, forward_z_ref, out_ref, scratch):
    step = pl.program_id(0)
    for g in range(0, G, 4):
        group = [field_ref[g + k] for k in range(4)]
        y_modes(group, forward_y_ref[...], scratch, (step * G + g) * M)

    @pl.when(step == XC // G - 1)
    def _():
        z_modes(scratch, forward_z_ref[...], out_ref)


def slope_kernel(
    spatial_ref, back_z_ref, back_y_ref, forward_y_ref, forward_z_ref, point_ref, cot_ref,
    slope_ref, out_ref, spread, scratch,
):
    step = pl.program_id(0)
    root = math.sqrt(2.0 / math.pi)

    @pl.when(step == 0)
    def _():
        from_z_modes(spatial_ref[...], back_z_ref[...], spread)

    for g in range(0, G, 4):
        group = []
        for k in range(0, 4, 2):
            both = from_y_modes(spread, back_y_ref[...], (step * G + g + k) * M)
            for h in range(2):
                pre = both[:, N * h : N * (h + 1)] + point_ref[g + k + h].astype(F32)
                square = pre * pre
                tanh = jnp.tanh(pre * (root + (root * 0.044715) * square))
                outer = pre * (root + (root * 3 * 0.044715) * square)
                slope = (0.5 + 0.5 * tanh) * (1.0 + outer * (1.0 - tanh))
                slope = (slope * cot_ref[g + k + h].astype(F32)).astype(BF)
                slope_ref[g + k + h] = slope
                group.append(slope)
        y_modes(group, forward_y_ref[...], scratch, (step * G + g) * M)

    @pl.when(step == XC // G - 1)
    def _():
        z_modes(scratch, forward_z_ref[...], out_ref)


def result_kernel(back_ref, back_z_ref, back_y_ref, point_ref, out_ref, spread):
    step = pl.program_id(0)

    @pl.when(step == 0)
    def _():
        from_z_modes(back_ref[...], back_z_ref[...], spread)

    for g in range(0, G, 2):
        both = from_y_modes(spread, back_y_ref[...], (step * G + g) * M)
        for h in range(2):
            out_ref[g + h] = (both[:, N * h : N * (h + 1)] + point_ref[g + h].astype(F32)).astype(BF)


ROWS = 16
YB = 32


def point_kernel(weight_ref, spread_ref, bias_ref, in_ref, out_ref, wide):
    size = C * ROWS

    @pl.when(pl.program_id(0) == 0)
    def _():
        rows = jnp.dot(spread_ref[...], weight_ref[...], preferred_element_type=F32).astype(BF)
        for k in range(0, size, 256):
            all_of = lax.dot_general(
                rows[k : k + 256], spread_ref[...], (((1,), (1,)), ((), ())), preferred_element_type=F32
            )
            row = lax.broadcasted_iota(jnp.int32, (256, size), 0)
            column = lax.broadcasted_iota(jnp.int32, (256, size), 1)
            wide[k : k + 256, :] = jnp.where(row % ROWS == column % ROWS, all_of, 0.0).astype(BF)

    for y in range(0, YB, 2 * ROWS):
        block = jnp.concatenate(
            [in_ref[0, :, y + k * ROWS : y + (k + 1) * ROWS, :].reshape(size, N) for k in range(2)], axis=1
        )
        for k in range(0, size, 256):
            part = jnp.dot(wide[k : k + 256, :], block, preferred_element_type=F32)
            bias = bias_ref[k : k + 256, :]
            chan = k // ROWS
            for h in range(2):
                out_ref[0, chan : chan + 256 // ROWS, y + h * ROWS : y + (h + 1) * ROWS, :] = (
                    (part[:, N * h : N * (h + 1)] + bias).astype(BF).reshape(256 // ROWS, ROWS, N)
                )


def x_modes(received, along_x):
    both = jnp.dot(along_x, received.astype(F32), precision=lax.Precision.HIGHEST, preferred_element_type=F32)
    half = OWN * M
    lane = lax.broadcasted_iota(jnp.int32, (half, XC), 1)
    picked = jnp.where(lane < C, both[:half], both[half:])
    return picked + pltpu.roll(picked, C, 1)


def from_x_modes(twice, back_x):
    lane = lax.broadcasted_iota(jnp.int32, (OWN * M, XC), 1)
    stacked = jnp.concatenate([jnp.where(lane < C, twice, 0.0), jnp.where(lane < C, 0.0, twice)], axis=0)
    return jnp.dot(back_x, stacked, precision=lax.Precision.HIGHEST, preferred_element_type=F32)


def mix_kernel(received_ref, along_x_ref, back_x_ref, weight_ref, out_ref, spectrum_ref):
    spectrum = x_modes(received_ref[...], along_x_ref[...]).astype(BF)
    spectrum_ref[...] = spectrum
    lane = lax.broadcasted_iota(jnp.int32, (OWN * M, XC), 1)
    row = lax.broadcasted_iota(jnp.int32, (OWN * M, XC), 0) % M
    wide = spectrum.astype(F32)
    spread = jnp.concatenate(
        [jnp.where(lane // C + 2 * k == row, wide, 0.0).astype(BF) for k in range(M // 2)], axis=1
    )
    mixed = jnp.concatenate(
        [
            jnp.dot(spread[M * p : M * (p + 1)], weight_ref[p], preferred_element_type=F32)
            for p in range(OWN)
        ],
        axis=0,
    )
    twice = jnp.concatenate([mixed, mixed], axis=1)
    out_ref[...] = from_x_modes(twice, back_x_ref[...]).astype(out_ref.dtype)


def mix_back_kernel(received_ref, along_x_ref, back_x_ref, weight_ref, spectrum_ref, out_ref, both_ref):
    hat = x_modes(received_ref[...], along_x_ref[...]).astype(BF)
    lane = lax.broadcasted_iota(jnp.int32, (OWN * M, XC), 1)
    both_ref[...] = jnp.where(lane < C, spectrum_ref[...].astype(F32), hat.astype(F32)).astype(BF)
    lane = lax.broadcasted_iota(jnp.int32, (M, XC), 1)
    row = lax.broadcasted_iota(jnp.int32, (M, XC), 0)
    parts = []
    for p in range(OWN):
        every = lax.dot_general(
            hat[M * p : M * (p + 1), :C], weight_ref[p], (((1,), (1,)), ((), ())), preferred_element_type=F32
        )
        total = sum(
            jnp.where(lane // C + 2 * k == row, every[:, XC * k : XC * (k + 1)], 0.0) for k in range(M // 2)
        )
        parts.append(total + pltpu.roll(total, C, 1))
    out_ref[...] = from_x_modes(jnp.concatenate(parts, axis=0), back_x_ref[...]).astype(out_ref.dtype)


def whole(shape):
    return pl.BlockSpec(shape, lambda *unused: (0,) * len(shape))


def planes(*unused):
    return pl.BlockSpec((G, N, N), lambda i: (i, 0, 0))


def params(mib):
    return pltpu.CompilerParams(vmem_limit_bytes=mib * 1024 * 1024)


def cost(flops, size):
    return pl.CostEstimate(flops=flops, bytes_accessed=size, transcendentals=0)


BIG = jax.ShapeDtypeStruct((XC, N, N), BF)
SMALL = jax.ShapeDtypeStruct((PAIRS, XC), BF)
ALL_BYTES = XC * N * N * 2


def to_modes(field, table):
    return pl.pallas_call(
        to_modes_kernel,
        grid=(XC // G,),
        in_specs=[planes(), whole((4 * M, 2 * N)), whole((M, N))],
        out_specs=whole((PAIRS, XC)),
        out_shape=SMALL,
        scratch_shapes=[pltpu.VMEM((XC * M, N), F32)],
        compiler_params=params(60),
        cost_estimate=cost(XC * N * N * 128, ALL_BYTES),
        name="to_modes",
    )(field, table["forward_y"], table["forward_z"])


def slopes(spatial, point, cot, table):
    return pl.pallas_call(
        slope_kernel,
        grid=(XC // G,),
        in_specs=[
            whole((PAIRS, XC)), whole((PAIRS, M * N)), whole((N, 2 * M)), whole((4 * M, 2 * N)),
            whole((M, N)), planes(), planes(),
        ],
        out_specs=(planes(), whole((PAIRS, XC))),
        out_shape=(BIG, SMALL),
        scratch_shapes=[pltpu.VMEM((XC * M, N), F32)] * 2,
        compiler_params=params(60),
        cost_estimate=cost(XC * N * N * 256, 3 * ALL_BYTES),
        name="slopes",
    )(spatial, table["back_z"], table["back_y"], table["forward_y"], table["forward_z"], point, cot)


def result(back, point, table):
    return pl.pallas_call(
        result_kernel,
        grid=(XC // G,),
        in_specs=[whole((PAIRS, XC)), whole((PAIRS, M * N)), whole((N, 2 * M)), planes()],
        out_specs=planes(),
        out_shape=BIG,
        scratch_shapes=[pltpu.VMEM((XC * M, N), F32)],
        compiler_params=params(60),
        cost_estimate=cost(XC * N * N * 128, 2 * ALL_BYTES),
        name="result",
    )(back, table["back_z"], table["back_y"], point)


def pointwise(weight, bias, array):
    size = C * ROWS
    spread = np.kron(np.eye(C, dtype=np.float32), np.ones((ROWS, 1), np.float32)).astype(BF)
    rows = jnp.broadcast_to(bias[:, None, None], (C, ROWS, N)).reshape(size, N)
    block = pl.BlockSpec((1, C, YB, N), lambda i: (i // (N // YB), 0, i % (N // YB), 0))
    return pl.pallas_call(
        point_kernel,
        grid=(XL * (N // YB),),
        in_specs=[whole((C, C)), whole((size, C)), whole((size, N)), block],
        out_specs=block,
        out_shape=jax.ShapeDtypeStruct((XL, C, N, N), BF),
        scratch_shapes=[pltpu.VMEM((size, size), BF)],
        compiler_params=params(60),
        cost_estimate=cost(XC * N * N * 2048, 2 * ALL_BYTES),
        name="pointwise",
    )(weight, spread, rows, array.reshape(XL, C, N, N)).reshape(XC, N, N)


def mix(received, weight, table):
    return pl.pallas_call(
        mix_kernel,
        out_shape=(SMALL, jax.ShapeDtypeStruct((OWN * M, XC), BF)),
        compiler_params=params(60),
        cost_estimate=cost(1 << 27, 1 << 21),
        name="mix",
    )(received, table["along_x"], table["back_x"], weight)


def mix_back(received, weight, spectrum, table):
    return pl.pallas_call(
        mix_back_kernel,
        out_shape=(SMALL, jax.ShapeDtypeStruct((OWN * M, XC), BF)),
        compiler_params=params(60),
        cost_estimate=cost(1 << 27, 1 << 21),
        name="mix_back",
    )(received, table["along_x"], table["back_x"], weight, spectrum)


def exchange(array):
    cut = array.reshape(GROUPS, OWN, XC)
    return lax.all_to_all(cut, "space", split_axis=0, concat_axis=0, tiled=True).reshape(PAIRS, XC)


def per_device(field, cotangent, mode_weight, point_weight, point_bias):
    table = {name: jnp.asarray(value) for name, value in tables().items()}
    sample = field.reshape(XC, N, N)
    cot = cotangent.reshape(XC, N, N)
    weight = mode_weight.reshape(OWN, M * C, C)

    received = exchange(to_modes(sample, table))
    point = pointwise(point_weight.T, point_bias, sample)
    spatial, spectrum = mix(received, weight, table)
    slope, grad_modes = slopes(exchange(spatial), point, cot, table)
    received = exchange(grad_modes)
    point_back = pointwise(point_weight, jnp.zeros((C,), F32), slope)
    back, both = mix_back(received, weight, spectrum, table)
    back = exchange(back)
    every = lax.all_gather(both, "dp").reshape(4, OWN, M, 2, C)
    mine = lax.dynamic_slice_in_dim(every, lax.axis_index("dp") * (M // 4), M // 4, axis=2)
    mode_grad = jnp.einsum("spmi,spmo->pmio", mine[:, :, :, 0], mine[:, :, :, 1], preferred_element_type=F32)
    field_grad = result(back, point_back, table)
    return field_grad.reshape(1, XL, C, N, N), mode_grad


def solution(mesh):
    return jax.shard_map(
        per_device,
        mesh=mesh,
        in_specs=(
            P("dp", "space", None, None, None),
            P("dp", "space", None, None, None),
            P("space", None, None, None),
            P(),
            P(),
        ),
        out_specs=(P("dp", "space", None, None, None), P("space", "dp", None, None)),
        check_vma=False,
    )
```

profile of v0, /device:TPU:16, one launch (start us, length us, event | category | flops | bytes accessed | tf_op | source)
XLA Modules:
  0.0 122.0 jit_solution(8791257964960194644)
XLA Ops:
  0.6 0.0 copy-start.4
  0.6 0.0 copy-start.5
  0.7 6.4 %to_modes.1 = bf16[256,128]{1,0:T(8,128)(2,1)} custom-call(bf16[128,128,128]{2,1,0:T(8,128)(2,1)} %bitcast.25, bf16[64,256]{1,0:T(8,128)(2,1)} %constant.28.clone.forward_y_ref, bf16[16,128]{1,0:T(8,128)(2,1)} %constant.30.clone.forward_z_ref), custom_call_target="tpu_custom_call" | custom-call | flops 268435456 | bytes 4194304 | tf_op jit(solution)/shard_map/to_modes/pallas_call | solution.py:250
  7.0 12.7 %all-to-all-start = ((bf16[64,4,128]{2,1,0:T(4,128)(2,1)}), bf16[64,4,128]{2,1,0:T(4,128)(2,1)S(1)}, u32[]{:S(2)}, u32[]{:S(2)}) async-start(bf16[64,4,128]{2,1,0:T(4,128)(2,1)} %bitcast.33), calls=%async_computation | async-start | bytes 131072 | tf_op jit(solution)/shard_map/all_to_all | solution.py:334
  19.7 0.0 copy-done.4
  19.7 0.7 copy.17
  20.4 0.0 copy-done.5
  20.4 0.1 broadcast_in_dim.10
  20.5 0.1 broadcast_in_dim.11
  20.6 9.9 %all-to-all-done = bf16[64,4,128]{2,1,0:T(4,128)(2,1)S(1)} async-done(((bf16[64,4,128]{2,1,0:T(4,128)(2,1)}), bf16[64,4,128]{2,1,0:T(4,128)(2,1)S(1)}, u32[]{:S(2)}, u32[]{:S(2)}) %all-to-all-start) | async-done | bytes 65568 | tf_op jit(solution)/shard_map/all_to_all | solution.py:334
  30.5 0.6 copy-done.3
  31.1 3.1 %mix.1 = (bf16[256,128]{1,0:T(8,128)(2,1)}, bf16[64,128]{1,0:T(8,128)(2,1)}) custom-call(bf16[256,128]{1,0:T(8,128)(2,1)} %bitcast.35, f32[128,256]{1,0:T(8,128)} %constant.32.clone.along_x_ref, f32[256,128]{1,0:T(8,128)} %constant.33.clone.back_x_ref, bf16[4,1024,64]{2,1,0:T(8,128)(2,1)} %bitcast.29), custom_call_target="tpu_custom_call" | custom-call | flops 134217728 | bytes 2097152 | tf_op jit(solution)/shard_map/mix/pallas_call | solution.py:313
  34.2 4.6 %all-to-all-start.1 = ((bf16[64,4,128]{2,1,0:T(4,128)(2,1)}), bf16[64,4,128]{2,1,0:T(4,128)(2,1)S(1)}, u32[]{:S(2)}, u32[]{:S(2)}) async-start(bf16[64,4,128]{2,1,0:T(4,128)(2,1)} %bitcast.36), calls=%async_computation.1 | async-start | bytes 131072 | tf_op jit(solution)/shard_map/all_to_all | solution.py:334
  38.8 1.0 broadcast_in_dim.12.bias_ref
  39.8 10.5 %pointwise.2 = bf16[2,64,128,128]{3,2,1,0:T(8,128)(2,1)} custom-call(bf16[64,64]{1,0:T(8,128)(2,1)} %bitcast.39, bf16[1024,64]{1,0:T(8,128)(2,1)} %constant.34.clone.spread_ref, f32[1024,128]{1,0:T(8,128)} %broadcast_in_dim.12.bias_ref, bf16[2,64,128,128]{3,2,1,0:T(8,128)(2,1)} %bitcast.26), custom_call_target="tpu_custom_call" | custom-call | flops 4294967296 | bytes 8388608 | tf_op jit(solution)/shard_map/pointwise/pallas_call | solution.py:299
  50.2 0.0 all-to-all-done.1
  50.2 0.6 copy-done
  50.9 13.8 %slopes.1 = (bf16[128,128,128]{2,1,0:T(8,128)(2,1)}, bf16[256,128]{1,0:T(8,128)(2,1)}) custom-call(bf16[256,128]{1,0:T(8,128)(2,1)} %bitcast.31, bf16[256,2048]{1,0:T(8,128)(2,1)} %constant.31.clone.back_z_ref, bf16[128,32]{1,0:T(8,128)(2,1)} %constant.29.clone.back_y_ref, bf16[64,256]{1,0:T(8,128)(2,1)} %constant.28.clone.forward_y_ref, ...), custom_call_target="tpu_custom_call" | custom-call | flops 536870912 | bytes 12582912 | tf_op jit(solution)/shard_map/slopes/pallas_call | solution.py:264
  64.7 11.3 %all-to-all-start.2 = ((bf16[64,4,128]{2,1,0:T(4,128)(2,1)}), bf16[64,4,128]{2,1,0:T(4,128)(2,1)S(1)}, u32[]{:S(2)}, u32[]{:S(2)}) async-start(bf16[64,4,128]{2,1,0:T(4,128)(2,1)} %bitcast.38), calls=%async_computation.2 | async-start | bytes 131072 | tf_op jit(solution)/shard_map/all_to_all | solution.py:334
  76.0 0.8 reshape.70.bias_ref
  76.8 10.5 %pointwise.3 = bf16[2,64,128,128]{3,2,1,0:T(8,128)(2,1)} custom-call(bf16[64,64]{1,0:T(8,128)(2,1)} %weight_ref.1, bf16[1024,64]{1,0:T(8,128)(2,1)} %constant.34.clone.spread_ref, f32[1024,128]{1,0:T(8,128)} %reshape.70.bias_ref, bf16[2,64,128,128]{3,2,1,0:T(8,128)(2,1)} %bitcast.40), custom_call_target="tpu_custom_call" | custom-call | flops 4294967296 | bytes 8388608 | tf_op jit(solution)/shard_map/pointwise/pallas_call | solution.py:299
  87.3 0.0 all-to-all-done.2
  87.3 0.6 copy-done.2
  88.0 3.1 %mix_back.1 = (bf16[256,128]{1,0:T(8,128)(2,1)}, bf16[64,128]{1,0:T(8,128)(2,1)}) custom-call(bf16[256,128]{1,0:T(8,128)(2,1)} %bitcast.34, f32[128,256]{1,0:T(8,128)} %constant.32.clone.along_x_ref, f32[256,128]{1,0:T(8,128)} %constant.33.clone.back_x_ref, bf16[4,1024,64]{2,1,0:T(8,128)(2,1)} %bitcast.30, bf16[64,128]{1,0:T(8,128)(2,1)} %get-tuple-element.10.spectrum_ref), custom_call_target="tpu_custom_call" | custom-call | flops 134217728 | bytes 2097152 | tf_op jit(solution)/shard_map/mix_back/pallas_call | solution.py:323
  91.0 11.3 %all-to-all-start.3 = ((bf16[64,4,128]{2,1,0:T(4,128)(2,1)}), bf16[64,4,128]{2,1,0:T(4,128)(2,1)S(1)}, u32[]{:S(2)}, u32[]{:S(2)}) async-start(bf16[64,4,128]{2,1,0:T(4,128)(2,1)} %bitcast.37), calls=%async_computation.3 | async-start | bytes 131072 | tf_op jit(solution)/shard_map/all_to_all | solution.py:334
  102.3 7.0 %all-gather = bf16[256,128]{1,0:T(8,128)(2,1)S(1)} all-gather(bf16[64,128]{1,0:T(8,128)(2,1)} %get-tuple-element.13), channel_id=2, replica_groups=mesh['dp'=4,'space'=64] {'dp'}, dimensions={0}, use_global_device_ids=true | all-gather | bytes 81920 | tf_op jit(solution)/shard_map/all_gather | solution.py:351
  109.4 0.1 reshape.74
  109.5 0.1 constant_dynamic-slice_fusion
  109.5 1.1 fusion
  110.6 2.5 %all-to-all-done.3 = bf16[64,4,128]{2,1,0:T(4,128)(2,1)S(1)} async-done(((bf16[64,4,128]{2,1,0:T(4,128)(2,1)}), bf16[64,4,128]{2,1,0:T(4,128)(2,1)S(1)}, u32[]{:S(2)}, u32[]{:S(2)}) %all-to-all-start.3) | async-done | bytes 65568 | tf_op jit(solution)/shard_map/all_to_all | solution.py:334
  113.1 0.6 copy-done.1
  113.7 8.3 %result.1 = bf16[128,128,128]{2,1,0:T(8,128)(2,1)} custom-call(bf16[256,128]{1,0:T(8,128)(2,1)} %bitcast.32, bf16[256,2048]{1,0:T(8,128)(2,1)} %constant.31.clone.back_z_ref, bf16[128,32]{1,0:T(8,128)(2,1)} %constant.29.clone.back_y_ref, bf16[128,128,128]{2,1,0:T(8,128)(2,1)} %bitcast.23), custom_call_target="tpu_custom_call" | custom-call | flops 268435456 | bytes 8388608 | tf_op jit(solution)/shard_map/result/pallas_call | solution.py:281
  (4 shorter events, 0.0 us)
Async XLA Ops:
  0.6 19.1 %copy-start.4 = (bf16[64,64]{1,0:T(8,128)(2,1)S(1)}, bf16[64,64]{1,0:T(8,128)(2,1)}, u32[]{:S(2)}) copy-start(bf16[64,64]{1,0:T(8,128)(2,1)} %weight_ref.1) | copy-start | bytes 24580
  0.6 19.8 %copy-start.5 = (f32[64]{0:T(128)S(1)}, f32[64]{0:T(128)}, u32[]{:S(2)}) copy-start(f32[64]{0:T(128)} %param.17) | copy-start | bytes 772
  7.0 23.4 %all-to-all-start = ((bf16[64,4,128]{2,1,0:T(4,128)(2,1)}), bf16[64,4,128]{2,1,0:T(4,128)(2,1)S(1)}, u32[]{:S(2)}, u32[]{:S(2)}) async-start(bf16[64,4,128]{2,1,0:T(4,128)(2,1)} %bitcast.33), calls=%async_computation | async-start | bytes 131072 | tf_op jit(solution)/shard_map/all_to_all | solution.py:334
  30.5 0.6 copy-start.3
  34.2 16.1 %all-to-all-start.1 = ((bf16[64,4,128]{2,1,0:T(4,128)(2,1)}), bf16[64,4,128]{2,1,0:T(4,128)(2,1)S(1)}, u32[]{:S(2)}, u32[]{:S(2)}) async-start(bf16[64,4,128]{2,1,0:T(4,128)(2,1)} %bitcast.36), calls=%async_computation.1 | async-start | bytes 131072 | tf_op jit(solution)/shard_map/all_to_all | solution.py:334
  50.2 0.6 copy-start
  64.7 22.6 %all-to-all-start.2 = ((bf16[64,4,128]{2,1,0:T(4,128)(2,1)}), bf16[64,4,128]{2,1,0:T(4,128)(2,1)S(1)}, u32[]{:S(2)}, u32[]{:S(2)}) async-start(bf16[64,4,128]{2,1,0:T(4,128)(2,1)} %bitcast.38), calls=%async_computation.2 | async-start | bytes 131072 | tf_op jit(solution)/shard_map/all_to_all | solution.py:334
  87.3 0.6 copy-start.2
  91.0 22.1 %all-to-all-start.3 = ((bf16[64,4,128]{2,1,0:T(4,128)(2,1)}), bf16[64,4,128]{2,1,0:T(4,128)(2,1)S(1)}, u32[]{:S(2)}, u32[]{:S(2)}) async-start(bf16[64,4,128]{2,1,0:T(4,128)(2,1)} %bitcast.37), calls=%async_computation.3 | async-start | bytes 131072 | tf_op jit(solution)/shard_map/all_to_all | solution.py:334
  113.1 0.6 copy-start.1
where the time goes:
time: 123 us; the launch traced here: 122 us
  Pallas kernels  55.7 us (45%)
  starting transfers between devices  39.8 us (32%)
  waiting for transfers between devices  12.4 us (10%)
  blocking collectives  7.02 us (6%)
  local copies, waits for them, and re-layouts  5.35 us (4%)
    all_to_all x4, starting transfers between devices, exchange(): lax.all_to_all(cut, 'space', split_axis=0, concat_axis=0, tiled=True)  39.8 us
    pallas_call x2, Pallas kernels, pointwise(): pl.pallas_call(point_kernel, grid=(XL * (N // YB),), in_specs=[whole((C,...  21 us
    pallas_call x1, Pallas kernels, slopes(): pl.pallas_call(slope_kernel, grid=(XC // G,), in_specs=[whole((PAIRS, XC)...  13.8 us
    all_to_all x4, waiting for transfers between devices, exchange(): lax.all_to_all(cut, 'space', split_axis=0, concat_axis=0, tiled=True)  12.4 us
    pallas_call x1, Pallas kernels, result(): pl.pallas_call(result_kernel, grid=(XC // G,), in_specs=[whole((PAIRS, XC...  8.32 us
    all_gather x1, blocking collectives, per_device(): every = lax.all_gather(both, 'dp').reshape(4, OWN, M, 2, C)  7.02 us
    pallas_call x1, Pallas kernels, to_modes(): pl.pallas_call(to_modes_kernel, grid=(XC // G,), in_specs=[planes(), whol...  6.39 us
    unnamed x13, local copies, waits for them, and re-layouts  3.21 us
  transfers between devices with their start and end apart: 4, of which 2 were waited for; matrix products, arithmetic and copies ran while one was open for 3% of the time, Pallas kernels for 17%

commit v1 on v0

v1 whole, which is shorter than its diff:
```python
import functools
import math

import jax
import jax.numpy as jnp
import numpy as np
from jax import lax
from jax.experimental import pallas as pl
from jax.experimental.pallas import tpu as pltpu
from jax.sharding import PartitionSpec as P

BF = jnp.bfloat16
F32 = jnp.float32

C = 64
M = 16
N = 128
XL = 2
XC = XL * C
PAIRS = M * M
OWN = 4
GROUPS = 64
CHUNKS = 8
G = XC // CHUNKS


def basis(length, count):
    points = np.arange(length)[:, None]
    order = np.arange(count)[None, :]
    freq = (order + 1) // 2
    phase = (points * freq % length).astype(np.float32) * np.float32(2.0 * math.pi / length)
    cosine = np.logical_or(order % 2 == 1, order == 0)
    table = np.where(cosine, np.cos(phase), np.sin(phase)) * np.float32(math.sqrt(2.0 / length))
    return table.astype(np.float32)


def split(table):
    high = table.astype(BF)
    return high, (table - high.astype(np.float32)).astype(BF)


def tables():
    base = basis(N, M)
    table_z = base.astype(BF)
    forward_y = np.concatenate([np.kron(np.eye(2, dtype=np.float32), part.astype(np.float32).T) for part in split(base)])
    back_y = np.concatenate(split(base), axis=1)
    by_plane = base.reshape(GROUPS, XL, M)
    along_x = np.einsum("sxm,pq->xpmsq", by_plane, np.eye(OWN, dtype=np.float32)).reshape(XL * OWN * M, GROUPS * OWN)
    return dict(
        forward_y=forward_y.astype(BF),
        forward_y_half=(0.5 * forward_y).astype(BF),
        spread=np.kron(np.eye(C, dtype=np.float32), np.ones((ROWS, 1), np.float32)).astype(BF),
        back_y=back_y.astype(BF),
        forward_z=np.ascontiguousarray(table_z.T),
        along_x=along_x,
        back_x=np.ascontiguousarray(along_x.T),
    )


def y_modes(group, forward_y, scratch, row):
    block = jnp.concatenate(
        [jnp.concatenate(group[0:2], axis=0), jnp.concatenate(group[2:4], axis=0)], axis=1
    )
    both = jnp.dot(forward_y, block, preferred_element_type=F32)
    modes = both[: 2 * M] + both[2 * M :]
    scratch[pl.ds(row, 2 * M), :] = modes[:, :N]
    scratch[pl.ds(row + 2 * M, 2 * M), :] = modes[:, N:]


def z_modes(scratch, forward_z, out_ref):
    for a in range(M):
        part = scratch[pl.ds(a, XC, stride=M), :].astype(BF)
        out_ref[M * a : M * (a + 1), :] = lax.dot_general(
            forward_z, part, (((1,), (1,)), ((), ())), preferred_element_type=F32
        ).astype(out_ref.dtype)


def from_z_modes(modes, table_z, scratch):
    for a in range(M):
        scratch[pl.ds(a, XC, stride=M), :] = lax.dot_general(
            modes[M * a : M * (a + 1)], table_z, (((0,), (0,)), ((), ())), preferred_element_type=F32
        )


def from_y_modes(scratch, back_y, row):
    pair = jnp.concatenate(
        [scratch[pl.ds(row, M), :].astype(BF), scratch[pl.ds(row + M, M), :].astype(BF)], axis=1
    )
    return jnp.dot(back_y, jnp.concatenate([pair, pair], axis=0), preferred_element_type=F32)


def fetch(source, target, sems):
    return lambda k: pltpu.make_async_copy(
        source.at[pl.ds(G * k, G)], target.at[pl.ds(G * k, G)], sems.at[k]
    )


def fetch(source, target, sems, first=0):
    return lambda k: pltpu.make_async_copy(
        source.at[pl.ds(G * (k - first), G)], target.at[pl.ds(G * k, G)], sems.at[k]
    )


def fetch_planes(planes, target, sems):
    half = CHUNKS // XL
    copies = [fetch(source, target, sems, half * plane) for plane, source in enumerate(planes)]
    return lambda k: copies[k // half](k)


def to_modes_kernel(field_ref, forward_y_ref, forward_z_ref, out_ref, held, scratch, forward_y, forward_z, sems, own_sems):
    small = [
        pltpu.make_async_copy(forward_y_ref, forward_y, own_sems.at[0]),
        pltpu.make_async_copy(forward_z_ref, forward_z, own_sems.at[1]),
    ]
    copy = fetch(field_ref, held, sems)
    for each in small:
        each.start()
    for k in range(CHUNKS):
        copy(k).start()
    for each in small:
        each.wait()
    for k in range(CHUNKS):
        copy(k).wait()
        for g in range(G * k, G * (k + 1), 4):
            y_modes([held[g + j] for j in range(4)], forward_y[...], scratch, g * M)
    z_modes(scratch, forward_z[...], out_ref)


def doubled_slope(pre, cot):
    root = math.sqrt(2.0 / math.pi)
    square = pre * pre
    tanh = jnp.tanh(pre * (root + (root * 0.044715) * square))
    outer = pre * (root + (root * 3 * 0.044715) * square)
    return (1.0 + tanh) * (1.0 + outer * (1.0 - tanh)) * cot


def slope_kernel(
    spatial_ref, table_z_ref, back_y_ref, forward_y_ref, point0_ref, point1_ref, cot_ref,
    slope_ref, out_ref, spread, scratch, point, cot, slope, sems,
):
    point_copy = fetch_planes((point0_ref, point1_ref), point, sems.at[0])
    cot_copy = fetch(cot_ref, cot, sems.at[1])
    slope_copy = fetch(slope, slope_ref, sems.at[2])
    for k in range(CHUNKS):
        point_copy(k).start()
        cot_copy(k).start()
    from_z_modes(spatial_ref[...], table_z_ref[...], spread)
    last = None
    for first in range(0, XC, 4):
        if first % G == 0:
            point_copy(first // G).wait()
            cot_copy(first // G).wait()
        group = []
        for at in range(first, first + 4, 2):
            both = from_y_modes(spread, back_y_ref[...], at * M).astype(BF)
            for h in range(2):
                value = doubled_slope(both[:, N * h : N * (h + 1)] + point[at + h], cot[at + h])
                slope[at + h] = value
                group.append(value)
        if last is not None:
            y_modes(last, forward_y_ref[...], scratch, (first - 4) * M)
        last = group
        if first % G == G - 4:
            slope_copy(first // G).start()
    y_modes(last, forward_y_ref[...], scratch, (XC - 4) * M)
    z_modes(scratch, table_z_ref[...], out_ref)
    for k in range(CHUNKS):
        slope_copy(k).wait()


def result_kernel(
    back_ref, table_z_ref, back_y_ref, weight_ref, spread_ref, both0_ref, both1_ref, both2_ref, both3_ref,
    point0_ref, slope_ref, out_ref, mode_grad_ref, spread, point, slope, held, wide, grads, sems, row_sems,
):
    half = CHUNKS // XL
    point_copy = fetch(point0_ref, point, sems.at[0])
    out_copy = fetch(held, out_ref, sems.at[1])
    slope_copy = fetch_rows(slope_ref.at[pl.ds(C, C)], slope, row_sems)
    for k in range(half):
        point_copy(k).start()
    for k in range(STEPS):
        slope_copy(k).start()
    from_z_modes(back_ref[...], table_z_ref[...], spread)

    def finish(k):
        for g in range(G * k, G * (k + 1), 2):
            both = from_y_modes(spread, back_y_ref[...], g * M)
            for h in range(2):
                held[g + h] = (both[:, N * h : N * (h + 1)] + point[g + h].astype(F32)).astype(BF)
        out_copy(k).start()

    for k in range(half):
        point_copy(k).wait()
        finish(k)
    widen(weight_ref, spread_ref, wide, False, 0.5)
    for k in range(STEPS):
        slope_copy(k).wait()
        point_rows(slope, wide, None, point.at[pl.ds(C, C)], k)
    for k in range(half, CHUNKS):
        finish(k)
    mode_gradient((both0_ref, both1_ref, both2_ref, both3_ref), grads, mode_grad_ref)
    for k in range(CHUNKS):
        out_copy(k).wait()


def mode_gradient(samples, grads, out_ref):
    quarter = M // len(samples)
    own = lax.axis_index("dp") * quarter
    for s, ref in enumerate(samples):
        grads[s] = ref[...].astype(F32)
    lane = lax.broadcasted_iota(jnp.int32, (M, quarter * C), 1)
    row = lax.broadcasted_iota(jnp.int32, (M, quarter * C), 0)
    for p in range(OWN):
        rows = jnp.concatenate([grads[s, pl.ds(p * M + own, quarter), :] for s in range(len(samples))], axis=0)
        spectrum = jnp.concatenate([rows[:, :C]] * quarter, axis=1)
        spectrum = jnp.where(lane // C == row % quarter, spectrum, 0.0).astype(BF)
        out_ref[p] = lax.dot_general(
            spectrum, rows[:, C:].astype(BF), (((0,), (0,)), ((), ())), preferred_element_type=F32
        ).reshape(quarter, C, C)


ROWS = 8
WIDE = C * ROWS


def widen(weight_ref, spread_ref, wide, transposed, factor):
    rows = lax.dot_general(
        spread_ref[...], weight_ref[...], (((1,), (int(transposed),)), ((), ())), preferred_element_type=F32
    ).astype(BF)
    for k in range(0, WIDE, 128):
        every = lax.dot_general(
            rows[k : k + 128], spread_ref[...], (((1,), (1,)), ((), ())), preferred_element_type=F32
        )
        row = lax.broadcasted_iota(jnp.int32, (128, WIDE), 0)
        column = lax.broadcasted_iota(jnp.int32, (128, WIDE), 1)
        wide[k : k + 128, :] = jnp.where(row % ROWS == column % ROWS, every * factor, 0.0).astype(BF)


YB = 32
STEPS = N // YB


def fetch_rows(source, target, sems):
    def copy(k):
        at = (slice(None), pl.ds(k * YB, YB))
        return pltpu.make_async_copy(source.at[at], target.at[at], sems.at[k])

    return copy


def point_rows(array, wide, bias, out, k):
    size = 256
    for y in range(k * YB, (k + 1) * YB, 2 * ROWS):
        values = array[:, y : y + 2 * ROWS, :].astype(F32)
        block = jnp.concatenate(
            [values[:, ROWS * h : ROWS * (h + 1)].reshape(WIDE, N).astype(BF) for h in range(2)], axis=1
        )
        for at in range(0, WIDE, size):
            part = jnp.dot(wide[at : at + size, :], block, preferred_element_type=F32)
            pieces = []
            for h in range(2):
                piece = part[:, N * h : N * (h + 1)]
                if bias is not None:
                    piece = piece + bias[at : at + size, :]
                pieces.append(piece.reshape(size // ROWS, ROWS, N))
            out[at // ROWS : (at + size) // ROWS, y : y + 2 * ROWS, :] = jnp.concatenate(pieces, axis=1).astype(
                out.dtype
            )


def point_kernel(plane, back, weight_ref, spread_ref, *refs):
    (*bias_ref, in_ref, out_ref), (array, out, wide, bias, sems) = refs[:-5], refs[-5:]
    copy = fetch_rows(in_ref.at[pl.ds(plane * C, C)], array, sems.at[0])
    out_copy = fetch_rows(out, out_ref, sems.at[1])
    for k in range(STEPS):
        copy(k).start()
    if bias_ref:
        bias[...] = lax.dot_general(
            spread_ref[...].astype(F32), jnp.broadcast_to(bias_ref[0][...], (N, C)), (((1,), (1,)), ((), ())),
            precision=lax.Precision.HIGHEST, preferred_element_type=F32,
        )
    widen(weight_ref, spread_ref, wide, not back, 0.5 if back else 1.0)
    for k in range(STEPS):
        copy(k).wait()
        point_rows(array, wide, bias if bias_ref else None, out, k)
        out_copy(k).start()
    for k in range(STEPS):
        out_copy(k).wait()


def x_modes(received, along_x):
    both = jnp.dot(along_x, received.astype(F32), precision=lax.Precision.HIGHEST, preferred_element_type=F32)
    half = OWN * M
    lane = lax.broadcasted_iota(jnp.int32, (half, XC), 1)
    picked = jnp.where(lane < C, both[:half], both[half:])
    return picked + pltpu.roll(picked, C, 1)


def from_x_modes(twice, back_x):
    lane = lax.broadcasted_iota(jnp.int32, (OWN * M, XC), 1)
    stacked = jnp.concatenate([jnp.where(lane < C, twice, 0.0), jnp.where(lane < C, 0.0, twice)], axis=0)
    return jnp.dot(back_x, stacked, precision=lax.Precision.HIGHEST, preferred_element_type=F32)


def mix_kernel(received_ref, along_x_ref, back_x_ref, weight_ref, out_ref, spectrum_ref):
    spectrum = x_modes(received_ref[...], along_x_ref[...]).astype(BF)
    spectrum_ref[...] = spectrum
    lane = lax.broadcasted_iota(jnp.int32, (OWN * M, XC), 1)
    row = lax.broadcasted_iota(jnp.int32, (OWN * M, XC), 0) % M
    wide = spectrum.astype(F32)
    spread = jnp.concatenate(
        [jnp.where(lane // C + 2 * k == row, wide, 0.0).astype(BF) for k in range(M // 2)], axis=1
    )
    mixed = jnp.concatenate(
        [
            jnp.dot(spread[M * p : M * (p + 1)], weight_ref[p], preferred_element_type=F32)
            for p in range(OWN)
        ],
        axis=0,
    )
    twice = jnp.concatenate([mixed, mixed], axis=1)
    out_ref[...] = from_x_modes(twice, back_x_ref[...]).astype(out_ref.dtype)


def mix_back_kernel(received_ref, along_x_ref, back_x_ref, weight_ref, spectrum_ref, out_ref, both_ref):
    hat = x_modes(received_ref[...], along_x_ref[...]).astype(BF)
    lane = lax.broadcasted_iota(jnp.int32, (OWN * M, XC), 1)
    both_ref[...] = jnp.where(lane < C, spectrum_ref[...].astype(F32), hat.astype(F32)).astype(BF)
    lane = lax.broadcasted_iota(jnp.int32, (M, XC), 1)
    row = lax.broadcasted_iota(jnp.int32, (M, XC), 0)
    parts = []
    for p in range(OWN):
        every = lax.dot_general(
            hat[M * p : M * (p + 1), :C], weight_ref[p], (((1,), (1,)), ((), ())), preferred_element_type=F32
        )
        total = sum(
            jnp.where(lane // C + 2 * k == row, every[:, XC * k : XC * (k + 1)], 0.0) for k in range(M // 2)
        )
        parts.append(total + pltpu.roll(total, C, 1))
    out_ref[...] = from_x_modes(jnp.concatenate(parts, axis=0), back_x_ref[...]).astype(out_ref.dtype)


SMALL = pl.BlockSpec(memory_space=pltpu.VMEM)
LARGE = pl.BlockSpec(memory_space=pltpu.HBM)


def params(mib):
    return pltpu.CompilerParams(vmem_limit_bytes=mib * 1024 * 1024)


def cost(flops, size):
    return pl.CostEstimate(flops=flops, bytes_accessed=size, transcendentals=0)


ALL_BYTES = XC * N * N * 2
LARGE_OUT = pltpu.HBM((XC, N, N), BF)
PLANE_OUT = pltpu.HBM((C, N, N), BF)
MODES_OUT = jax.ShapeDtypeStruct((PAIRS, XC), BF)
OWN_OUT = jax.ShapeDtypeStruct((OWN * M, XC), BF)
WHOLE = pltpu.VMEM((XC, N, N), BF)
PLANE = pltpu.VMEM((C, N, N), BF)
SPREAD = pltpu.VMEM((XC * M, N), F32)


def large(array):
    return pltpu.with_memory_space_constraint(array, pltpu.HBM)


def sems(arrays, count):
    return pltpu.SemaphoreType.DMA((arrays, count))


def to_modes(field, table):
    small = (table["forward_y"], table["forward_z"])
    return pl.pallas_call(
        to_modes_kernel,
        in_specs=[LARGE] * 3,
        out_specs=SMALL,
        out_shape=MODES_OUT,
        scratch_shapes=[
            WHOLE, SPREAD, *[pltpu.VMEM(each.shape, BF) for each in small],
            pltpu.SemaphoreType.DMA((CHUNKS,)), pltpu.SemaphoreType.DMA((2,)),
        ],
        compiler_params=params(40),
        cost_estimate=cost(XC * N * N * 128, ALL_BYTES),
        name="to_modes",
    )(large(field), *map(large, small))


def slopes(spatial, points, cot, table):
    return pl.pallas_call(
        slope_kernel,
        in_specs=[SMALL] * 4 + [LARGE] * 3,
        out_specs=(LARGE, SMALL),
        out_shape=(LARGE_OUT, MODES_OUT),
        scratch_shapes=[SPREAD] * 2 + [WHOLE] * 3 + [sems(3, CHUNKS)],
        compiler_params=params(40),
        cost_estimate=cost(XC * N * N * 256, 3 * ALL_BYTES),
        name="slopes",
    )(
        spatial, table["forward_z"], table["back_y"], table["forward_y_half"], *map(large, points), large(cot),
    )


def result(back, weight, samples, point0, slope, table):
    return pl.pallas_call(
        result_kernel,
        in_specs=[SMALL] * 9 + [LARGE] * 2,
        out_specs=(LARGE, SMALL),
        out_shape=(LARGE_OUT, jax.ShapeDtypeStruct((OWN, M // 4, C, C), F32)),
        scratch_shapes=[
            SPREAD, WHOLE, PLANE, WHOLE, pltpu.VMEM((WIDE, WIDE), BF), pltpu.VMEM((4, OWN * M, XC), F32),
            sems(2, CHUNKS), pltpu.SemaphoreType.DMA((STEPS,)),
        ],
        compiler_params=params(40),
        cost_estimate=cost(XC * N * N * 512, 2 * ALL_BYTES),
        name="result",
    )(
        back, table["forward_z"], table["back_y"], weight, table["spread"], *samples, large(point0), large(slope)
    )


def pointwise(plane, back, weight, bias, array, table):
    operands = [weight, table["spread"]] + ([] if back else [bias.reshape(1, C)])
    return pl.pallas_call(
        functools.partial(point_kernel, plane, back),
        in_specs=[SMALL] * len(operands) + [LARGE],
        out_specs=LARGE,
        out_shape=PLANE_OUT,
        scratch_shapes=[
            PLANE, PLANE, pltpu.VMEM((WIDE, WIDE), BF), pltpu.VMEM((WIDE, N), F32), sems(2, STEPS),
        ],
        compiler_params=params(40),
        cost_estimate=cost(C * N * N * 1024, ALL_BYTES),
        name="pointwise",
    )(*operands, large(array))


def mix(received, weight, table):
    return pl.pallas_call(
        mix_kernel,
        in_specs=[SMALL] * 4,
        out_specs=(SMALL, SMALL),
        out_shape=(MODES_OUT, OWN_OUT),
        compiler_params=params(40),
        cost_estimate=cost(1 << 27, 1 << 21),
        name="mix",
    )(received, table["along_x"], table["back_x"], weight)


def mix_back(received, weight, spectrum, table):
    return pl.pallas_call(
        mix_back_kernel,
        in_specs=[SMALL] * 5,
        out_specs=(SMALL, SMALL),
        out_shape=(MODES_OUT, OWN_OUT),
        compiler_params=params(40),
        cost_estimate=cost(1 << 27, 1 << 21),
        name="mix_back",
    )(received, table["along_x"], table["back_x"], weight, spectrum)


def exchange(array):
    cut = array.reshape(GROUPS, OWN, XC)
    return lax.all_to_all(cut, "space", split_axis=0, concat_axis=0, tiled=True).reshape(PAIRS, XC)


def over_samples(both):
    return [both] + [lax.ppermute(both, "dp", [(i, (i + k) % 4) for i in range(4)]) for k in range(1, 4)]


def per_device(field, cotangent, mode_weight, point_weight, point_bias):
    table = {name: jnp.asarray(value) for name, value in tables().items()}
    sample = field.reshape(XC, N, N)
    cot = cotangent.reshape(XC, N, N)
    weight = mode_weight.reshape(OWN, M * C, C)

    modes, sample = lax.optimization_barrier((to_modes(sample, table), sample))
    received = exchange(modes)
    point0 = pointwise(0, False, point_weight, point_bias, sample, table)
    received, point0 = lax.optimization_barrier((received, point0))
    spatial, spectrum = mix(received, weight, table)
    later, spatial = lax.optimization_barrier((sample, spatial))
    received = exchange(spatial)
    point1 = pointwise(1, False, point_weight, point_bias, later, table)
    slope, grad_modes = slopes(received, (point0, point1), cot, table)
    received = exchange(grad_modes)
    point_back0 = pointwise(0, True, point_weight, None, slope, table)
    received, point_back0 = lax.optimization_barrier((received, point_back0))
    back, both = mix_back(received, weight, spectrum, table)
    field_grad, mode_grad = result(exchange(back), point_weight, over_samples(both), point_back0, slope, table)
    return field_grad.reshape(1, XL, C, N, N), mode_grad


def solution(mesh):
    return jax.shard_map(
        per_device,
        mesh=mesh,
        in_specs=(
            P("dp", "space", None, None, None),
            P("dp", "space", None, None, None),
            P("space", None, None, None),
            P(),
            P(),
        ),
        out_specs=(P("dp", "space", None, None, None), P("space", "dp", None, None)),
        check_vma=False,
    )
```

time: 123 us -> 93.9 us (0.76)
  Pallas kernels: 55.7 us -> 34.6 us
  waiting for transfers between devices: 12.4 us -> 29.8 us
  starting transfers between devices: 39.8 us -> 28 us
  blocking collectives: 7.02 us -> 0 us
  local copies, waits for them, and re-layouts: 5.35 us -> 0.06 us
    pallas_call x7 -> x8, Pallas kernels: 55.7 us -> 34.6 us  [the longest x3 12.3 us: pointwise(): pl.pallas_call(functools.partial(point_kernel, plane, back), in_specs=[SM...]
    all_to_all x4, starting transfers between devices: 39.8 us -> 27.1 us  [exchange(): lax.all_to_all(cut, 'space', split_axis=0, concat_axis=0, tiled=True)]
    all_to_all x4, waiting for transfers between devices: 12.4 us -> 25.1 us  [exchange(): lax.all_to_all(cut, 'space', split_axis=0, concat_axis=0, tiled=True)]
    all_gather x1 -> x0, blocking collectives: 7.02 us -> none  [per_device(): every = lax.all_gather(both, 'dp').reshape(4, OWN, M, 2, C)]
    ppermute x0 -> x3, waiting for transfers between devices: none -> 4.68 us  [over_samples(): lax.ppermute(both, 'dp', [(i, (i + k) % 4) for i in range(4)])]
    unnamed x13 -> x18, local copies, waits for them, and re-layouts: 3.21 us -> 0.06 us
  transfers between devices with their start and end apart: 4 -> 7, of which waited for: 2 -> 7; matrix products, arithmetic and copies ran while one was open for 3% -> 0% of each run, Pallas kernels for 17% -> 13%
where the time goes in v1:
time: 93.9 us; the launch traced here: 93.5 us
  Pallas kernels  34.6 us (37%)
  waiting for transfers between devices  29.8 us (32%)
  starting transfers between devices  28 us (30%)
  between operations  0.98 us (1%)
    all_to_all x4, starting transfers between devices, exchange(): lax.all_to_all(cut, 'space', split_axis=0, concat_axis=0, tiled=True)  27.1 us
    all_to_all x4, waiting for transfers between devices, exchange(): lax.all_to_all(cut, 'space', split_axis=0, concat_axis=0, tiled=True)  25.1 us
    pallas_call x3, Pallas kernels, pointwise(): pl.pallas_call(functools.partial(point_kernel, plane, back), in_specs=[SM...  12.3 us
    pallas_call x1, Pallas kernels, slopes(): pl.pallas_call(slope_kernel, in_specs=[SMALL] * 4 + [LARGE] * 3, out_spec...  7.49 us
    pallas_call x1, Pallas kernels, result(): pl.pallas_call(result_kernel, in_specs=[SMALL] * 9 + [LARGE] * 2, out_spe...  6.81 us
    ppermute x3, waiting for transfers between devices, over_samples(): lax.ppermute(both, 'dp', [(i, (i + k) % 4) for i in range(4)])  4.68 us
    pallas_call x1, Pallas kernels, to_modes(): pl.pallas_call(to_modes_kernel, in_specs=[LARGE] * 3, out_specs=SMALL, ou...  4.64 us
  transfers between devices with their start and end apart: 7, of which 7 were waited for; matrix products, arithmetic and copies ran while one was open for 0% of the time, Pallas kernels for 13%

profile of v1, /device:TPU:16, one launch (start us, length us, event | category | flops | bytes accessed | tf_op | source)
XLA Modules:
  0.0 93.5 jit_solution(13960175740619935250)
XLA Ops:
  0.6 0.0 copy-start.1
  0.7 4.6 %to_modes.1 = bf16[256,128]{1,0:T(8,128)(2,1)} custom-call(bf16[128,128,128]{2,1,0:T(8,128)(2,1)} %bitcast.21, bf16[64,256]{1,0:T(8,128)(2,1)} %constant.14.clone.forward_y_ref, bf16[16,128]{1,0:T(8,128)(2,1)} %constant.18.clone.forward_z_ref.table_z_ref), custom_call_target="tpu_custom_call" | custom-call | flops 268435456 | bytes 4194304 | tf_op jit(solution)/shard_map/to_modes/pallas_call | solution.py:375
  5.3 0.0 copy-start
  5.3 0.0 copy-start.2
  5.3 0.0 copy-start.3
  5.3 12.8 %all-to-all-start = ((bf16[64,4,128]{2,1,0:T(4,128)(2,1)}), bf16[64,4,128]{2,1,0:T(4,128)(2,1)S(1)}, u32[]{:S(2)}, u32[]{:S(2)}) async-start(bf16[64,4,128]{2,1,0:T(4,128)(2,1)} %bitcast.1), calls=%async_computation | async-start | bytes 131072 | tf_op jit(solution)/shard_map/all_to_all | solution.py:465
  18.2 0.0 copy-done.1
  18.2 0.0 copy-done.4
  18.2 0.0 copy-done.8
  18.2 4.1 %pointwise.3.point0_ref = bf16[64,128,128]{2,1,0:T(8,128)(2,1)} custom-call(bf16[64,64]{1,0:T(8,128)(2,1)S(1)} %copy-done.4, bf16[512,64]{1,0:T(8,128)(2,1)S(1)} %copy-done.1, f32[1,64]{1,0:T(1,128)S(1)} %bitcast.19, bf16[128,128,128]{2,1,0:T(8,128)(2,1)} %bitcast.22), custom_call_target="tpu_custom_call" | custom-call | flops 1073741824 | bytes 4194304 | tf_op jit(solution)/shard_map/pointwise/pallas_call | solution.py:425
  22.3 0.0 copy-start.5
  22.3 0.0 copy-start.6
  22.3 0.0 copy-start.7
  22.3 6.6 %all-to-all-done = bf16[64,4,128]{2,1,0:T(4,128)(2,1)S(1)} async-done(((bf16[64,4,128]{2,1,0:T(4,128)(2,1)}), bf16[64,4,128]{2,1,0:T(4,128)(2,1)S(1)}, u32[]{:S(2)}, u32[]{:S(2)}) %all-to-all-start) | async-done | bytes 65568 | tf_op jit(solution)/shard_map/all_to_all | solution.py:465
  28.9 1.7 %mix.1 = (bf16[256,128]{1,0:T(8,128)(2,1)}, bf16[64,128]{1,0:T(8,128)(2,1)S(1)}) custom-call(bf16[256,128]{1,0:T(8,128)(2,1)S(1)} %bitcast.18, f32[128,256]{1,0:T(8,128)S(1)} %copy-done.3, f32[256,128]{1,0:T(8,128)S(1)} %copy-done.2, bf16[4,1024,64]{2,1,0:T(8,128)(2,1)S(1)} %bitcast.13), custom_call_target="tpu_custom_call" | custom-call | flops 134217728 | bytes 2097152 | tf_op jit(solution)/shard_map/mix/pallas_call | solution.py:440
  30.6 4.8 %all-to-all-start.1 = ((bf16[64,4,128]{2,1,0:T(4,128)(2,1)}), bf16[64,4,128]{2,1,0:T(4,128)(2,1)S(1)}, u32[]{:S(2)}, u32[]{:S(2)}) async-start(bf16[64,4,128]{2,1,0:T(4,128)(2,1)} %bitcast.5), calls=%async_computation.1 | async-start | bytes 131072 | tf_op jit(solution)/shard_map/all_to_all | solution.py:465
  35.3 4.2 %pointwise.4.point1_ref = bf16[64,128,128]{2,1,0:T(8,128)(2,1)} custom-call(bf16[64,64]{1,0:T(8,128)(2,1)S(1)} %copy-done.4, bf16[512,64]{1,0:T(8,128)(2,1)S(1)} %copy-done.1, f32[1,64]{1,0:T(1,128)S(1)} %bitcast.20, bf16[128,128,128]{2,1,0:T(8,128)(2,1)} %bitcast.23), custom_call_target="tpu_custom_call" | custom-call | flops 1073741824 | bytes 4194304 | tf_op jit(solution)/shard_map/pointwise/pallas_call | solution.py:425
  39.5 6.6 %all-to-all-done.1 = bf16[64,4,128]{2,1,0:T(4,128)(2,1)S(1)} async-done(((bf16[64,4,128]{2,1,0:T(4,128)(2,1)}), bf16[64,4,128]{2,1,0:T(4,128)(2,1)S(1)}, u32[]{:S(2)}, u32[]{:S(2)}) %all-to-all-start.1) | async-done | bytes 65568 | tf_op jit(solution)/shard_map/all_to_all | solution.py:465
  46.1 7.5 %slopes.1 = (bf16[128,128,128]{2,1,0:T(8,128)(2,1)}, bf16[256,128]{1,0:T(8,128)(2,1)}) custom-call(bf16[256,128]{1,0:T(8,128)(2,1)S(1)} %bitcast.16, bf16[16,128]{1,0:T(8,128)(2,1)S(1)} %copy-done.6, bf16[128,32]{1,0:T(8,128)(2,1)S(1)} %copy-done.5, bf16[64,256]{1,0:T(8,128)(2,1)S(1)} %copy-done.7, bf16[64,128,128]{2,1,0:T(8,128)(2,1)} %pointwise.3.point0_ref, ...), custom_call_target="tpu_custom_call" | custom-call | flops 536870912 | bytes 12582912 | tf_op jit(solution)/shard_map/slopes/pallas_call | solution.py:391
  53.6 4.9 %all-to-all-start.2 = ((bf16[64,4,128]{2,1,0:T(4,128)(2,1)}), bf16[64,4,128]{2,1,0:T(4,128)(2,1)S(1)}, u32[]{:S(2)}, u32[]{:S(2)}) async-start(bf16[64,4,128]{2,1,0:T(4,128)(2,1)} %bitcast.8), calls=%async_computation.2 | async-start | bytes 131072 | tf_op jit(solution)/shard_map/all_to_all | solution.py:465
  58.5 4.0 %pointwise.5.point0_ref = bf16[64,128,128]{2,1,0:T(8,128)(2,1)} custom-call(bf16[64,64]{1,0:T(8,128)(2,1)S(1)} %copy-done.4, bf16[512,64]{1,0:T(8,128)(2,1)S(1)} %copy-done.1, bf16[128,128,128]{2,1,0:T(8,128)(2,1)} %get-tuple-element.26.refs_0_.slope_ref), custom_call_target="tpu_custom_call" | custom-call | flops 1073741824 | bytes 4194304 | tf_op jit(solution)/shard_map/pointwise/pallas_call | solution.py:425
  62.5 6.8 %all-to-all-done.2 = bf16[64,4,128]{2,1,0:T(4,128)(2,1)S(1)} async-done(((bf16[64,4,128]{2,1,0:T(4,128)(2,1)}), bf16[64,4,128]{2,1,0:T(4,128)(2,1)S(1)}, u32[]{:S(2)}, u32[]{:S(2)}) %all-to-all-start.2) | async-done | bytes 65568 | tf_op jit(solution)/shard_map/all_to_all | solution.py:465
  69.3 1.8 %mix_back.1 = (bf16[256,128]{1,0:T(8,128)(2,1)}, bf16[64,128]{1,0:T(8,128)(2,1)S(1)}) custom-call(bf16[256,128]{1,0:T(8,128)(2,1)S(1)} %bitcast.17, f32[128,256]{1,0:T(8,128)S(1)} %copy-done.3, f32[256,128]{1,0:T(8,128)S(1)} %copy-done.2, bf16[4,1024,64]{2,1,0:T(8,128)(2,1)S(1)} %bitcast.14, bf16[64,128]{1,0:T(8,128)(2,1)S(1)} %get-tuple-element.28.spectrum_ref), custom_call_target="tpu_custom_call" | custom-call | flops 134217728 | bytes 2097152 | tf_op jit(solution)/shard_map/mix_back/pallas_call | solution.py:452
  71.1 4.6 %all-to-all-start.3 = ((bf16[64,4,128]{2,1,0:T(4,128)(2,1)}), bf16[64,4,128]{2,1,0:T(4,128)(2,1)S(1)}, u32[]{:S(2)}, u32[]{:S(2)}) async-start(bf16[64,4,128]{2,1,0:T(4,128)(2,1)} %bitcast.10), calls=%async_computation.3 | async-start | bytes 131072 | tf_op jit(solution)/shard_map/all_to_all | solution.py:465
  75.7 0.1 collective-permute-start.2
  75.8 0.9 collective-permute-start.1
  76.7 0.0 collective-permute-start
  76.7 0.7 collective-permute-done.2.both3_ref
  77.4 3.8 %collective-permute-done.1.both2_ref = bf16[64,128]{1,0:T(8,128)(2,1)S(1)} collective-permute-done((bf16[64,128]{1,0:T(8,128)(2,1)S(1)}, bf16[64,128]{1,0:T(8,128)(2,1)S(1)}, u32[]{:S(2)}, u32[]{:S(2)}) %collective-permute-start.1) | collective-permute-done | bytes 16416 | tf_op jit(solution)/shard_map/ppermute | solution.py:469
  81.2 0.2 collective-permute-done.both1_ref
  81.4 5.1 %all-to-all-done.3 = bf16[64,4,128]{2,1,0:T(4,128)(2,1)S(1)} async-done(((bf16[64,4,128]{2,1,0:T(4,128)(2,1)}), bf16[64,4,128]{2,1,0:T(4,128)(2,1)S(1)}, u32[]{:S(2)}, u32[]{:S(2)}) %all-to-all-start.3) | async-done | bytes 65568 | tf_op jit(solution)/shard_map/all_to_all | solution.py:465
  86.5 6.8 %result.1 = (bf16[128,128,128]{2,1,0:T(8,128)(2,1)}, f32[4,4,64,64]{3,2,1,0:T(8,128)}) custom-call(bf16[256,128]{1,0:T(8,128)(2,1)S(1)} %bitcast.15, bf16[16,128]{1,0:T(8,128)(2,1)S(1)} %copy-done.6, bf16[128,32]{1,0:T(8,128)(2,1)S(1)} %copy-done.5, bf16[64,64]{1,0:T(8,128)(2,1)S(1)} %copy-done.4, bf16[512,64]{1,0:T(8,128)(2,1)S(1)} %copy-done.1, ...), custom_call_target="tpu_custom_call" | custom-call | flops 1073741824 | bytes 8388608 | tf_op jit(solution)/shard_map/result/pallas_call | solution.py:406
  (8 shorter events, 0.0 us)
Async XLA Ops:
  0.6 17.5 %copy-start.1 = (bf16[512,64]{1,0:T(8,128)(2,1)S(1)}, bf16[512,64]{1,0:T(8,128)(2,1)}, u32[]{:S(2)}) copy-start(bf16[512,64]{1,0:T(8,128)(2,1)} %constant.16.clone.spread_ref) | copy-start | bytes 196612
  0.6 17.5 %copy-start.4 = (bf16[64,64]{1,0:T(8,128)(2,1)S(1)}, bf16[64,64]{1,0:T(8,128)(2,1)}, u32[]{:S(2)}) copy-start(bf16[64,64]{1,0:T(8,128)(2,1)} %weight_ref.7) | copy-start | bytes 24580
  0.7 17.5 %copy-start.8 = (f32[64]{0:T(128)S(1)}, f32[64]{0:T(128)}, u32[]{:S(2)}) copy-start(f32[64]{0:T(128)} %param.16) | copy-start | bytes 772
  5.3 23.6 %copy-start = (bf16[4,16,64,64]{3,2,1,0:T(8,128)(2,1)S(1)}, bf16[4,16,64,64]{3,2,1,0:T(8,128)(2,1)}, u32[]{:S(2)}) copy-start(bf16[4,16,64,64]{3,2,1,0:T(8,128)(2,1)} %param.14) | copy-start | bytes 1572868
  5.3 23.6 %copy-start.2 = (f32[256,128]{1,0:T(8,128)S(1)}, f32[256,128]{1,0:T(8,128)}, u32[]{:S(2)}) copy-start(f32[256,128]{1,0:T(8,128)} %constant.20.clone.back_x_ref) | copy-start | bytes 393220
  5.3 23.6 %copy-start.3 = (f32[128,256]{1,0:T(8,128)S(1)}, f32[128,256]{1,0:T(8,128)}, u32[]{:S(2)}) copy-start(f32[128,256]{1,0:T(8,128)} %constant.19.clone.along_x_ref) | copy-start | bytes 393220
  5.3 23.6 %all-to-all-start = ((bf16[64,4,128]{2,1,0:T(4,128)(2,1)}), bf16[64,4,128]{2,1,0:T(4,128)(2,1)S(1)}, u32[]{:S(2)}, u32[]{:S(2)}) async-start(bf16[64,4,128]{2,1,0:T(4,128)(2,1)} %bitcast.1), calls=%async_computation | async-start | bytes 131072 | tf_op jit(solution)/shard_map/all_to_all | solution.py:465
  22.3 23.8 %copy-start.5 = (bf16[128,32]{1,0:T(8,128)(2,1)S(1)}, bf16[128,32]{1,0:T(8,128)(2,1)}, u32[]{:S(2)}) copy-start(bf16[128,32]{1,0:T(8,128)(2,1)} %constant.17.clone.back_y_ref) | copy-start | bytes 24580
  22.3 23.8 %copy-start.6 = (bf16[16,128]{1,0:T(8,128)(2,1)S(1)}, bf16[16,128]{1,0:T(8,128)(2,1)}, u32[]{:S(2)}) copy-start(bf16[16,128]{1,0:T(8,128)(2,1)} %constant.18.clone.forward_z_ref.table_z_ref) | copy-start | bytes 12292
  22.3 23.8 %copy-start.7 = (bf16[64,256]{1,0:T(8,128)(2,1)S(1)}, bf16[64,256]{1,0:T(8,128)(2,1)}, u32[]{:S(2)}) copy-start(bf16[64,256]{1,0:T(8,128)(2,1)} %constant.15.clone.forward_y_ref) | copy-start | bytes 98308
  30.6 15.5 %all-to-all-start.1 = ((bf16[64,4,128]{2,1,0:T(4,128)(2,1)}), bf16[64,4,128]{2,1,0:T(4,128)(2,1)S(1)}, u32[]{:S(2)}, u32[]{:S(2)}) async-start(bf16[64,4,128]{2,1,0:T(4,128)(2,1)} %bitcast.5), calls=%async_computation.1 | async-start | bytes 131072 | tf_op jit(solution)/shard_map/all_to_all | solution.py:465
  53.6 15.7 %all-to-all-start.2 = ((bf16[64,4,128]{2,1,0:T(4,128)(2,1)}), bf16[64,4,128]{2,1,0:T(4,128)(2,1)S(1)}, u32[]{:S(2)}, u32[]{:S(2)}) async-start(bf16[64,4,128]{2,1,0:T(4,128)(2,1)} %bitcast.8), calls=%async_computation.2 | async-start | bytes 131072 | tf_op jit(solution)/shard_map/all_to_all | solution.py:465
  71.1 15.4 %all-to-all-start.3 = ((bf16[64,4,128]{2,1,0:T(4,128)(2,1)}), bf16[64,4,128]{2,1,0:T(4,128)(2,1)S(1)}, u32[]{:S(2)}, u32[]{:S(2)}) async-start(bf16[64,4,128]{2,1,0:T(4,128)(2,1)} %bitcast.10), calls=%async_computation.3 | async-start | bytes 131072 | tf_op jit(solution)/shard_map/all_to_all | solution.py:465
  75.7 1.7 %collective-permute-start.2 = (bf16[64,128]{1,0:T(8,128)(2,1)S(1)}, bf16[64,128]{1,0:T(8,128)(2,1)S(1)}, u32[]{:S(2)}, u32[]{:S(2)}) collective-permute-start(bf16[64,128]{1,0:T(8,128)(2,1)S(1)} %get-tuple-element.30.both0_ref), channel_id=1, source_target_pairs={{0,192},{64,0},{128,64},{192,128},{1,193},{65,1},{129,65},{193,129... | collective-permute-start | bytes 49160 | tf_op jit(solution)/shard_map/ppermute | solution.py:469
  75.8 5.4 %collective-permute-start.1 = (bf16[64,128]{1,0:T(8,128)(2,1)S(1)}, bf16[64,128]{1,0:T(8,128)(2,1)S(1)}, u32[]{:S(2)}, u32[]{:S(2)}) collective-permute-start(bf16[64,128]{1,0:T(8,128)(2,1)S(1)} %get-tuple-element.30.both0_ref), channel_id=1, source_target_pairs={{0,128},{64,192},{128,0},{192,64},{1,129},{65,193},{129,1},{193,65... | collective-permute-start | bytes 49160 | tf_op jit(solution)/shard_map/ppermute | solution.py:469
  76.7 4.7 %collective-permute-start = (bf16[64,128]{1,0:T(8,128)(2,1)S(1)}, bf16[64,128]{1,0:T(8,128)(2,1)S(1)}, u32[]{:S(2)}, u32[]{:S(2)}) collective-permute-start(bf16[64,128]{1,0:T(8,128)(2,1)S(1)} %get-tuple-element.30.both0_ref), channel_id=1, source_target_pairs={{0,64},{64,128},{128,192},{192,0},{1,65},{65,129},{129,193},{193,1... | collective-permute-start | bytes 49160 | tf_op jit(solution)/shard_map/ppermute | solution.py:469

commit v2 on v1

--- a/solution.py
+++ b/solution.py
@@ -20,8 +20,8 @@
 PAIRS = M * M
 OWN = 4
 GROUPS = 64
-CHUNKS = 8
-G = XC // CHUNKS
+SLOPE_HEAD = 16
+RESULT_HEAD = 32
 
 
 def basis(length, count):
@@ -52,8 +52,8 @@
         spread=np.kron(np.eye(C, dtype=np.float32), np.ones((ROWS, 1), np.float32)).astype(BF),
         back_y=back_y.astype(BF),
         forward_z=np.ascontiguousarray(table_z.T),
-        along_x=along_x,
-        back_x=np.ascontiguousarray(along_x.T),
+        along_x=np.stack(split(along_x)),
+        back_x=np.stack(split(np.ascontiguousarray(along_x.T))),
     )
 
 
@@ -89,41 +89,40 @@
     return jnp.dot(back_y, jnp.concatenate([pair, pair], axis=0), preferred_element_type=F32)
 
 
-def fetch(source, target, sems):
-    return lambda k: pltpu.make_async_copy(
-        source.at[pl.ds(G * k, G)], target.at[pl.ds(G * k, G)], sems.at[k]
-    )
-
-
-def fetch(source, target, sems, first=0):
-    return lambda k: pltpu.make_async_copy(
-        source.at[pl.ds(G * (k - first), G)], target.at[pl.ds(G * k, G)], sems.at[k]
-    )
-
-
-def fetch_planes(planes, target, sems):
-    half = CHUNKS // XL
-    copies = [fetch(source, target, sems, half * plane) for plane, source in enumerate(planes)]
-    return lambda k: copies[k // half](k)
-
-
-def to_modes_kernel(field_ref, forward_y_ref, forward_z_ref, out_ref, held, scratch, forward_y, forward_z, sems, own_sems):
+def pieces(source, target, sems, cuts, first=0):
+    return {
+        low: pltpu.make_async_copy(
+            source.at[pl.ds(low - first, high - low)], target.at[pl.ds(low, high - low)], sems.at[k]
+        )
+        for k, (low, high) in enumerate(zip(cuts, cuts[1:]))
+    }
+
+
+FIELD_CUTS = (0, 48, 96, 128)
+
+
+def to_modes_kernel(
+    field_ref, forward_y_ref, forward_z_ref, out_ref, held, scratch, forward_y, forward_z, sems, small_sems
+):
     small = [
-        pltpu.make_async_copy(forward_y_ref, forward_y, own_sems.at[0]),
-        pltpu.make_async_copy(forward_z_ref, forward_z, own_sems.at[1]),
+        pltpu.make_async_copy(forward_y_ref, forward_y, small_sems.at[0]),
+        pltpu.make_async_copy(forward_z_ref, forward_z, small_sems.at[1]),
     ]
-    copy = fetch(field_ref, held, sems)
-    for each in small:
-        each.start()
-    for k in range(CHUNKS):
-        copy(k).start()
-    for each in small:
-        each.wait()
-    for k in range(CHUNKS):
-        copy(k).wait()
-        for g in range(G * k, G * (k + 1), 4):
-            y_modes([held[g + j] for j in range(4)], forward_y[...], scratch, g * M)
+    copies = pieces(field_ref, held, sems, FIELD_CUTS)
+    for copy in (*small, *copies.values()):
+        copy.start()
+    for copy in small:
+        copy.wait()
+    for g in range(0, XC, 4):
+        if g in copies:
+            copies[g].wait()
+        y_modes([held[g + j] for j in range(4)], forward_y[...], scratch, g * M)
     z_modes(scratch, forward_z[...], out_ref)
+
+
+SLOPE_CUTS = (0, SLOPE_HEAD, 40, C, 96, 128)
+SLOPE_OUT_CUTS = (0, 32, 64, 96, 112, 128)
+RESULT_CUTS = (0, RESULT_HEAD, C, 96, 112, 128)
 
 
 def doubled_slope(pre, cot):
@@ -135,72 +134,73 @@
 
 
 def slope_kernel(
-    spatial_ref, table_z_ref, back_y_ref, forward_y_ref, point0_ref, point1_ref, cot_ref,
-    slope_ref, out_ref, spread, scratch, point, cot, slope, sems,
+    spatial_ref, table_z_ref, back_y_ref, forward_y_ref, point_head_ref, cot_head_ref,
+    point0_ref, point1_ref, cot_ref, slope_ref, out_ref, spread, scratch, point, cot, slope, sems,
 ):
-    point_copy = fetch_planes((point0_ref, point1_ref), point, sems.at[0])
-    cot_copy = fetch(cot_ref, cot, sems.at[1])
-    slope_copy = fetch(slope, slope_ref, sems.at[2])
-    for k in range(CHUNKS):
-        point_copy(k).start()
-        cot_copy(k).start()
+    point_copies = pieces(point0_ref, point, sems.at[0], SLOPE_CUTS[1:4])
+    point_copies |= pieces(point1_ref, point, sems.at[1], SLOPE_CUTS[3:], C)
+    cot_copies = pieces(cot_ref, cot, sems.at[2], SLOPE_CUTS[1:])
+    slope_copies = pieces(slope, slope_ref, sems.at[3], SLOPE_OUT_CUTS)
+    for low in SLOPE_CUTS[1:-1]:
+        point_copies[low].start()
+        cot_copies[low].start()
     from_z_modes(spatial_ref[...], table_z_ref[...], spread)
     last = None
     for first in range(0, XC, 4):
-        if first % G == 0:
-            point_copy(first // G).wait()
-            cot_copy(first // G).wait()
+        if first in cot_copies:
+            point_copies[first].wait()
+            cot_copies[first].wait()
+        point_at, cot_at = (point, cot) if first >= SLOPE_HEAD else (point_head_ref, cot_head_ref)
         group = []
         for at in range(first, first + 4, 2):
             both = from_y_modes(spread, back_y_ref[...], at * M).astype(BF)
             for h in range(2):
-                value = doubled_slope(both[:, N * h : N * (h + 1)] + point[at + h], cot[at + h])
+                value = doubled_slope(both[:, N * h : N * (h + 1)] + point_at[at + h], cot_at[at + h])
                 slope[at + h] = value
                 group.append(value)
         if last is not None:
             y_modes(last, forward_y_ref[...], scratch, (first - 4) * M)
         last = group
-        if first % G == G - 4:
-            slope_copy(first // G).start()
+        for low, high in zip(SLOPE_OUT_CUTS, SLOPE_OUT_CUTS[1:]):
+            if first + 4 == high:
+                slope_copies[low].start()
     y_modes(last, forward_y_ref[...], scratch, (XC - 4) * M)
     z_modes(scratch, table_z_ref[...], out_ref)
-    for k in range(CHUNKS):
-        slope_copy(k).wait()
+    for copy in slope_copies.values():
+        copy.wait()
 
 
 def result_kernel(
-    back_ref, table_z_ref, back_y_ref, weight_ref, spread_ref, both0_ref, both1_ref, both2_ref, both3_ref,
-    point0_ref, slope_ref, out_ref, mode_grad_ref, spread, point, slope, held, wide, grads, sems, row_sems,
+    back_ref, table_z_ref, back_y_ref, wide_ref, both0_ref, both1_ref, both2_ref, both3_ref, head_ref,
+    point0_ref, slope_ref, out_ref, mode_grad_ref, spread, point, slope, held, grads, sems, row_sems,
 ):
-    half = CHUNKS // XL
-    point_copy = fetch(point0_ref, point, sems.at[0])
-    out_copy = fetch(held, out_ref, sems.at[1])
-    slope_copy = fetch_rows(slope_ref.at[pl.ds(C, C)], slope, row_sems)
-    for k in range(half):
-        point_copy(k).start()
-    for k in range(STEPS):
+    (point_copy,) = pieces(point0_ref, point, sems.at[0], (RESULT_HEAD, C)).values()
+    out_copies = pieces(held, out_ref, sems.at[1], RESULT_CUTS)
+    slope_copy = fetch_rows(slope_ref.at[pl.ds(C, C)], slope, row_sems, 2 * YB)
+    point_copy.start()
+    for k in range(STEPS // 2):
         slope_copy(k).start()
     from_z_modes(back_ref[...], table_z_ref[...], spread)
 
-    def finish(k):
-        for g in range(G * k, G * (k + 1), 2):
+    def finish(low, high):
+        for g in range(low, high, 2):
             both = from_y_modes(spread, back_y_ref[...], g * M)
             for h in range(2):
-                held[g + h] = (both[:, N * h : N * (h + 1)] + point[g + h].astype(F32)).astype(BF)
-        out_copy(k).start()
-
-    for k in range(half):
-        point_copy(k).wait()
-        finish(k)
-    widen(weight_ref, spread_ref, wide, False, 0.5)
-    for k in range(STEPS):
-        slope_copy(k).wait()
-        point_rows(slope, wide, None, point.at[pl.ds(C, C)], k)
-    for k in range(half, CHUNKS):
-        finish(k)
+                other = head_ref[g + h] if g < RESULT_HEAD else point[g + h]
+                held[g + h] = (both[:, N * h : N * (h + 1)] + other.astype(F32)).astype(BF)
+        out_copies[low].start()
+
+    for low, high in zip(RESULT_CUTS, RESULT_CUTS[1:]):
+        if low == RESULT_HEAD:
+            point_copy.wait()
+        if low == C:
+            for k in range(STEPS // 2):
+                slope_copy(k).wait()
+                point_rows(slope, wide_ref, None, point.at[pl.ds(C, C)], k, 2 * YB)
+        finish(low, high)
     mode_gradient((both0_ref, both1_ref, both2_ref, both3_ref), grads, mode_grad_ref)
-    for k in range(CHUNKS):
-        out_copy(k).wait()
+    for copy in out_copies.values():
+        copy.wait()
 
 
 def mode_gradient(samples, grads, out_ref):
@@ -240,17 +240,17 @@
 STEPS = N // YB
 
 
-def fetch_rows(source, target, sems):
+def fetch_rows(source, target, sems, count=YB):
     def copy(k):
-        at = (slice(None), pl.ds(k * YB, YB))
+        at = (slice(None), pl.ds(k * count, count))
         return pltpu.make_async_copy(source.at[at], target.at[at], sems.at[k])
 
     return copy
 
 
-def point_rows(array, wide, bias, out, k):
+def point_rows(array, wide, bias, out, k, count=YB):
     size = 256
-    for y in range(k * YB, (k + 1) * YB, 2 * ROWS):
+    for y in range(k * count, (k + 1) * count, 2 * ROWS):
         values = array[:, y : y + 2 * ROWS, :].astype(F32)
         block = jnp.concatenate(
             [values[:, ROWS * h : ROWS * (h + 1)].reshape(WIDE, N).astype(BF) for h in range(2)], axis=1
@@ -269,27 +269,41 @@
 
 
 def point_kernel(plane, back, weight_ref, spread_ref, *refs):
-    (*bias_ref, in_ref, out_ref), (array, out, wide, bias, sems) = refs[:-5], refs[-5:]
+    refs, (array, out, bias, sems, head_sem) = refs[:-5], refs[-5:]
+    if back:
+        in_ref, out_ref, head_ref, wide = refs
+    elif plane:
+        bias_ref, in_ref, out_ref, wide = refs
+    else:
+        bias_ref, cot_ref, in_ref, out_ref, head_ref, cot_head_ref, wide = refs
     copy = fetch_rows(in_ref.at[pl.ds(plane * C, C)], array, sems.at[0])
     out_copy = fetch_rows(out, out_ref, sems.at[1])
     for k in range(STEPS):
         copy(k).start()
-    if bias_ref:
+    if not back and not plane:
+        head_copy = pltpu.make_async_copy(cot_ref.at[pl.ds(0, SLOPE_HEAD)], cot_head_ref, head_sem)
+        head_copy.start()
+    if not back:
         bias[...] = lax.dot_general(
-            spread_ref[...].astype(F32), jnp.broadcast_to(bias_ref[0][...], (N, C)), (((1,), (1,)), ((), ())),
+            spread_ref[...].astype(F32), jnp.broadcast_to(bias_ref[...], (N, C)), (((1,), (1,)), ((), ())),
             precision=lax.Precision.HIGHEST, preferred_element_type=F32,
         )
     widen(weight_ref, spread_ref, wide, not back, 0.5 if back else 1.0)
     for k in range(STEPS):
         copy(k).wait()
-        point_rows(array, wide, bias if bias_ref else None, out, k)
+        point_rows(array, wide, None if back else bias, out, k)
         out_copy(k).start()
+    if not plane:
+        head_ref[...] = out[: head_ref.shape[0]]
     for k in range(STEPS):
         out_copy(k).wait()
+    if not back and not plane:
+        head_copy.wait()
 
 
 def x_modes(received, along_x):
-    both = jnp.dot(along_x, received.astype(F32), precision=lax.Precision.HIGHEST, preferred_element_type=F32)
+    both = jnp.dot(along_x[0], received, preferred_element_type=F32)
+    both += jnp.dot(along_x[1], received, preferred_element_type=F32)
     half = OWN * M
     lane = lax.broadcasted_iota(jnp.int32, (half, XC), 1)
     picked = jnp.where(lane < C, both[:half], both[half:])
@@ -299,7 +313,10 @@
 def from_x_modes(twice, back_x):
     lane = lax.broadcasted_iota(jnp.int32, (OWN * M, XC), 1)
     stacked = jnp.concatenate([jnp.where(lane < C, twice, 0.0), jnp.where(lane < C, 0.0, twice)], axis=0)
-    return jnp.dot(back_x, stacked, precision=lax.Precision.HIGHEST, preferred_element_type=F32)
+    stacked = stacked.astype(BF)
+    return jnp.dot(back_x[0], stacked, preferred_element_type=F32) + jnp.dot(
+        back_x[1], stacked, preferred_element_type=F32
+    )
 
 
 def mix_kernel(received_ref, along_x_ref, back_x_ref, weight_ref, out_ref, spectrum_ref):
@@ -379,7 +396,7 @@
         out_shape=MODES_OUT,
         scratch_shapes=[
             WHOLE, SPREAD, *[pltpu.VMEM(each.shape, BF) for each in small],
-            pltpu.SemaphoreType.DMA((CHUNKS,)), pltpu.SemaphoreType.DMA((2,)),
+            pltpu.SemaphoreType.DMA((len(FIELD_CUTS) - 1,)), pltpu.SemaphoreType.DMA((2,)),
         ],
         compiler_params=params(40),
         cost_estimate=cost(XC * N * N * 128, ALL_BYTES),
@@ -387,53 +404,57 @@
     )(large(field), *map(large, small))
 
 
-def slopes(spatial, points, cot, table):
+def slopes(spatial, heads, points, cot, table):
     return pl.pallas_call(
         slope_kernel,
-        in_specs=[SMALL] * 4 + [LARGE] * 3,
+        in_specs=[SMALL] * 6 + [LARGE] * 3,
         out_specs=(LARGE, SMALL),
         out_shape=(LARGE_OUT, MODES_OUT),
-        scratch_shapes=[SPREAD] * 2 + [WHOLE] * 3 + [sems(3, CHUNKS)],
+        scratch_shapes=[SPREAD] * 2 + [WHOLE] * 3 + [sems(4, len(SLOPE_OUT_CUTS))],
         compiler_params=params(40),
         cost_estimate=cost(XC * N * N * 256, 3 * ALL_BYTES),
         name="slopes",
     )(
-        spatial, table["forward_z"], table["back_y"], table["forward_y_half"], *map(large, points), large(cot),
-    )
-
-
-def result(back, weight, samples, point0, slope, table):
+        spatial, table["forward_z"], table["back_y"], table["forward_y_half"], *heads,
+        *map(large, points), large(cot),
+    )
+
+
+def result(back, wide, samples, head, point0, slope, table):
     return pl.pallas_call(
         result_kernel,
         in_specs=[SMALL] * 9 + [LARGE] * 2,
         out_specs=(LARGE, SMALL),
         out_shape=(LARGE_OUT, jax.ShapeDtypeStruct((OWN, M // 4, C, C), F32)),
         scratch_shapes=[
-            SPREAD, WHOLE, PLANE, WHOLE, pltpu.VMEM((WIDE, WIDE), BF), pltpu.VMEM((4, OWN * M, XC), F32),
-            sems(2, CHUNKS), pltpu.SemaphoreType.DMA((STEPS,)),
+            SPREAD, WHOLE, PLANE, WHOLE, pltpu.VMEM((4, OWN * M, XC), F32),
+            sems(2, len(RESULT_CUTS)), pltpu.SemaphoreType.DMA((STEPS,)),
         ],
         compiler_params=params(40),
         cost_estimate=cost(XC * N * N * 512, 2 * ALL_BYTES),
         name="result",
     )(
-        back, table["forward_z"], table["back_y"], weight, table["spread"], *samples, large(point0), large(slope)
-    )
-
-
-def pointwise(plane, back, weight, bias, array, table):
+        back, table["forward_z"], table["back_y"], wide, *samples, head, large(point0), large(slope)
+    )
+
+
+def pointwise(plane, back, weight, bias, array, table, cot=None):
     operands = [weight, table["spread"]] + ([] if back else [bias.reshape(1, C)])
+    sources = ([] if cot is None else [cot]) + [array]
+    wide = pltpu.VMEM((WIDE, WIDE), BF)
+    head = pltpu.VMEM((RESULT_HEAD if back else SLOPE_HEAD, N, N), BF)
+    kept = [head] * (0 if plane else 1 + (cot is not None)) + [wide] * back
     return pl.pallas_call(
         functools.partial(point_kernel, plane, back),
-        in_specs=[SMALL] * len(operands) + [LARGE],
-        out_specs=LARGE,
-        out_shape=PLANE_OUT,
-        scratch_shapes=[
-            PLANE, PLANE, pltpu.VMEM((WIDE, WIDE), BF), pltpu.VMEM((WIDE, N), F32), sems(2, STEPS),
-        ],
+        in_specs=[SMALL] * len(operands) + [LARGE] * len(sources),
+        out_specs=[LARGE] + [SMALL] * len(kept),
+        out_shape=[PLANE_OUT] + kept,
+        scratch_shapes=[wide] * (not back)
+        + [PLANE, PLANE, pltpu.VMEM((WIDE, N), F32), sems(2, STEPS), pltpu.SemaphoreType.DMA],
         compiler_params=params(40),
         cost_estimate=cost(C * N * N * 1024, ALL_BYTES),
         name="pointwise",
-    )(*operands, large(array))
+    )(*operands, *map(large, sources))
 
 
 def mix(received, weight, table):
@@ -466,7 +487,7 @@
 
 
 def over_samples(both):
-    return [both] + [lax.ppermute(both, "dp", [(i, (i + k) % 4) for i in range(4)]) for k in range(1, 4)]
+    return [both] + [lax.ppermute(both, "dp", [(i, i ^ k) for i in range(4)]) for k in range(1, 4)]
 
 
 def per_device(field, cotangent, mode_weight, point_weight, point_bias):
@@ -477,18 +498,20 @@
 
     modes, sample = lax.optimization_barrier((to_modes(sample, table), sample))
     received = exchange(modes)
-    point0 = pointwise(0, False, point_weight, point_bias, sample, table)
+    point0, *heads = pointwise(0, False, point_weight, point_bias, sample, table, cot)
     received, point0 = lax.optimization_barrier((received, point0))
     spatial, spectrum = mix(received, weight, table)
     later, spatial = lax.optimization_barrier((sample, spatial))
     received = exchange(spatial)
-    point1 = pointwise(1, False, point_weight, point_bias, later, table)
-    slope, grad_modes = slopes(received, (point0, point1), cot, table)
+    (point1,) = pointwise(1, False, point_weight, point_bias, later, table)
+    slope, grad_modes = slopes(received, heads, (point0, point1), cot, table)
     received = exchange(grad_modes)
-    point_back0 = pointwise(0, True, point_weight, None, slope, table)
+    point_back0, head, wide = pointwise(0, True, point_weight, None, slope, table)
     received, point_back0 = lax.optimization_barrier((received, point_back0))
     back, both = mix_back(received, weight, spectrum, table)
-    field_grad, mode_grad = result(exchange(back), point_weight, over_samples(both), point_back0, slope, table)
+    field_grad, mode_grad = result(
+        exchange(back), wide, over_samples(both), head, point_back0, slope, table
+    )
     return field_grad.reshape(1, XL, C, N, N), mode_grad
 
 

time: 93.9 us -> 90.5 us (0.964)
  Pallas kernels: 34.6 us -> 31.5 us
  waiting for transfers between devices: 29.8 us -> 27.1 us
  starting transfers between devices: 28 us -> 30.6 us
    ppermute x3, waiting for transfers between devices: 4.68 us -> 1.99 us  [over_samples(): lax.ppermute(both, 'dp', [(i, i ^ k) for i in range(4)])]
    ppermute x3, starting transfers between devices: 0.97 us -> 3.44 us  [over_samples(): lax.ppermute(both, 'dp', [(i, i ^ k) for i in range(4)])]
    pallas_call x1, Pallas kernels: 6.81 us -> 5.6 us  [result(): pl.pallas_call(result_kernel, in_specs=[SMALL] * 9 + [LARGE] * 2, out_spe...]
  transfers between devices with their start and end apart: 7 -> 7, of which waited for: 7 -> 6; matrix products, arithmetic and copies ran while one was open for 0% -> 0% of each run, Pallas kernels for 13% -> 14%
where the time goes in v2:
time: 90.5 us; the launch traced here: 90.2 us
  Pallas kernels  31.5 us (35%)
  starting transfers between devices  30.6 us (34%)
  waiting for transfers between devices  27.1 us (30%)
  between operations  0.98 us (1%)
    all_to_all x4, starting transfers between devices, exchange(): lax.all_to_all(cut, 'space', split_axis=0, concat_axis=0, tiled=True)  27.1 us
    all_to_all x4, waiting for transfers between devices, exchange(): lax.all_to_all(cut, 'space', split_axis=0, concat_axis=0, tiled=True)  25.1 us
    pallas_call x3, Pallas kernels, pointwise(): pl.pallas_call(functools.partial(point_kernel, plane, back), in_specs=[SM...  12.4 us
    pallas_call x1, Pallas kernels, slopes(): pl.pallas_call(slope_kernel, in_specs=[SMALL] * 6 + [LARGE] * 3, out_spec...  6.76 us
    pallas_call x1, Pallas kernels, result(): pl.pallas_call(result_kernel, in_specs=[SMALL] * 9 + [LARGE] * 2, out_spe...  5.6 us
    pallas_call x1, Pallas kernels, to_modes(): pl.pallas_call(to_modes_kernel, in_specs=[LARGE] * 3, out_specs=SMALL, ou...  3.84 us
    ppermute x3, starting transfers between devices, over_samples(): lax.ppermute(both, 'dp', [(i, i ^ k) for i in range(4)])  3.44 us
    ppermute x3, waiting for transfers between devices, over_samples(): lax.ppermute(both, 'dp', [(i, i ^ k) for i in range(4)])  1.99 us
  transfers between devices with their start and end apart: 7, of which 6 were waited for; matrix products, arithmetic and copies ran while one was open for 0% of the time, Pallas kernels for 14%

profile of v2, /device:TPU:16, one launch (start us, length us, event | category | flops | bytes accessed | tf_op | source)
XLA Modules:
  0.0 90.2 jit_solution(14267630580448164821)
XLA Ops:
  0.6 0.0 copy-start.1
  0.6 0.0 copy-start.4
  0.7 0.0 copy-start.8
  0.7 3.8 %to_modes.1 = bf16[256,128]{1,0:T(8,128)(2,1)} custom-call(bf16[128,128,128]{2,1,0:T(8,128)(2,1)} %bitcast.21, bf16[64,256]{1,0:T(8,128)(2,1)} %constant.14.clone.forward_y_ref, bf16[16,128]{1,0:T(8,128)(2,1)} %constant.18.clone.forward_z_ref.table_z_ref), custom_call_target="tpu_custom_call" | custom-call | flops 268435456 | bytes 4194304 | tf_op jit(solution)/shard_map/to_modes/pallas_call | solution.py:392
  4.5 12.7 %all-to-all-start = ((bf16[64,4,128]{2,1,0:T(4,128)(2,1)}), bf16[64,4,128]{2,1,0:T(4,128)(2,1)S(1)}, u32[]{:S(2)}, u32[]{:S(2)}) async-start(bf16[64,4,128]{2,1,0:T(4,128)(2,1)} %bitcast.1), calls=%async_computation | async-start | bytes 131072 | tf_op jit(solution)/shard_map/all_to_all | solution.py:486
  17.2 0.0 copy-start
  17.2 0.0 copy-start.2
  17.2 0.0 copy-start.3
  17.2 4.4 %pointwise.3 = (bf16[64,128,128]{2,1,0:T(8,128)(2,1)}, bf16[16,128,128]{2,1,0:T(8,128)(2,1)S(1)}, bf16[16,128,128]{2,1,0:T(8,128)(2,1)S(1)}) custom-call(bf16[64,64]{1,0:T(8,128)(2,1)S(1)} %copy-done.4, bf16[512,64]{1,0:T(8,128)(2,1)S(1)} %copy-done.1, f32[1,64]{1,0:T(1,128)S(1)} %bitcast.19, bf16[128,128,128]{2,1,0:T(8,128)(2,1)} %bitcast.24, ...), custom_call_target="tpu_custom_call" | custom-call | flops 1073741824 | bytes 4194304 | tf_op jit(solution)/shard_map/pointwise/pallas_call | solution.py:447
  21.6 0.0 copy-start.5
  21.6 0.0 copy-start.6
  21.6 0.0 copy-start.7
  21.7 6.3 %all-to-all-done = bf16[64,4,128]{2,1,0:T(4,128)(2,1)S(1)} async-done(((bf16[64,4,128]{2,1,0:T(4,128)(2,1)}), bf16[64,4,128]{2,1,0:T(4,128)(2,1)S(1)}, u32[]{:S(2)}, u32[]{:S(2)}) %all-to-all-start) | async-done | bytes 65568 | tf_op jit(solution)/shard_map/all_to_all | solution.py:486
  28.0 1.4 %mix.1 = (bf16[256,128]{1,0:T(8,128)(2,1)}, bf16[64,128]{1,0:T(8,128)(2,1)S(1)}) custom-call(bf16[256,128]{1,0:T(8,128)(2,1)S(1)} %bitcast.18, bf16[2,128,256]{2,1,0:T(8,128)(2,1)S(1)} %copy-done.3, bf16[2,256,128]{2,1,0:T(8,128)(2,1)S(1)} %copy-done.2, bf16[4,1024,64]{2,1,0:T(8,128)(2,1)S(1)} %bitcast.13), custom_call_target="tpu_custom_call" | custom-call | flops 134217728 | bytes 2097152 | tf_op jit(solution)/shard_map/mix/pallas_call | solution.py:461
  29.3 5.0 %all-to-all-start.1 = ((bf16[64,4,128]{2,1,0:T(4,128)(2,1)}), bf16[64,4,128]{2,1,0:T(4,128)(2,1)S(1)}, u32[]{:S(2)}, u32[]{:S(2)}) async-start(bf16[64,4,128]{2,1,0:T(4,128)(2,1)} %bitcast.6), calls=%async_computation.1 | async-start | bytes 131072 | tf_op jit(solution)/shard_map/all_to_all | solution.py:486
  34.4 4.2 %pointwise.4.point1_ref = bf16[64,128,128]{2,1,0:T(8,128)(2,1)} custom-call(bf16[64,64]{1,0:T(8,128)(2,1)S(1)} %copy-done.4, bf16[512,64]{1,0:T(8,128)(2,1)S(1)} %copy-done.1, f32[1,64]{1,0:T(1,128)S(1)} %bitcast.20, bf16[128,128,128]{2,1,0:T(8,128)(2,1)} %bitcast.23), custom_call_target="tpu_custom_call" | custom-call | flops 1073741824 | bytes 4194304 | tf_op jit(solution)/shard_map/pointwise/pallas_call | solution.py:447
  38.5 6.6 %all-to-all-done.1 = bf16[64,4,128]{2,1,0:T(4,128)(2,1)S(1)} async-done(((bf16[64,4,128]{2,1,0:T(4,128)(2,1)}), bf16[64,4,128]{2,1,0:T(4,128)(2,1)S(1)}, u32[]{:S(2)}, u32[]{:S(2)}) %all-to-all-start.1) | async-done | bytes 65568 | tf_op jit(solution)/shard_map/all_to_all | solution.py:486
  45.2 0.0 copy-done.6
  45.2 6.8 %slopes.1 = (bf16[128,128,128]{2,1,0:T(8,128)(2,1)}, bf16[256,128]{1,0:T(8,128)(2,1)}) custom-call(bf16[256,128]{1,0:T(8,128)(2,1)S(1)} %bitcast.16, bf16[16,128]{1,0:T(8,128)(2,1)S(1)} %copy-done.6, bf16[128,32]{1,0:T(8,128)(2,1)S(1)} %copy-done.5, bf16[64,256]{1,0:T(8,128)(2,1)S(1)} %copy-done.7, ...), custom_call_target="tpu_custom_call" | custom-call | flops 536870912 | bytes 12582912 | tf_op jit(solution)/shard_map/slopes/pallas_call | solution.py:408
  51.9 4.8 %all-to-all-start.2 = ((bf16[64,4,128]{2,1,0:T(4,128)(2,1)}), bf16[64,4,128]{2,1,0:T(4,128)(2,1)S(1)}, u32[]{:S(2)}, u32[]{:S(2)}) async-start(bf16[64,4,128]{2,1,0:T(4,128)(2,1)} %bitcast.8), calls=%async_computation.2 | async-start | bytes 131072 | tf_op jit(solution)/shard_map/all_to_all | solution.py:486
  56.8 3.8 %pointwise.5 = (bf16[64,128,128]{2,1,0:T(8,128)(2,1)}, bf16[32,128,128]{2,1,0:T(8,128)(2,1)S(1)}, bf16[512,512]{1,0:T(8,128)(2,1)S(1)}) custom-call(bf16[64,64]{1,0:T(8,128)(2,1)S(1)} %copy-done.4, bf16[512,64]{1,0:T(8,128)(2,1)S(1)} %copy-done.1, bf16[128,128,128]{2,1,0:T(8,128)(2,1)} %get-tuple-element.35.refs_0_.slope_ref), custom_call_target="tpu_custom_call" | custom-call | flops 1073741824 | bytes 4194304 | tf_op jit(solution)/shard_map/pointwise/pallas_call | solution.py:447
  60.6 6.9 %all-to-all-done.2 = bf16[64,4,128]{2,1,0:T(4,128)(2,1)S(1)} async-done(((bf16[64,4,128]{2,1,0:T(4,128)(2,1)}), bf16[64,4,128]{2,1,0:T(4,128)(2,1)S(1)}, u32[]{:S(2)}, u32[]{:S(2)}) %all-to-all-start.2) | async-done | bytes 65568 | tf_op jit(solution)/shard_map/all_to_all | solution.py:486
  67.5 1.5 %mix_back.1 = (bf16[256,128]{1,0:T(8,128)(2,1)}, bf16[64,128]{1,0:T(8,128)(2,1)S(1)}) custom-call(bf16[256,128]{1,0:T(8,128)(2,1)S(1)} %bitcast.17, bf16[2,128,256]{2,1,0:T(8,128)(2,1)S(1)} %copy-done.3, bf16[2,256,128]{2,1,0:T(8,128)(2,1)S(1)} %copy-done.2, bf16[4,1024,64]{2,1,0:T(8,128)(2,1)S(1)} %bitcast.14, ...), custom_call_target="tpu_custom_call" | custom-call | flops 134217728 | bytes 2097152 | tf_op jit(solution)/shard_map/mix_back/pallas_call | solution.py:473
  69.0 4.6 %all-to-all-start.3 = ((bf16[64,4,128]{2,1,0:T(4,128)(2,1)}), bf16[64,4,128]{2,1,0:T(4,128)(2,1)S(1)}, u32[]{:S(2)}, u32[]{:S(2)}) async-start(bf16[64,4,128]{2,1,0:T(4,128)(2,1)} %bitcast.10), calls=%async_computation.3 | async-start | bytes 131072 | tf_op jit(solution)/shard_map/all_to_all | solution.py:486
  73.6 0.1 collective-permute-start.2
  73.7 0.7 collective-permute-start.1
  74.5 2.6 %collective-permute-start = (bf16[64,128]{1,0:T(8,128)(2,1)S(1)}, bf16[64,128]{1,0:T(8,128)(2,1)S(1)}, u32[]{:S(2)}, u32[]{:S(2)}) collective-permute-start(bf16[64,128]{1,0:T(8,128)(2,1)S(1)} %get-tuple-element.41.both0_ref), channel_id=1, source_target_pairs={{0,64},{64,0},{128,192},{192,128},{1,65},{65,1},{129,193},{193,129... | collective-permute-start | bytes 49160 | tf_op jit(solution)/shard_map/ppermute | solution.py:490
  77.1 1.3 %collective-permute-done.2.both3_ref = bf16[64,128]{1,0:T(8,128)(2,1)S(1)} collective-permute-done((bf16[64,128]{1,0:T(8,128)(2,1)S(1)}, bf16[64,128]{1,0:T(8,128)(2,1)S(1)}, u32[]{:S(2)}, u32[]{:S(2)}) %collective-permute-start.2) | collective-permute-done | bytes 16416 | tf_op jit(solution)/shard_map/ppermute | solution.py:490
  78.4 0.7 collective-permute-done.1.both2_ref
  79.1 0.0 collective-permute-done.both1_ref
  79.1 5.3 %all-to-all-done.3 = bf16[64,4,128]{2,1,0:T(4,128)(2,1)S(1)} async-done(((bf16[64,4,128]{2,1,0:T(4,128)(2,1)}), bf16[64,4,128]{2,1,0:T(4,128)(2,1)S(1)}, u32[]{:S(2)}, u32[]{:S(2)}) %all-to-all-start.3) | async-done | bytes 65568 | tf_op jit(solution)/shard_map/all_to_all | solution.py:486
  84.4 5.6 %result.1 = (bf16[128,128,128]{2,1,0:T(8,128)(2,1)}, f32[4,4,64,64]{3,2,1,0:T(8,128)}) custom-call(bf16[256,128]{1,0:T(8,128)(2,1)S(1)} %bitcast.15, bf16[16,128]{1,0:T(8,128)(2,1)S(1)} %copy-done.6, bf16[128,32]{1,0:T(8,128)(2,1)S(1)} %copy-done.5, bf16[512,512]{1,0:T(8,128)(2,1)S(1)} %get-tuple-element.40.wide_ref, ...), custom_call_target="tpu_custom_call" | custom-call | flops 1073741824 | bytes 8388608 | tf_op jit(solution)/shard_map/result/pallas_call | solution.py:424
  (8 shorter events, 0.0 us)
Async XLA Ops:
  0.6 16.6 %copy-start.1 = (bf16[512,64]{1,0:T(8,128)(2,1)S(1)}, bf16[512,64]{1,0:T(8,128)(2,1)}, u32[]{:S(2)}) copy-start(bf16[512,64]{1,0:T(8,128)(2,1)} %constant.16.clone.spread_ref) | copy-start | bytes 196612
  0.6 16.6 %copy-start.4 = (bf16[64,64]{1,0:T(8,128)(2,1)S(1)}, bf16[64,64]{1,0:T(8,128)(2,1)}, u32[]{:S(2)}) copy-start(bf16[64,64]{1,0:T(8,128)(2,1)} %weight_ref.5) | copy-start | bytes 24580
  0.7 16.6 %copy-start.8 = (f32[64]{0:T(128)S(1)}, f32[64]{0:T(128)}, u32[]{:S(2)}) copy-start(f32[64]{0:T(128)} %param.16) | copy-start | bytes 772
  4.5 23.4 %all-to-all-start = ((bf16[64,4,128]{2,1,0:T(4,128)(2,1)}), bf16[64,4,128]{2,1,0:T(4,128)(2,1)S(1)}, u32[]{:S(2)}, u32[]{:S(2)}) async-start(bf16[64,4,128]{2,1,0:T(4,128)(2,1)} %bitcast.1), calls=%async_computation | async-start | bytes 131072 | tf_op jit(solution)/shard_map/all_to_all | solution.py:486
  17.2 10.7 %copy-start = (bf16[4,16,64,64]{3,2,1,0:T(8,128)(2,1)S(1)}, bf16[4,16,64,64]{3,2,1,0:T(8,128)(2,1)}, u32[]{:S(2)}) copy-start(bf16[4,16,64,64]{3,2,1,0:T(8,128)(2,1)} %param.14) | copy-start | bytes 1572868
  17.2 10.7 %copy-start.2 = (bf16[2,256,128]{2,1,0:T(8,128)(2,1)S(1)}, bf16[2,256,128]{2,1,0:T(8,128)(2,1)}, u32[]{:S(2)}) copy-start(bf16[2,256,128]{2,1,0:T(8,128)(2,1)} %constant.20.clone.back_x_ref) | copy-start | bytes 393220
  17.2 10.7 %copy-start.3 = (bf16[2,128,256]{2,1,0:T(8,128)(2,1)S(1)}, bf16[2,128,256]{2,1,0:T(8,128)(2,1)}, u32[]{:S(2)}) copy-start(bf16[2,128,256]{2,1,0:T(8,128)(2,1)} %constant.19.clone.along_x_ref) | copy-start | bytes 393220
  21.6 23.6 %copy-start.5 = (bf16[128,32]{1,0:T(8,128)(2,1)S(1)}, bf16[128,32]{1,0:T(8,128)(2,1)}, u32[]{:S(2)}) copy-start(bf16[128,32]{1,0:T(8,128)(2,1)} %constant.17.clone.back_y_ref) | copy-start | bytes 24580
  21.6 23.5 %copy-start.6 = (bf16[16,128]{1,0:T(8,128)(2,1)S(1)}, bf16[16,128]{1,0:T(8,128)(2,1)}, u32[]{:S(2)}) copy-start(bf16[16,128]{1,0:T(8,128)(2,1)} %constant.18.clone.forward_z_ref.table_z_ref) | copy-start | bytes 12292
  21.6 23.5 %copy-start.7 = (bf16[64,256]{1,0:T(8,128)(2,1)S(1)}, bf16[64,256]{1,0:T(8,128)(2,1)}, u32[]{:S(2)}) copy-start(bf16[64,256]{1,0:T(8,128)(2,1)} %constant.15.clone.forward_y_ref) | copy-start | bytes 98308
  29.3 15.8 %all-to-all-start.1 = ((bf16[64,4,128]{2,1,0:T(4,128)(2,1)}), bf16[64,4,128]{2,1,0:T(4,128)(2,1)S(1)}, u32[]{:S(2)}, u32[]{:S(2)}) async-start(bf16[64,4,128]{2,1,0:T(4,128)(2,1)} %bitcast.6), calls=%async_computation.1 | async-start | bytes 131072 | tf_op jit(solution)/shard_map/all_to_all | solution.py:486
  51.9 15.6 %all-to-all-start.2 = ((bf16[64,4,128]{2,1,0:T(4,128)(2,1)}), bf16[64,4,128]{2,1,0:T(4,128)(2,1)S(1)}, u32[]{:S(2)}, u32[]{:S(2)}) async-start(bf16[64,4,128]{2,1,0:T(4,128)(2,1)} %bitcast.8), calls=%async_computation.2 | async-start | bytes 131072 | tf_op jit(solution)/shard_map/all_to_all | solution.py:486
  69.0 15.4 %all-to-all-start.3 = ((bf16[64,4,128]{2,1,0:T(4,128)(2,1)}), bf16[64,4,128]{2,1,0:T(4,128)(2,1)S(1)}, u32[]{:S(2)}, u32[]{:S(2)}) async-start(bf16[64,4,128]{2,1,0:T(4,128)(2,1)} %bitcast.10), calls=%async_computation.3 | async-start | bytes 131072 | tf_op jit(solution)/shard_map/all_to_all | solution.py:486
  73.6 4.8 %collective-permute-start.2 = (bf16[64,128]{1,0:T(8,128)(2,1)S(1)}, bf16[64,128]{1,0:T(8,128)(2,1)S(1)}, u32[]{:S(2)}, u32[]{:S(2)}) collective-permute-start(bf16[64,128]{1,0:T(8,128)(2,1)S(1)} %get-tuple-element.41.both0_ref), channel_id=1, source_target_pairs={{0,192},{64,128},{128,64},{192,0},{1,193},{65,129},{129,65},{193,1... | collective-permute-start | bytes 49160 | tf_op jit(solution)/shard_map/ppermute | solution.py:490
  73.7 5.3 %collective-permute-start.1 = (bf16[64,128]{1,0:T(8,128)(2,1)S(1)}, bf16[64,128]{1,0:T(8,128)(2,1)S(1)}, u32[]{:S(2)}, u32[]{:S(2)}) collective-permute-start(bf16[64,128]{1,0:T(8,128)(2,1)S(1)} %get-tuple-element.41.both0_ref), channel_id=1, source_target_pairs={{0,128},{64,192},{128,0},{192,64},{1,129},{65,193},{129,1},{193,65... | collective-permute-start | bytes 49160 | tf_op jit(solution)/shard_map/ppermute | solution.py:490
  74.5 4.6 %collective-permute-start = (bf16[64,128]{1,0:T(8,128)(2,1)S(1)}, bf16[64,128]{1,0:T(8,128)(2,1)S(1)}, u32[]{:S(2)}, u32[]{:S(2)}) collective-permute-start(bf16[64,128]{1,0:T(8,128)(2,1)S(1)} %get-tuple-element.41.both0_ref), channel_id=1, source_target_pairs={{0,64},{64,0},{128,192},{192,128},{1,65},{65,1},{129,193},{193,129... | collective-permute-start | bytes 49160 | tf_op jit(solution)/shard_map/ppermute | solution.py:490

commit v3 on v2

--- a/solution.py
+++ b/solution.py
@@ -67,12 +67,15 @@
     scratch[pl.ds(row + 2 * M, 2 * M), :] = modes[:, N:]
 
 
-def z_modes(scratch, forward_z, out_ref):
+def z_modes(scratch, forward_z, modes, out_ref, sem):
     for a in range(M):
         part = scratch[pl.ds(a, XC, stride=M), :].astype(BF)
-        out_ref[M * a : M * (a + 1), :] = lax.dot_general(
+        modes[M * a : M * (a + 1), :] = lax.dot_general(
             forward_z, part, (((1,), (1,)), ((), ())), preferred_element_type=F32
-        ).astype(out_ref.dtype)
+        ).astype(BF)
+    copy = pltpu.make_async_copy(modes, out_ref, sem)
+    copy.start()
+    return copy
 
 
 def from_z_modes(modes, table_z, scratch):
@@ -102,7 +105,7 @@
 
 
 def to_modes_kernel(
-    field_ref, forward_y_ref, forward_z_ref, out_ref, held, scratch, forward_y, forward_z, sems, small_sems
+    field_ref, forward_y_ref, forward_z_ref, out_ref, held, scratch, modes, forward_y, forward_z, sems, small_sems
 ):
     small = [
         pltpu.make_async_copy(forward_y_ref, forward_y, small_sems.at[0]),
@@ -117,12 +120,26 @@
         if g in copies:
             copies[g].wait()
         y_modes([held[g + j] for j in range(4)], forward_y[...], scratch, g * M)
-    z_modes(scratch, forward_z[...], out_ref)
+    z_modes(scratch, forward_z[...], modes, out_ref, small_sems.at[2]).wait()
 
 
 SLOPE_CUTS = (0, SLOPE_HEAD, 40, C, 96, 128)
-SLOPE_OUT_CUTS = (0, 32, 64, 96, 112, 128)
+SLOPE_OUT_CUTS = (0, 32, 64, 88, 104, 116, 128)
 RESULT_CUTS = (0, RESULT_HEAD, C, 96, 112, 128)
+AHEAD = 2
+BEHIND = 2
+
+
+def ahead_of(product, count):
+    ready = {}
+
+    def take(at):
+        for each in range(at, min(at + 2 * count + 2, XC), 2):
+            if each not in ready:
+                ready[each] = product(each)
+        return ready[at]
+
+    return take
 
 
 def doubled_slope(pre, cot):
@@ -135,7 +152,7 @@
 
 def slope_kernel(
     spatial_ref, table_z_ref, back_y_ref, forward_y_ref, point_head_ref, cot_head_ref,
-    point0_ref, point1_ref, cot_ref, slope_ref, out_ref, spread, scratch, point, cot, slope, sems,
+    point0_ref, point1_ref, cot_ref, slope_ref, out_ref, spread, scratch, modes, point, cot, slope, sems, out_sem,
 ):
     point_copies = pieces(point0_ref, point, sems.at[0], SLOPE_CUTS[1:4])
     point_copies |= pieces(point1_ref, point, sems.at[1], SLOPE_CUTS[3:], C)
@@ -145,7 +162,8 @@
         point_copies[low].start()
         cot_copies[low].start()
     from_z_modes(spatial_ref[...], table_z_ref[...], spread)
-    last = None
+    spectral = ahead_of(lambda at: from_y_modes(spread, back_y_ref[...], at * M).astype(BF), AHEAD)
+    waiting = []
     for first in range(0, XC, 4):
         if first in cot_copies:
             point_copies[first].wait()
@@ -153,26 +171,28 @@
         point_at, cot_at = (point, cot) if first >= SLOPE_HEAD else (point_head_ref, cot_head_ref)
         group = []
         for at in range(first, first + 4, 2):
-            both = from_y_modes(spread, back_y_ref[...], at * M).astype(BF)
+            both = spectral(at)
             for h in range(2):
                 value = doubled_slope(both[:, N * h : N * (h + 1)] + point_at[at + h], cot_at[at + h])
                 slope[at + h] = value
                 group.append(value)
-        if last is not None:
-            y_modes(last, forward_y_ref[...], scratch, (first - 4) * M)
-        last = group
+        waiting.append((group, first))
+        if len(waiting) > BEHIND:
+            group, row = waiting.pop(0)
+            y_modes(group, forward_y_ref[...], scratch, row * M)
         for low, high in zip(SLOPE_OUT_CUTS, SLOPE_OUT_CUTS[1:]):
             if first + 4 == high:
                 slope_copies[low].start()
-    y_modes(last, forward_y_ref[...], scratch, (XC - 4) * M)
-    z_modes(scratch, table_z_ref[...], out_ref)
-    for copy in slope_copies.values():
+    for group, row in waiting:
+        y_modes(group, forward_y_ref[...], scratch, row * M)
+    out_copy = z_modes(scratch, table_z_ref[...], modes, out_ref, out_sem)
+    for copy in (*slope_copies.values(), out_copy):
         copy.wait()
 
 
 def result_kernel(
     back_ref, table_z_ref, back_y_ref, wide_ref, both0_ref, both1_ref, both2_ref, both3_ref, head_ref,
-    point0_ref, slope_ref, out_ref, mode_grad_ref, spread, point, slope, held, grads, sems, row_sems,
+    point0_ref, slope_ref, out_ref, mode_grad_ref, spread, point, slope, held, grads, total, sems, row_sems, sem,
 ):
     (point_copy,) = pieces(point0_ref, point, sems.at[0], (RESULT_HEAD, C)).values()
     out_copies = pieces(held, out_ref, sems.at[1], RESULT_CUTS)
@@ -180,11 +200,16 @@
     point_copy.start()
     for k in range(STEPS // 2):
         slope_copy(k).start()
+    mode_gradient((both0_ref, both1_ref, both2_ref, both3_ref), grads, total)
+    mode_copy = pltpu.make_async_copy(total, mode_grad_ref, sem)
+    mode_copy.start()
     from_z_modes(back_ref[...], table_z_ref[...], spread)
+
+    spectral = ahead_of(lambda at: from_y_modes(spread, back_y_ref[...], at * M), 1)
 
     def finish(low, high):
         for g in range(low, high, 2):
-            both = from_y_modes(spread, back_y_ref[...], g * M)
+            both = spectral(g)
             for h in range(2):
                 other = head_ref[g + h] if g < RESULT_HEAD else point[g + h]
                 held[g + h] = (both[:, N * h : N * (h + 1)] + other.astype(F32)).astype(BF)
@@ -198,8 +223,7 @@
                 slope_copy(k).wait()
                 point_rows(slope, wide_ref, None, point.at[pl.ds(C, C)], k, 2 * YB)
         finish(low, high)
-    mode_gradient((both0_ref, both1_ref, both2_ref, both3_ref), grads, mode_grad_ref)
-    for copy in out_copies.values():
+    for copy in (*out_copies.values(), mode_copy):
         copy.wait()
 
 
@@ -372,7 +396,9 @@
 ALL_BYTES = XC * N * N * 2
 LARGE_OUT = pltpu.HBM((XC, N, N), BF)
 PLANE_OUT = pltpu.HBM((C, N, N), BF)
-MODES_OUT = jax.ShapeDtypeStruct((PAIRS, XC), BF)
+MODES_OUT = pltpu.HBM((PAIRS, XC), BF)
+MODES = pltpu.VMEM((PAIRS, XC), BF)
+SMALL_OUT = jax.ShapeDtypeStruct((PAIRS, XC), BF)
 OWN_OUT = jax.ShapeDtypeStruct((OWN * M, XC), BF)
 WHOLE = pltpu.VMEM((XC, N, N), BF)
 PLANE = pltpu.VMEM((C, N, N), BF)
@@ -392,11 +418,11 @@
     return pl.pallas_call(
         to_modes_kernel,
         in_specs=[LARGE] * 3,
-        out_specs=SMALL,
+        out_specs=LARGE,
         out_shape=MODES_OUT,
         scratch_shapes=[
-            WHOLE, SPREAD, *[pltpu.VMEM(each.shape, BF) for each in small],
-            pltpu.SemaphoreType.DMA((len(FIELD_CUTS) - 1,)), pltpu.SemaphoreType.DMA((2,)),
+            WHOLE, SPREAD, MODES, *[pltpu.VMEM(each.shape, BF) for each in small],
+            pltpu.SemaphoreType.DMA((len(FIELD_CUTS) - 1,)), pltpu.SemaphoreType.DMA((3,)),
         ],
         compiler_params=params(40),
         cost_estimate=cost(XC * N * N * 128, ALL_BYTES),
@@ -408,9 +434,10 @@
     return pl.pallas_call(
         slope_kernel,
         in_specs=[SMALL] * 6 + [LARGE] * 3,
-        out_specs=(LARGE, SMALL),
+        out_specs=(LARGE, LARGE),
         out_shape=(LARGE_OUT, MODES_OUT),
-        scratch_shapes=[SPREAD] * 2 + [WHOLE] * 3 + [sems(4, len(SLOPE_OUT_CUTS))],
+        scratch_shapes=[SPREAD] * 2 + [MODES] + [WHOLE] * 3
+        + [sems(4, len(SLOPE_OUT_CUTS)), pltpu.SemaphoreType.DMA],
         compiler_params=params(40),
         cost_estimate=cost(XC * N * N * 256, 3 * ALL_BYTES),
         name="slopes",
@@ -424,11 +451,11 @@
     return pl.pallas_call(
         result_kernel,
         in_specs=[SMALL] * 9 + [LARGE] * 2,
-        out_specs=(LARGE, SMALL),
-        out_shape=(LARGE_OUT, jax.ShapeDtypeStruct((OWN, M // 4, C, C), F32)),
+        out_specs=(LARGE, LARGE),
+        out_shape=(LARGE_OUT, pltpu.HBM((OWN, M // 4, C, C), F32)),
         scratch_shapes=[
-            SPREAD, WHOLE, PLANE, WHOLE, pltpu.VMEM((4, OWN * M, XC), F32),
-            sems(2, len(RESULT_CUTS)), pltpu.SemaphoreType.DMA((STEPS,)),
+            SPREAD, WHOLE, PLANE, WHOLE, pltpu.VMEM((4, OWN * M, XC), F32), pltpu.VMEM((OWN, M // 4, C, C), F32),
+            sems(2, len(RESULT_CUTS)), pltpu.SemaphoreType.DMA((STEPS,)), pltpu.SemaphoreType.DMA,
         ],
         compiler_params=params(40),
         cost_estimate=cost(XC * N * N * 512, 2 * ALL_BYTES),
@@ -462,7 +489,7 @@
         mix_kernel,
         in_specs=[SMALL] * 4,
         out_specs=(SMALL, SMALL),
-        out_shape=(MODES_OUT, OWN_OUT),
+        out_shape=(SMALL_OUT, OWN_OUT),
         compiler_params=params(40),
         cost_estimate=cost(1 << 27, 1 << 21),
         name="mix",
@@ -474,7 +501,7 @@
         mix_back_kernel,
         in_specs=[SMALL] * 5,
         out_specs=(SMALL, SMALL),
-        out_shape=(MODES_OUT, OWN_OUT),
+        out_shape=(SMALL_OUT, OWN_OUT),
         compiler_params=params(40),
         cost_estimate=cost(1 << 27, 1 << 21),
         name="mix_back",
@@ -487,7 +514,11 @@
 
 
 def over_samples(both):
-    return [both] + [lax.ppermute(both, "dp", [(i, i ^ k) for i in range(4)]) for k in range(1, 4)]
+    def swap(array, k):
+        return lax.ppermute(array, "dp", [(i, i ^ k) for i in range(4)])
+
+    far = swap(both, 2)
+    return [both, far, swap(both, 1), swap(far, 1)]
 
 
 def per_device(field, cotangent, mode_weight, point_weight, point_bias):

time: 90.5 us -> 88.7 us (0.980)
  starting transfers between devices: 30.6 us -> 27.9 us
  waiting for transfers between devices: 27.1 us -> 29.8 us
  Pallas kernels: 31.5 us -> 29.7 us
    ppermute x3, waiting for transfers between devices: 1.99 us -> 5.86 us  [swap(): return lax.ppermute(array, 'dp', [(i, i ^ k) for i in range(4)])]
    ppermute x3, starting transfers between devices: 3.44 us -> 0.68 us  [swap(): return lax.ppermute(array, 'dp', [(i, i ^ k) for i in range(4)])]
    all_to_all x4, waiting for transfers between devices: 25.1 us -> 23.9 us  [exchange(): lax.all_to_all(cut, 'space', split_axis=0, concat_axis=0, tiled=True)]
    pallas_call x1, Pallas kernels: 6.76 us -> 5.67 us  [slopes(): pl.pallas_call(slope_kernel, in_specs=[SMALL] * 6 + [LARGE] * 3, out_spec...]
where the time goes in v3:
time: 88.7 us; the launch traced here: 88.4 us
  waiting for transfers between devices  29.8 us (34%)
  Pallas kernels  29.7 us (33%)
  starting transfers between devices  27.9 us (31%)
  between operations  0.97 us (1%)
    all_to_all x4, starting transfers between devices, exchange(): lax.all_to_all(cut, 'space', split_axis=0, concat_axis=0, tiled=True)  27.2 us
    all_to_all x4, waiting for transfers between devices, exchange(): lax.all_to_all(cut, 'space', split_axis=0, concat_axis=0, tiled=True)  23.9 us
    pallas_call x3, Pallas kernels, pointwise(): pl.pallas_call(functools.partial(point_kernel, plane, back), in_specs=[SM...  12.4 us
    ppermute x3, waiting for transfers between devices, swap(): return lax.ppermute(array, 'dp', [(i, i ^ k) for i in range(4)])  5.86 us
    pallas_call x1, Pallas kernels, slopes(): pl.pallas_call(slope_kernel, in_specs=[SMALL] * 6 + [LARGE] * 3, out_spec...  5.67 us
    pallas_call x1, Pallas kernels, result(): pl.pallas_call(result_kernel, in_specs=[SMALL] * 9 + [LARGE] * 2, out_spe...  4.91 us
    pallas_call x1, Pallas kernels, to_modes(): pl.pallas_call(to_modes_kernel, in_specs=[LARGE] * 3, out_specs=LARGE, ou...  3.84 us
  transfers between devices with their start and end apart: 7, of which 6 were waited for; matrix products, arithmetic and copies ran while one was open for 0% of the time, Pallas kernels for 14%

profile of v3, /device:TPU:16, one launch (start us, length us, event | category | flops | bytes accessed | tf_op | source)
XLA Modules:
  0.0 88.4 jit_solution(5213634109472512582)
XLA Ops:
  0.6 0.0 copy-start.1
  0.6 0.0 copy-start.4
  0.7 0.0 copy-start.8
  0.7 3.8 %to_modes.1 = bf16[256,128]{1,0:T(8,128)(2,1)} custom-call(bf16[128,128,128]{2,1,0:T(8,128)(2,1)} %bitcast.21, bf16[64,256]{1,0:T(8,128)(2,1)} %constant.14.clone.forward_y_ref, bf16[16,128]{1,0:T(8,128)(2,1)} %constant.18.clone.forward_z_ref.table_z_ref), custom_call_target="tpu_custom_call" | custom-call | flops 268435456 | bytes 4194304 | tf_op jit(solution)/shard_map/to_modes/pallas_call | solution.py:418
  4.5 12.7 %all-to-all-start = ((bf16[64,4,128]{2,1,0:T(4,128)(2,1)}), bf16[64,4,128]{2,1,0:T(4,128)(2,1)S(1)}, u32[]{:S(2)}, u32[]{:S(2)}) async-start(bf16[64,4,128]{2,1,0:T(4,128)(2,1)} %bitcast.26), calls=%async_computation | async-start | bytes 131072 | tf_op jit(solution)/shard_map/all_to_all | solution.py:513
  17.2 0.0 copy-done.1
  17.2 0.0 copy-start
  17.2 0.0 copy-start.2
  17.2 0.0 copy-start.3
  17.3 4.3 %pointwise.3 = (bf16[64,128,128]{2,1,0:T(8,128)(2,1)}, bf16[16,128,128]{2,1,0:T(8,128)(2,1)S(1)}, bf16[16,128,128]{2,1,0:T(8,128)(2,1)S(1)}) custom-call(bf16[64,64]{1,0:T(8,128)(2,1)S(1)} %copy-done.4, bf16[512,64]{1,0:T(8,128)(2,1)S(1)} %copy-done.1, f32[1,64]{1,0:T(1,128)S(1)} %bitcast.19, bf16[128,128,128]{2,1,0:T(8,128)(2,1)} %bitcast.24, ...), custom_call_target="tpu_custom_call" | custom-call | flops 1073741824 | bytes 4194304 | tf_op jit(solution)/shard_map/pointwise/pallas_call | solution.py:474
  21.6 0.0 copy-start.5
  21.6 0.0 copy-start.6
  21.6 0.0 copy-start.7
  21.6 6.3 %all-to-all-done = bf16[64,4,128]{2,1,0:T(4,128)(2,1)S(1)} async-done(((bf16[64,4,128]{2,1,0:T(4,128)(2,1)}), bf16[64,4,128]{2,1,0:T(4,128)(2,1)S(1)}, u32[]{:S(2)}, u32[]{:S(2)}) %all-to-all-start) | async-done | bytes 65568 | tf_op jit(solution)/shard_map/all_to_all | solution.py:513
  28.0 1.4 %mix.1 = (bf16[256,128]{1,0:T(8,128)(2,1)}, bf16[64,128]{1,0:T(8,128)(2,1)S(1)}) custom-call(bf16[256,128]{1,0:T(8,128)(2,1)S(1)} %bitcast.18, bf16[2,128,256]{2,1,0:T(8,128)(2,1)S(1)} %copy-done.3, bf16[2,256,128]{2,1,0:T(8,128)(2,1)S(1)} %copy-done.2, bf16[4,1024,64]{2,1,0:T(8,128)(2,1)S(1)} %bitcast.13), custom_call_target="tpu_custom_call" | custom-call | flops 134217728 | bytes 2097152 | tf_op jit(solution)/shard_map/mix/pallas_call | solution.py:488
  29.4 5.0 %all-to-all-start.1 = ((bf16[64,4,128]{2,1,0:T(4,128)(2,1)}), bf16[64,4,128]{2,1,0:T(4,128)(2,1)S(1)}, u32[]{:S(2)}, u32[]{:S(2)}) async-start(bf16[64,4,128]{2,1,0:T(4,128)(2,1)} %bitcast.6), calls=%async_computation.1 | async-start | bytes 131072 | tf_op jit(solution)/shard_map/all_to_all | solution.py:513
  34.4 4.2 %pointwise.4.point1_ref = bf16[64,128,128]{2,1,0:T(8,128)(2,1)} custom-call(bf16[64,64]{1,0:T(8,128)(2,1)S(1)} %copy-done.4, bf16[512,64]{1,0:T(8,128)(2,1)S(1)} %copy-done.1, f32[1,64]{1,0:T(1,128)S(1)} %bitcast.20, bf16[128,128,128]{2,1,0:T(8,128)(2,1)} %bitcast.23), custom_call_target="tpu_custom_call" | custom-call | flops 1073741824 | bytes 4194304 | tf_op jit(solution)/shard_map/pointwise/pallas_call | solution.py:474
  38.5 6.6 %all-to-all-done.1 = bf16[64,4,128]{2,1,0:T(4,128)(2,1)S(1)} async-done(((bf16[64,4,128]{2,1,0:T(4,128)(2,1)}), bf16[64,4,128]{2,1,0:T(4,128)(2,1)S(1)}, u32[]{:S(2)}, u32[]{:S(2)}) %all-to-all-start.1) | async-done | bytes 65568 | tf_op jit(solution)/shard_map/all_to_all | solution.py:513
  45.2 5.7 %slopes.1 = (bf16[128,128,128]{2,1,0:T(8,128)(2,1)}, bf16[256,128]{1,0:T(8,128)(2,1)}) custom-call(bf16[256,128]{1,0:T(8,128)(2,1)S(1)} %bitcast.16, bf16[16,128]{1,0:T(8,128)(2,1)S(1)} %copy-done.6, bf16[128,32]{1,0:T(8,128)(2,1)S(1)} %copy-done.5, bf16[64,256]{1,0:T(8,128)(2,1)S(1)} %copy-done.7, ...), custom_call_target="tpu_custom_call" | custom-call | flops 536870912 | bytes 12582912 | tf_op jit(solution)/shard_map/slopes/pallas_call | solution.py:434
  50.8 4.9 %all-to-all-start.2 = ((bf16[64,4,128]{2,1,0:T(4,128)(2,1)}), bf16[64,4,128]{2,1,0:T(4,128)(2,1)S(1)}, u32[]{:S(2)}, u32[]{:S(2)}) async-start(bf16[64,4,128]{2,1,0:T(4,128)(2,1)} %bitcast.27), calls=%async_computation.2 | async-start | bytes 131072 | tf_op jit(solution)/shard_map/all_to_all | solution.py:513
  55.8 3.8 %pointwise.5 = (bf16[64,128,128]{2,1,0:T(8,128)(2,1)}, bf16[32,128,128]{2,1,0:T(8,128)(2,1)S(1)}, bf16[512,512]{1,0:T(8,128)(2,1)S(1)}) custom-call(bf16[64,64]{1,0:T(8,128)(2,1)S(1)} %copy-done.4, bf16[512,64]{1,0:T(8,128)(2,1)S(1)} %copy-done.1, bf16[128,128,128]{2,1,0:T(8,128)(2,1)} %get-tuple-element.35.refs_0_.slope_ref), custom_call_target="tpu_custom_call" | custom-call | flops 1073741824 | bytes 4194304 | tf_op jit(solution)/shard_map/pointwise/pallas_call | solution.py:474
  59.6 6.8 %all-to-all-done.2 = bf16[64,4,128]{2,1,0:T(4,128)(2,1)S(1)} async-done(((bf16[64,4,128]{2,1,0:T(4,128)(2,1)}), bf16[64,4,128]{2,1,0:T(4,128)(2,1)S(1)}, u32[]{:S(2)}, u32[]{:S(2)}) %all-to-all-start.2) | async-done | bytes 65568 | tf_op jit(solution)/shard_map/all_to_all | solution.py:513
  66.4 1.5 %mix_back.1 = (bf16[256,128]{1,0:T(8,128)(2,1)}, bf16[64,128]{1,0:T(8,128)(2,1)S(1)}) custom-call(bf16[256,128]{1,0:T(8,128)(2,1)S(1)} %bitcast.17, bf16[2,128,256]{2,1,0:T(8,128)(2,1)S(1)} %copy-done.3, bf16[2,256,128]{2,1,0:T(8,128)(2,1)S(1)} %copy-done.2, bf16[4,1024,64]{2,1,0:T(8,128)(2,1)S(1)} %bitcast.14, ...), custom_call_target="tpu_custom_call" | custom-call | flops 134217728 | bytes 2097152 | tf_op jit(solution)/shard_map/mix_back/pallas_call | solution.py:500
  67.9 4.6 %all-to-all-start.3 = ((bf16[64,4,128]{2,1,0:T(4,128)(2,1)}), bf16[64,4,128]{2,1,0:T(4,128)(2,1)S(1)}, u32[]{:S(2)}, u32[]{:S(2)}) async-start(bf16[64,4,128]{2,1,0:T(4,128)(2,1)} %bitcast.10), calls=%async_computation.3 | async-start | bytes 131072 | tf_op jit(solution)/shard_map/all_to_all | solution.py:513
  72.5 0.7 collective-permute-start
  73.2 0.0 collective-permute-start.1
  73.2 4.7 %collective-permute-done.both1_ref = bf16[64,128]{1,0:T(8,128)(2,1)S(1)} collective-permute-done((bf16[64,128]{1,0:T(8,128)(2,1)S(1)}, bf16[64,128]{1,0:T(8,128)(2,1)S(1)}, u32[]{:S(2)}, u32[]{:S(2)}) %collective-permute-start) | collective-permute-done | bytes 16416 | tf_op jit(solution)/shard_map/ppermute | solution.py:518
  77.9 0.0 collective-permute-start.2
  77.9 0.0 collective-permute-done.1.both2_ref
  77.9 1.2 %collective-permute-done.2.both3_ref = bf16[64,128]{1,0:T(8,128)(2,1)S(1)} collective-permute-done((bf16[64,128]{1,0:T(8,128)(2,1)S(1)}, bf16[64,128]{1,0:T(8,128)(2,1)S(1)}, u32[]{:S(2)}, u32[]{:S(2)}) %collective-permute-start.2) | collective-permute-done | bytes 16416 | tf_op jit(solution)/shard_map/ppermute | solution.py:518
  79.1 4.2 %all-to-all-done.3 = bf16[64,4,128]{2,1,0:T(4,128)(2,1)S(1)} async-done(((bf16[64,4,128]{2,1,0:T(4,128)(2,1)}), bf16[64,4,128]{2,1,0:T(4,128)(2,1)S(1)}, u32[]{:S(2)}, u32[]{:S(2)}) %all-to-all-start.3) | async-done | bytes 65568 | tf_op jit(solution)/shard_map/all_to_all | solution.py:513
  83.3 4.9 %result.1 = (bf16[128,128,128]{2,1,0:T(8,128)(2,1)}, f32[4,4,64,64]{3,2,1,0:T(8,128)}) custom-call(bf16[256,128]{1,0:T(8,128)(2,1)S(1)} %bitcast.15, bf16[16,128]{1,0:T(8,128)(2,1)S(1)} %copy-done.6, bf16[128,32]{1,0:T(8,128)(2,1)S(1)} %copy-done.5, bf16[512,512]{1,0:T(8,128)(2,1)S(1)} %get-tuple-element.40.wide_ref, ...), custom_call_target="tpu_custom_call" | custom-call | flops 1073741824 | bytes 8388608 | tf_op jit(solution)/shard_map/result/pallas_call | solution.py:451
  (8 shorter events, 0.0 us)
Async XLA Ops:
  0.6 16.6 %copy-start.1 = (bf16[512,64]{1,0:T(8,128)(2,1)S(1)}, bf16[512,64]{1,0:T(8,128)(2,1)}, u32[]{:S(2)}) copy-start(bf16[512,64]{1,0:T(8,128)(2,1)} %constant.16.clone.spread_ref) | copy-start | bytes 196612
  0.6 16.6 %copy-start.4 = (bf16[64,64]{1,0:T(8,128)(2,1)S(1)}, bf16[64,64]{1,0:T(8,128)(2,1)}, u32[]{:S(2)}) copy-start(bf16[64,64]{1,0:T(8,128)(2,1)} %weight_ref.5) | copy-start | bytes 24580
  0.7 16.6 %copy-start.8 = (f32[64]{0:T(128)S(1)}, f32[64]{0:T(128)}, u32[]{:S(2)}) copy-start(f32[64]{0:T(128)} %param.16) | copy-start | bytes 772
  4.5 23.4 %all-to-all-start = ((bf16[64,4,128]{2,1,0:T(4,128)(2,1)}), bf16[64,4,128]{2,1,0:T(4,128)(2,1)S(1)}, u32[]{:S(2)}, u32[]{:S(2)}) async-start(bf16[64,4,128]{2,1,0:T(4,128)(2,1)} %bitcast.26), calls=%async_computation | async-start | bytes 131072 | tf_op jit(solution)/shard_map/all_to_all | solution.py:513
  17.2 10.7 %copy-start = (bf16[4,16,64,64]{3,2,1,0:T(8,128)(2,1)S(1)}, bf16[4,16,64,64]{3,2,1,0:T(8,128)(2,1)}, u32[]{:S(2)}) copy-start(bf16[4,16,64,64]{3,2,1,0:T(8,128)(2,1)} %param.14) | copy-start | bytes 1572868
  17.2 10.7 %copy-start.2 = (bf16[2,256,128]{2,1,0:T(8,128)(2,1)S(1)}, bf16[2,256,128]{2,1,0:T(8,128)(2,1)}, u32[]{:S(2)}) copy-start(bf16[2,256,128]{2,1,0:T(8,128)(2,1)} %constant.20.clone.back_x_ref) | copy-start | bytes 393220
  17.2 10.7 %copy-start.3 = (bf16[2,128,256]{2,1,0:T(8,128)(2,1)S(1)}, bf16[2,128,256]{2,1,0:T(8,128)(2,1)}, u32[]{:S(2)}) copy-start(bf16[2,128,256]{2,1,0:T(8,128)(2,1)} %constant.19.clone.along_x_ref) | copy-start | bytes 393220
  21.6 23.6 %copy-start.5 = (bf16[128,32]{1,0:T(8,128)(2,1)S(1)}, bf16[128,32]{1,0:T(8,128)(2,1)}, u32[]{:S(2)}) copy-start(bf16[128,32]{1,0:T(8,128)(2,1)} %constant.17.clone.back_y_ref) | copy-start | bytes 24580
  21.6 23.5 %copy-start.6 = (bf16[16,128]{1,0:T(8,128)(2,1)S(1)}, bf16[16,128]{1,0:T(8,128)(2,1)}, u32[]{:S(2)}) copy-start(bf16[16,128]{1,0:T(8,128)(2,1)} %constant.18.clone.forward_z_ref.table_z_ref) | copy-start | bytes 12292
  21.6 23.5 %copy-start.7 = (bf16[64,256]{1,0:T(8,128)(2,1)S(1)}, bf16[64,256]{1,0:T(8,128)(2,1)}, u32[]{:S(2)}) copy-start(bf16[64,256]{1,0:T(8,128)(2,1)} %constant.15.clone.forward_y_ref) | copy-start | bytes 98308
  29.4 15.8 %all-to-all-start.1 = ((bf16[64,4,128]{2,1,0:T(4,128)(2,1)}), bf16[64,4,128]{2,1,0:T(4,128)(2,1)S(1)}, u32[]{:S(2)}, u32[]{:S(2)}) async-start(bf16[64,4,128]{2,1,0:T(4,128)(2,1)} %bitcast.6), calls=%async_computation.1 | async-start | bytes 131072 | tf_op jit(solution)/shard_map/all_to_all | solution.py:513
  50.8 15.5 %all-to-all-start.2 = ((bf16[64,4,128]{2,1,0:T(4,128)(2,1)}), bf16[64,4,128]{2,1,0:T(4,128)(2,1)S(1)}, u32[]{:S(2)}, u32[]{:S(2)}) async-start(bf16[64,4,128]{2,1,0:T(4,128)(2,1)} %bitcast.27), calls=%async_computation.2 | async-start | bytes 131072 | tf_op jit(solution)/shard_map/all_to_all | solution.py:513
  67.9 15.4 %all-to-all-start.3 = ((bf16[64,4,128]{2,1,0:T(4,128)(2,1)}), bf16[64,4,128]{2,1,0:T(4,128)(2,1)S(1)}, u32[]{:S(2)}, u32[]{:S(2)}) async-start(bf16[64,4,128]{2,1,0:T(4,128)(2,1)} %bitcast.10), calls=%async_computation.3 | async-start | bytes 131072 | tf_op jit(solution)/shard_map/all_to_all | solution.py:513
  72.5 5.4 %collective-permute-start = (bf16[64,128]{1,0:T(8,128)(2,1)S(1)}, bf16[64,128]{1,0:T(8,128)(2,1)S(1)}, u32[]{:S(2)}, u32[]{:S(2)}) collective-permute-start(bf16[64,128]{1,0:T(8,128)(2,1)S(1)} %get-tuple-element.41.both0_ref), channel_id=1, source_target_pairs={{0,128},{64,192},{128,0},{192,64},{1,129},{65,193},{129,1},{193,65... | collective-permute-start | bytes 49160 | tf_op jit(solution)/shard_map/ppermute | solution.py:518
  73.2 4.7 %collective-permute-start.1 = (bf16[64,128]{1,0:T(8,128)(2,1)S(1)}, bf16[64,128]{1,0:T(8,128)(2,1)S(1)}, u32[]{:S(2)}, u32[]{:S(2)}) collective-permute-start(bf16[64,128]{1,0:T(8,128)(2,1)S(1)} %get-tuple-element.41.both0_ref), channel_id=1, source_target_pairs={{0,64},{64,0},{128,192},{192,128},{1,65},{65,1},{129,193},{193,129... | collective-permute-start | bytes 49160 | tf_op jit(solution)/shard_map/ppermute | solution.py:518
  77.9 1.2 %collective-permute-start.2 = (bf16[64,128]{1,0:T(8,128)(2,1)S(1)}, bf16[64,128]{1,0:T(8,128)(2,1)S(1)}, u32[]{:S(2)}, u32[]{:S(2)}) collective-permute-start(bf16[64,128]{1,0:T(8,128)(2,1)S(1)} %collective-permute-done.both1_ref), channel_id=1, source_target_pairs={{0,64},{64,0},{128,192},{192,128},{1,65},{65,1},{129,193},{193,129... | collective-permute-start | bytes 49160 | tf_op jit(solution)/shard_map/ppermute | solution.py:518

commit v4 on v3

--- a/solution.py
+++ b/solution.py
@@ -125,7 +125,7 @@
 
 SLOPE_CUTS = (0, SLOPE_HEAD, 40, C, 96, 128)
 SLOPE_OUT_CUTS = (0, 32, 64, 88, 104, 116, 128)
-RESULT_CUTS = (0, RESULT_HEAD, C, 96, 112, 128)
+RESULT_CUTS = (0, RESULT_HEAD, C, C + RESULT_HEAD, 112, 128)
 AHEAD = 2
 BEHIND = 2
 
@@ -191,38 +191,30 @@
 
 
 def result_kernel(
-    back_ref, table_z_ref, back_y_ref, wide_ref, both0_ref, both1_ref, both2_ref, both3_ref, head_ref,
-    point0_ref, slope_ref, out_ref, mode_grad_ref, spread, point, slope, held, grads, total, sems, row_sems, sem,
+    back_ref, table_z_ref, back_y_ref, both0_ref, both1_ref, both2_ref, both3_ref, head0_ref, head1_ref,
+    point0_ref, point1_ref, out_ref, mode_grad_ref, spread, point, held, grads, total, sems, sem,
 ):
-    (point_copy,) = pieces(point0_ref, point, sems.at[0], (RESULT_HEAD, C)).values()
-    out_copies = pieces(held, out_ref, sems.at[1], RESULT_CUTS)
-    slope_copy = fetch_rows(slope_ref.at[pl.ds(C, C)], slope, row_sems, 2 * YB)
-    point_copy.start()
-    for k in range(STEPS // 2):
-        slope_copy(k).start()
+    head = head0_ref.shape[0]
+    point_copies = pieces(point0_ref, point, sems.at[0], (head, C))
+    point_copies |= pieces(point1_ref, point, sems.at[1], (C + head, XC), C)
+    out_copies = pieces(held, out_ref, sems.at[2], RESULT_CUTS)
+    for copy in point_copies.values():
+        copy.start()
     mode_gradient((both0_ref, both1_ref, both2_ref, both3_ref), grads, total)
     mode_copy = pltpu.make_async_copy(total, mode_grad_ref, sem)
     mode_copy.start()
     from_z_modes(back_ref[...], table_z_ref[...], spread)
-
     spectral = ahead_of(lambda at: from_y_modes(spread, back_y_ref[...], at * M), 1)
-
-    def finish(low, high):
+    for low, high in zip(RESULT_CUTS, RESULT_CUTS[1:]):
+        if low in point_copies:
+            point_copies[low].wait()
         for g in range(low, high, 2):
             both = spectral(g)
             for h in range(2):
-                other = head_ref[g + h] if g < RESULT_HEAD else point[g + h]
+                plane, channel = divmod(g + h, C)
+                other = (head0_ref, head1_ref)[plane][channel] if channel < head else point[g + h]
                 held[g + h] = (both[:, N * h : N * (h + 1)] + other.astype(F32)).astype(BF)
         out_copies[low].start()
-
-    for low, high in zip(RESULT_CUTS, RESULT_CUTS[1:]):
-        if low == RESULT_HEAD:
-            point_copy.wait()
-        if low == C:
-            for k in range(STEPS // 2):
-                slope_copy(k).wait()
-                point_rows(slope, wide_ref, None, point.at[pl.ds(C, C)], k, 2 * YB)
-        finish(low, high)
     for copy in (*out_copies.values(), mode_copy):
         copy.wait()
 
@@ -292,37 +284,54 @@
             )
 
 
-def point_kernel(plane, back, weight_ref, spread_ref, *refs):
-    refs, (array, out, bias, sems, head_sem) = refs[:-5], refs[-5:]
-    if back:
-        in_ref, out_ref, head_ref, wide = refs
-    elif plane:
-        bias_ref, in_ref, out_ref, wide = refs
+def point_kernel(plane, weight_ref, spread_ref, bias_ref, *refs):
+    refs, (array, out, bias, wide, sems, head_sem) = refs[:-6], refs[-6:]
+    if plane:
+        in_ref, out_ref = refs
     else:
-        bias_ref, cot_ref, in_ref, out_ref, head_ref, cot_head_ref, wide = refs
+        cot_ref, in_ref, out_ref, head_ref, cot_head_ref = refs
+        head_copy = pltpu.make_async_copy(cot_ref.at[pl.ds(0, SLOPE_HEAD)], cot_head_ref, head_sem)
     copy = fetch_rows(in_ref.at[pl.ds(plane * C, C)], array, sems.at[0])
     out_copy = fetch_rows(out, out_ref, sems.at[1])
     for k in range(STEPS):
         copy(k).start()
-    if not back and not plane:
-        head_copy = pltpu.make_async_copy(cot_ref.at[pl.ds(0, SLOPE_HEAD)], cot_head_ref, head_sem)
+    if not plane:
         head_copy.start()
-    if not back:
-        bias[...] = lax.dot_general(
-            spread_ref[...].astype(F32), jnp.broadcast_to(bias_ref[...], (N, C)), (((1,), (1,)), ((), ())),
-            precision=lax.Precision.HIGHEST, preferred_element_type=F32,
-        )
-    widen(weight_ref, spread_ref, wide, not back, 0.5 if back else 1.0)
+    bias[...] = lax.dot_general(
+        spread_ref[...].astype(F32), jnp.broadcast_to(bias_ref[...], (N, C)), (((1,), (1,)), ((), ())),
+        precision=lax.Precision.HIGHEST, preferred_element_type=F32,
+    )
+    widen(weight_ref, spread_ref, wide, True, 1.0)
     for k in range(STEPS):
         copy(k).wait()
-        point_rows(array, wide, None if back else bias, out, k)
+        point_rows(array, wide, bias, out, k)
         out_copy(k).start()
     if not plane:
-        head_ref[...] = out[: head_ref.shape[0]]
+        head_ref[...] = out[:SLOPE_HEAD]
+        head_copy.wait()
     for k in range(STEPS):
         out_copy(k).wait()
-    if not back and not plane:
-        head_copy.wait()
+
+
+def point_back_kernel(plane, *refs):
+    refs, (array, out, sems) = refs[:-3], refs[-3:]
+    if plane:
+        wide, in_ref, out_ref, head_ref = refs
+    else:
+        weight_ref, spread_ref, in_ref, out_ref, head_ref, wide = refs
+    copy = fetch_rows(in_ref.at[pl.ds(plane * C, C)], array, sems.at[0])
+    out_copy = fetch_rows(out, out_ref, sems.at[1])
+    for k in range(STEPS):
+        copy(k).start()
+    if not plane:
+        widen(weight_ref, spread_ref, wide, False, 0.5)
+    for k in range(STEPS):
+        copy(k).wait()
+        point_rows(array, wide, None, out, k)
+        out_copy(k).start()
+    head_ref[...] = out[:RESULT_HEAD]
+    for k in range(STEPS):
+        out_copy(k).wait()
 
 
 def x_modes(received, along_x):
@@ -447,41 +456,51 @@
     )
 
 
-def result(back, wide, samples, head, point0, slope, table):
+def result(back, samples, heads, points, table):
     return pl.pallas_call(
         result_kernel,
         in_specs=[SMALL] * 9 + [LARGE] * 2,
         out_specs=(LARGE, LARGE),
         out_shape=(LARGE_OUT, pltpu.HBM((OWN, M // 4, C, C), F32)),
         scratch_shapes=[
-            SPREAD, WHOLE, PLANE, WHOLE, pltpu.VMEM((4, OWN * M, XC), F32), pltpu.VMEM((OWN, M // 4, C, C), F32),
-            sems(2, len(RESULT_CUTS)), pltpu.SemaphoreType.DMA((STEPS,)), pltpu.SemaphoreType.DMA,
+            SPREAD, WHOLE, WHOLE, pltpu.VMEM((4, OWN * M, XC), F32), pltpu.VMEM((OWN, M // 4, C, C), F32),
+            sems(3, len(RESULT_CUTS)), pltpu.SemaphoreType.DMA,
         ],
         compiler_params=params(40),
-        cost_estimate=cost(XC * N * N * 512, 2 * ALL_BYTES),
+        cost_estimate=cost(XC * N * N * 128, 2 * ALL_BYTES),
         name="result",
-    )(
-        back, table["forward_z"], table["back_y"], wide, *samples, head, large(point0), large(slope)
-    )
-
-
-def pointwise(plane, back, weight, bias, array, table, cot=None):
-    operands = [weight, table["spread"]] + ([] if back else [bias.reshape(1, C)])
+    )(back, table["forward_z"], table["back_y"], *samples, *heads, *map(large, points))
+
+
+WIDENED = pltpu.VMEM((WIDE, WIDE), BF)
+HALF = dict(
+    compiler_params=params(40), cost_estimate=cost(C * N * N * 1024, ALL_BYTES), name="pointwise"
+)
+
+
+def pointwise(plane, weight, bias, array, table, cot=None):
     sources = ([] if cot is None else [cot]) + [array]
-    wide = pltpu.VMEM((WIDE, WIDE), BF)
-    head = pltpu.VMEM((RESULT_HEAD if back else SLOPE_HEAD, N, N), BF)
-    kept = [head] * (0 if plane else 1 + (cot is not None)) + [wide] * back
-    return pl.pallas_call(
-        functools.partial(point_kernel, plane, back),
-        in_specs=[SMALL] * len(operands) + [LARGE] * len(sources),
+    heads = [pltpu.VMEM((SLOPE_HEAD, N, N), BF)] * (0 if plane else 2)
+    return pl.pallas_call(
+        functools.partial(point_kernel, plane),
+        in_specs=[SMALL] * 3 + [LARGE] * len(sources),
+        out_specs=[LARGE] + [SMALL] * len(heads),
+        out_shape=[PLANE_OUT] + heads,
+        scratch_shapes=[PLANE, PLANE, pltpu.VMEM((WIDE, N), F32), WIDENED, sems(2, STEPS), pltpu.SemaphoreType.DMA],
+        **HALF,
+    )(weight, table["spread"], bias.reshape(1, C), *map(large, sources))
+
+
+def pointwise_back(plane, weights, array):
+    kept = [pltpu.VMEM((RESULT_HEAD, N, N), BF)] + [WIDENED] * (not plane)
+    return pl.pallas_call(
+        functools.partial(point_back_kernel, plane),
+        in_specs=[SMALL] * len(weights) + [LARGE],
         out_specs=[LARGE] + [SMALL] * len(kept),
         out_shape=[PLANE_OUT] + kept,
-        scratch_shapes=[wide] * (not back)
-        + [PLANE, PLANE, pltpu.VMEM((WIDE, N), F32), sems(2, STEPS), pltpu.SemaphoreType.DMA],
-        compiler_params=params(40),
-        cost_estimate=cost(C * N * N * 1024, ALL_BYTES),
-        name="pointwise",
-    )(*operands, *map(large, sources))
+        scratch_shapes=[PLANE, PLANE, sems(2, STEPS)],
+        **HALF,
+    )(*weights, large(array))
 
 
 def mix(received, weight, table):
@@ -514,11 +533,7 @@
 
 
 def over_samples(both):
-    def swap(array, k):
-        return lax.ppermute(array, "dp", [(i, i ^ k) for i in range(4)])
-
-    far = swap(both, 2)
-    return [both, far, swap(both, 1), swap(far, 1)]
+    return [both] + [lax.ppermute(both, "dp", [(i, i ^ k) for i in range(4)]) for k in (2, 3, 1)]
 
 
 def per_device(field, cotangent, mode_weight, point_weight, point_bias):
@@ -529,19 +544,22 @@
 
     modes, sample = lax.optimization_barrier((to_modes(sample, table), sample))
     received = exchange(modes)
-    point0, *heads = pointwise(0, False, point_weight, point_bias, sample, table, cot)
+    point0, *heads = pointwise(0, point_weight, point_bias, sample, table, cot)
     received, point0 = lax.optimization_barrier((received, point0))
     spatial, spectrum = mix(received, weight, table)
     later, spatial = lax.optimization_barrier((sample, spatial))
     received = exchange(spatial)
-    (point1,) = pointwise(1, False, point_weight, point_bias, later, table)
+    (point1,) = pointwise(1, point_weight, point_bias, later, table)
     slope, grad_modes = slopes(received, heads, (point0, point1), cot, table)
     received = exchange(grad_modes)
-    point_back0, head, wide = pointwise(0, True, point_weight, None, slope, table)
+    point_back0, head0, wide = pointwise_back(0, (point_weight, table["spread"]), slope)
     received, point_back0 = lax.optimization_barrier((received, point_back0))
     back, both = mix_back(received, weight, spectrum, table)
+    later, back = lax.optimization_barrier((slope, back))
+    back = exchange(back)
+    point_back1, head1 = pointwise_back(1, (wide,), later)
     field_grad, mode_grad = result(
-        exchange(back), wide, over_samples(both), head, point_back0, slope, table
+        back, over_samples(both), (head0, head1), (point_back0, point_back1), table
     )
     return field_grad.reshape(1, XL, C, N, N), mode_grad
 

time: 88.7 us -> 87.3 us (0.984)
  waiting for transfers between devices: 29.8 us -> 22.7 us
  starting transfers between devices: 27.9 us -> 31 us
  Pallas kernels: 29.7 us -> 32.2 us
    ppermute x3, waiting for transfers between devices: 5.86 us -> 0.01 us  [over_samples(): lax.ppermute(both, 'dp', [(i, i ^ k) for i in range(4)])]
    pallas_call x3 -> x4, Pallas kernels: 12.4 us -> 16.3 us  [the longest x2 8.57 us: pointwise(): pl.pallas_call(functools.partial(point_kernel, plane), in_specs=[SMALL] *...]
    ppermute x3, starting transfers between devices: 0.68 us -> 3.74 us  [over_samples(): lax.ppermute(both, 'dp', [(i, i ^ k) for i in range(4)])]
    pallas_call x1, Pallas kernels: 4.91 us -> 3.46 us  [result(): pl.pallas_call(result_kernel, in_specs=[SMALL] * 9 + [LARGE] * 2, out_spe...]
    all_to_all x4, waiting for transfers between devices: 23.9 us -> 22.7 us  [exchange(): lax.all_to_all(cut, 'space', split_axis=0, concat_axis=0, tiled=True)]
  transfers between devices with their start and end apart: 7 -> 7, of which waited for: 6 -> 4; matrix products, arithmetic and copies ran while one was open for 0% -> 0% of each run, Pallas kernels for 14% -> 19%
where the time goes in v4:
time: 87.3 us; the launch traced here: 86.9 us
  Pallas kernels  32.2 us (37%)
  starting transfers between devices  31 us (36%)
  waiting for transfers between devices  22.7 us (26%)
  between operations  1.01 us (1%)
    all_to_all x4, starting transfers between devices, exchange(): lax.all_to_all(cut, 'space', split_axis=0, concat_axis=0, tiled=True)  27.2 us
    all_to_all x4, waiting for transfers between devices, exchange(): lax.all_to_all(cut, 'space', split_axis=0, concat_axis=0, tiled=True)  22.7 us
    pallas_call x2, Pallas kernels, pointwise(): pl.pallas_call(functools.partial(point_kernel, plane), in_specs=[SMALL] *...  8.57 us
    pallas_call x2, Pallas kernels, pointwise_back(): pl.pallas_call(functools.partial(point_back_kernel, plane), in_specs=[SMA...  7.76 us
    pallas_call x1, Pallas kernels, slopes(): pl.pallas_call(slope_kernel, in_specs=[SMALL] * 6 + [LARGE] * 3, out_spec...  5.67 us
    pallas_call x1, Pallas kernels, to_modes(): pl.pallas_call(to_modes_kernel, in_specs=[LARGE] * 3, out_specs=LARGE, ou...  3.84 us
    ppermute x3, starting transfers between devices, over_samples(): lax.ppermute(both, 'dp', [(i, i ^ k) for i in range(4)])  3.74 us
    pallas_call x1, Pallas kernels, result(): pl.pallas_call(result_kernel, in_specs=[SMALL] * 9 + [LARGE] * 2, out_spe...  3.46 us
  transfers between devices with their start and end apart: 7, of which 4 were waited for; matrix products, arithmetic and copies ran while one was open for 0% of the time, Pallas kernels for 19%

profile of v4, /device:TPU:16, one launch (start us, length us, event | category | flops | bytes accessed | tf_op | source)
XLA Modules:
  0.0 86.9 jit_solution(11873860304228540350)
XLA Ops:
  0.6 0.0 copy-start.1
  0.7 3.8 %to_modes.1 = bf16[256,128]{1,0:T(8,128)(2,1)} custom-call(bf16[128,128,128]{2,1,0:T(8,128)(2,1)} %bitcast.21, bf16[64,256]{1,0:T(8,128)(2,1)} %constant.14.clone.forward_y_ref, bf16[16,128]{1,0:T(8,128)(2,1)} %constant.18.clone.forward_z_ref.table_z_ref), custom_call_target="tpu_custom_call" | custom-call | flops 268435456 | bytes 4194304 | tf_op jit(solution)/shard_map/to_modes/pallas_call | solution.py:427
  4.5 12.7 %all-to-all-start = ((bf16[64,4,128]{2,1,0:T(4,128)(2,1)}), bf16[64,4,128]{2,1,0:T(4,128)(2,1)S(1)}, u32[]{:S(2)}, u32[]{:S(2)}) async-start(bf16[64,4,128]{2,1,0:T(4,128)(2,1)} %bitcast.26), calls=%async_computation | async-start | bytes 131072 | tf_op jit(solution)/shard_map/all_to_all | solution.py:532
  17.2 0.0 copy-start
  17.2 0.0 copy-start.2
  17.2 0.0 copy-start.3
  17.3 4.4 %pointwise.4 = (bf16[64,128,128]{2,1,0:T(8,128)(2,1)}, bf16[16,128,128]{2,1,0:T(8,128)(2,1)S(1)}, bf16[16,128,128]{2,1,0:T(8,128)(2,1)S(1)}) custom-call(bf16[64,64]{1,0:T(8,128)(2,1)S(1)} %copy-done.4, bf16[512,64]{1,0:T(8,128)(2,1)S(1)} %copy-done.1, f32[1,64]{1,0:T(1,128)S(1)} %bitcast.19, bf16[128,128,128]{2,1,0:T(8,128)(2,1)} %bitcast.24, ...), custom_call_target="tpu_custom_call" | custom-call | flops 1073741824 | bytes 4194304 | tf_op jit(solution)/shard_map/pointwise/pallas_call | solution.py:484
  21.6 0.0 copy-start.5
  21.7 0.0 copy-start.6
  21.7 0.0 copy-start.7
  21.7 6.3 %all-to-all-done = bf16[64,4,128]{2,1,0:T(4,128)(2,1)S(1)} async-done(((bf16[64,4,128]{2,1,0:T(4,128)(2,1)}), bf16[64,4,128]{2,1,0:T(4,128)(2,1)S(1)}, u32[]{:S(2)}, u32[]{:S(2)}) %all-to-all-start) | async-done | bytes 65568 | tf_op jit(solution)/shard_map/all_to_all | solution.py:532
  28.0 0.0 copy-done.2
  28.0 1.4 %mix.1 = (bf16[256,128]{1,0:T(8,128)(2,1)}, bf16[64,128]{1,0:T(8,128)(2,1)S(1)}) custom-call(bf16[256,128]{1,0:T(8,128)(2,1)S(1)} %bitcast.18, bf16[2,128,256]{2,1,0:T(8,128)(2,1)S(1)} %copy-done.3, bf16[2,256,128]{2,1,0:T(8,128)(2,1)S(1)} %copy-done.2, bf16[4,1024,64]{2,1,0:T(8,128)(2,1)S(1)} %bitcast.13), custom_call_target="tpu_custom_call" | custom-call | flops 134217728 | bytes 2097152 | tf_op jit(solution)/shard_map/mix/pallas_call | solution.py:507
  29.4 5.1 %all-to-all-start.1 = ((bf16[64,4,128]{2,1,0:T(4,128)(2,1)}), bf16[64,4,128]{2,1,0:T(4,128)(2,1)S(1)}, u32[]{:S(2)}, u32[]{:S(2)}) async-start(bf16[64,4,128]{2,1,0:T(4,128)(2,1)} %bitcast.6), calls=%async_computation.1 | async-start | bytes 131072 | tf_op jit(solution)/shard_map/all_to_all | solution.py:532
  34.4 4.2 %pointwise.5.point1_ref = bf16[64,128,128]{2,1,0:T(8,128)(2,1)} custom-call(bf16[64,64]{1,0:T(8,128)(2,1)S(1)} %copy-done.4, bf16[512,64]{1,0:T(8,128)(2,1)S(1)} %copy-done.1, f32[1,64]{1,0:T(1,128)S(1)} %bitcast.20, bf16[128,128,128]{2,1,0:T(8,128)(2,1)} %bitcast.23), custom_call_target="tpu_custom_call" | custom-call | flops 1073741824 | bytes 4194304 | tf_op jit(solution)/shard_map/pointwise/pallas_call | solution.py:484
  38.6 6.6 %all-to-all-done.1 = bf16[64,4,128]{2,1,0:T(4,128)(2,1)S(1)} async-done(((bf16[64,4,128]{2,1,0:T(4,128)(2,1)}), bf16[64,4,128]{2,1,0:T(4,128)(2,1)S(1)}, u32[]{:S(2)}, u32[]{:S(2)}) %all-to-all-start.1) | async-done | bytes 65568 | tf_op jit(solution)/shard_map/all_to_all | solution.py:532
  45.2 0.0 copy-done.6
  45.2 5.7 %slopes.1 = (bf16[128,128,128]{2,1,0:T(8,128)(2,1)}, bf16[256,128]{1,0:T(8,128)(2,1)}) custom-call(bf16[256,128]{1,0:T(8,128)(2,1)S(1)} %bitcast.16, bf16[16,128]{1,0:T(8,128)(2,1)S(1)} %copy-done.6, bf16[128,32]{1,0:T(8,128)(2,1)S(1)} %copy-done.5, bf16[64,256]{1,0:T(8,128)(2,1)S(1)} %copy-done.7, ...), custom_call_target="tpu_custom_call" | custom-call | flops 536870912 | bytes 12582912 | tf_op jit(solution)/shard_map/slopes/pallas_call | solution.py:443
  50.9 4.9 %all-to-all-start.2 = ((bf16[64,4,128]{2,1,0:T(4,128)(2,1)}), bf16[64,4,128]{2,1,0:T(4,128)(2,1)S(1)}, u32[]{:S(2)}, u32[]{:S(2)}) async-start(bf16[64,4,128]{2,1,0:T(4,128)(2,1)} %bitcast.27), calls=%async_computation.2 | async-start | bytes 131072 | tf_op jit(solution)/shard_map/all_to_all | solution.py:532
  55.8 3.9 %pointwise.6 = (bf16[64,128,128]{2,1,0:T(8,128)(2,1)}, bf16[32,128,128]{2,1,0:T(8,128)(2,1)S(1)}, bf16[512,512]{1,0:T(8,128)(2,1)S(1)}) custom-call(bf16[64,64]{1,0:T(8,128)(2,1)S(1)} %copy-done.4, bf16[512,64]{1,0:T(8,128)(2,1)S(1)} %copy-done.1, bf16[128,128,128]{2,1,0:T(8,128)(2,1)} %get-tuple-element.48.refs_2_.refs_1_), custom_call_target="tpu_custom_call" | custom-call | flops 1073741824 | bytes 4194304 | tf_op jit(solution)/shard_map/pointwise/pallas_call | solution.py:496
  59.7 6.7 %all-to-all-done.2 = bf16[64,4,128]{2,1,0:T(4,128)(2,1)S(1)} async-done(((bf16[64,4,128]{2,1,0:T(4,128)(2,1)}), bf16[64,4,128]{2,1,0:T(4,128)(2,1)S(1)}, u32[]{:S(2)}, u32[]{:S(2)}) %all-to-all-start.2) | async-done | bytes 65568 | tf_op jit(solution)/shard_map/all_to_all | solution.py:532
  66.4 1.5 %mix_back.1 = (bf16[256,128]{1,0:T(8,128)(2,1)}, bf16[64,128]{1,0:T(8,128)(2,1)S(1)}) custom-call(bf16[256,128]{1,0:T(8,128)(2,1)S(1)} %bitcast.17, bf16[2,128,256]{2,1,0:T(8,128)(2,1)S(1)} %copy-done.3, bf16[2,256,128]{2,1,0:T(8,128)(2,1)S(1)} %copy-done.2, bf16[4,1024,64]{2,1,0:T(8,128)(2,1)S(1)} %bitcast.14, ...), custom_call_target="tpu_custom_call" | custom-call | flops 134217728 | bytes 2097152 | tf_op jit(solution)/shard_map/mix_back/pallas_call | solution.py:519
  67.9 4.6 %all-to-all-start.3 = ((bf16[64,4,128]{2,1,0:T(4,128)(2,1)}), bf16[64,4,128]{2,1,0:T(4,128)(2,1)S(1)}, u32[]{:S(2)}, u32[]{:S(2)}) async-start(bf16[64,4,128]{2,1,0:T(4,128)(2,1)} %bitcast.10), calls=%async_computation.3 | async-start | bytes 131072 | tf_op jit(solution)/shard_map/all_to_all | solution.py:532
  72.6 0.1 collective-permute-start.2
  72.7 0.7 collective-permute-start.1
  73.4 2.9 %collective-permute-start = (bf16[64,128]{1,0:T(8,128)(2,1)S(1)}, bf16[64,128]{1,0:T(8,128)(2,1)S(1)}, u32[]{:S(2)}, u32[]{:S(2)}) collective-permute-start(bf16[64,128]{1,0:T(8,128)(2,1)S(1)} %get-tuple-element.45.both0_ref), channel_id=1, source_target_pairs={{0,128},{64,192},{128,0},{192,64},{1,129},{65,193},{129,1},{193,65... | collective-permute-start | bytes 49160 | tf_op jit(solution)/shard_map/ppermute | solution.py:536
  76.3 3.9 %pointwise.7 = (bf16[64,128,128]{2,1,0:T(8,128)(2,1)}, bf16[32,128,128]{2,1,0:T(8,128)(2,1)S(1)}) custom-call(bf16[512,512]{1,0:T(8,128)(2,1)S(1)} %get-tuple-element.47.refs_0_, bf16[128,128,128]{2,1,0:T(8,128)(2,1)} %get-tuple-element.48.refs_2_.refs_1_), custom_call_target="tpu_custom_call" | custom-call | flops 1073741824 | bytes 4194304 | tf_op jit(solution)/shard_map/pointwise/pallas_call | solution.py:496
  80.2 0.0 collective-permute-done.2.both3_ref
  80.2 0.0 collective-permute-done.1.both2_ref
  80.2 0.0 collective-permute-done.both1_ref
  80.2 3.1 %all-to-all-done.3 = bf16[64,4,128]{2,1,0:T(4,128)(2,1)S(1)} async-done(((bf16[64,4,128]{2,1,0:T(4,128)(2,1)}), bf16[64,4,128]{2,1,0:T(4,128)(2,1)S(1)}, u32[]{:S(2)}, u32[]{:S(2)}) %all-to-all-start.3) | async-done | bytes 65568 | tf_op jit(solution)/shard_map/all_to_all | solution.py:532
  83.3 3.5 %result.1 = (bf16[128,128,128]{2,1,0:T(8,128)(2,1)}, f32[4,4,64,64]{3,2,1,0:T(8,128)}) custom-call(bf16[256,128]{1,0:T(8,128)(2,1)S(1)} %bitcast.15, bf16[16,128]{1,0:T(8,128)(2,1)S(1)} %copy-done.6, bf16[128,32]{1,0:T(8,128)(2,1)S(1)} %copy-done.5, bf16[64,128]{1,0:T(8,128)(2,1)S(1)} %get-tuple-element.45.both0_ref, ...), custom_call_target="tpu_custom_call" | custom-call | flops 268435456 | bytes 8388608 | tf_op jit(solution)/shard_map/result/pallas_call | solution.py:460
  (9 shorter events, 0.0 us)
Async XLA Ops:
  0.6 16.6 %copy-start.1 = (bf16[512,64]{1,0:T(8,128)(2,1)S(1)}, bf16[512,64]{1,0:T(8,128)(2,1)}, u32[]{:S(2)}) copy-start(bf16[512,64]{1,0:T(8,128)(2,1)} %constant.16.clone.spread_ref.refs_1_) | copy-start | bytes 196612
  0.6 16.6 %copy-start.4 = (bf16[64,64]{1,0:T(8,128)(2,1)S(1)}, bf16[64,64]{1,0:T(8,128)(2,1)}, u32[]{:S(2)}) copy-start(bf16[64,64]{1,0:T(8,128)(2,1)} %refs_0_.1) | copy-start | bytes 24580
  0.7 16.6 %copy-start.8 = (f32[64]{0:T(128)S(1)}, f32[64]{0:T(128)}, u32[]{:S(2)}) copy-start(f32[64]{0:T(128)} %param.16) | copy-start | bytes 772
  4.5 23.4 %all-to-all-start = ((bf16[64,4,128]{2,1,0:T(4,128)(2,1)}), bf16[64,4,128]{2,1,0:T(4,128)(2,1)S(1)}, u32[]{:S(2)}, u32[]{:S(2)}) async-start(bf16[64,4,128]{2,1,0:T(4,128)(2,1)} %bitcast.26), calls=%async_computation | async-start | bytes 131072 | tf_op jit(solution)/shard_map/all_to_all | solution.py:532
  17.2 10.7 %copy-start = (bf16[4,16,64,64]{3,2,1,0:T(8,128)(2,1)S(1)}, bf16[4,16,64,64]{3,2,1,0:T(8,128)(2,1)}, u32[]{:S(2)}) copy-start(bf16[4,16,64,64]{3,2,1,0:T(8,128)(2,1)} %param.14) | copy-start | bytes 1572868
  17.2 10.7 %copy-start.2 = (bf16[2,256,128]{2,1,0:T(8,128)(2,1)S(1)}, bf16[2,256,128]{2,1,0:T(8,128)(2,1)}, u32[]{:S(2)}) copy-start(bf16[2,256,128]{2,1,0:T(8,128)(2,1)} %constant.20.clone.back_x_ref) | copy-start | bytes 393220
  17.2 10.7 %copy-start.3 = (bf16[2,128,256]{2,1,0:T(8,128)(2,1)S(1)}, bf16[2,128,256]{2,1,0:T(8,128)(2,1)}, u32[]{:S(2)}) copy-start(bf16[2,128,256]{2,1,0:T(8,128)(2,1)} %constant.19.clone.along_x_ref) | copy-start | bytes 393220
  21.6 23.6 %copy-start.5 = (bf16[128,32]{1,0:T(8,128)(2,1)S(1)}, bf16[128,32]{1,0:T(8,128)(2,1)}, u32[]{:S(2)}) copy-start(bf16[128,32]{1,0:T(8,128)(2,1)} %constant.17.clone.back_y_ref) | copy-start | bytes 24580
  21.7 23.5 %copy-start.6 = (bf16[16,128]{1,0:T(8,128)(2,1)S(1)}, bf16[16,128]{1,0:T(8,128)(2,1)}, u32[]{:S(2)}) copy-start(bf16[16,128]{1,0:T(8,128)(2,1)} %constant.18.clone.forward_z_ref.table_z_ref) | copy-start | bytes 12292
  21.7 23.5 %copy-start.7 = (bf16[64,256]{1,0:T(8,128)(2,1)S(1)}, bf16[64,256]{1,0:T(8,128)(2,1)}, u32[]{:S(2)}) copy-start(bf16[64,256]{1,0:T(8,128)(2,1)} %constant.15.clone.forward_y_ref) | copy-start | bytes 98308
  29.4 15.8 %all-to-all-start.1 = ((bf16[64,4,128]{2,1,0:T(4,128)(2,1)}), bf16[64,4,128]{2,1,0:T(4,128)(2,1)S(1)}, u32[]{:S(2)}, u32[]{:S(2)}) async-start(bf16[64,4,128]{2,1,0:T(4,128)(2,1)} %bitcast.6), calls=%async_computation.1 | async-start | bytes 131072 | tf_op jit(solution)/shard_map/all_to_all | solution.py:532
  50.9 15.5 %all-to-all-start.2 = ((bf16[64,4,128]{2,1,0:T(4,128)(2,1)}), bf16[64,4,128]{2,1,0:T(4,128)(2,1)S(1)}, u32[]{:S(2)}, u32[]{:S(2)}) async-start(bf16[64,4,128]{2,1,0:T(4,128)(2,1)} %bitcast.27), calls=%async_computation.2 | async-start | bytes 131072 | tf_op jit(solution)/shard_map/all_to_all | solution.py:532
  67.9 15.4 %all-to-all-start.3 = ((bf16[64,4,128]{2,1,0:T(4,128)(2,1)}), bf16[64,4,128]{2,1,0:T(4,128)(2,1)S(1)}, u32[]{:S(2)}, u32[]{:S(2)}) async-start(bf16[64,4,128]{2,1,0:T(4,128)(2,1)} %bitcast.10), calls=%async_computation.3 | async-start | bytes 131072 | tf_op jit(solution)/shard_map/all_to_all | solution.py:532
  72.6 7.6 %collective-permute-start.2 = (bf16[64,128]{1,0:T(8,128)(2,1)S(1)}, bf16[64,128]{1,0:T(8,128)(2,1)S(1)}, u32[]{:S(2)}, u32[]{:S(2)}) collective-permute-start(bf16[64,128]{1,0:T(8,128)(2,1)S(1)} %get-tuple-element.45.both0_ref), channel_id=1, source_target_pairs={{0,64},{64,0},{128,192},{192,128},{1,65},{65,1},{129,193},{193,129... | collective-permute-start | bytes 49160 | tf_op jit(solution)/shard_map/ppermute | solution.py:536
  72.7 7.5 %collective-permute-start.1 = (bf16[64,128]{1,0:T(8,128)(2,1)S(1)}, bf16[64,128]{1,0:T(8,128)(2,1)S(1)}, u32[]{:S(2)}, u32[]{:S(2)}) collective-permute-start(bf16[64,128]{1,0:T(8,128)(2,1)S(1)} %get-tuple-element.45.both0_ref), channel_id=1, source_target_pairs={{0,192},{64,128},{128,64},{192,0},{1,193},{65,129},{129,65},{193,1... | collective-permute-start | bytes 49160 | tf_op jit(solution)/shard_map/ppermute | solution.py:536
  73.4 6.8 %collective-permute-start = (bf16[64,128]{1,0:T(8,128)(2,1)S(1)}, bf16[64,128]{1,0:T(8,128)(2,1)S(1)}, u32[]{:S(2)}, u32[]{:S(2)}) collective-permute-start(bf16[64,128]{1,0:T(8,128)(2,1)S(1)} %get-tuple-element.45.both0_ref), channel_id=1, source_target_pairs={{0,128},{64,192},{128,0},{192,64},{1,129},{65,193},{129,1},{193,65... | collective-permute-start | bytes 49160 | tf_op jit(solution)/shard_map/ppermute | solution.py:536

commit v5 on v4

--- a/solution.py
+++ b/solution.py
@@ -21,7 +21,7 @@
 OWN = 4
 GROUPS = 64
 SLOPE_HEAD = 16
-RESULT_HEAD = 32
+RESULT_HEADS = (32, 48)
 
 
 def basis(length, count):
@@ -125,7 +125,7 @@
 
 SLOPE_CUTS = (0, SLOPE_HEAD, 40, C, 96, 128)
 SLOPE_OUT_CUTS = (0, 32, 64, 88, 104, 116, 128)
-RESULT_CUTS = (0, RESULT_HEAD, C, C + RESULT_HEAD, 112, 128)
+RESULT_CUTS = (0, RESULT_HEADS[0], C, 96, C + RESULT_HEADS[1], 128)
 AHEAD = 2
 BEHIND = 2
 
@@ -194,9 +194,8 @@
     back_ref, table_z_ref, back_y_ref, both0_ref, both1_ref, both2_ref, both3_ref, head0_ref, head1_ref,
     point0_ref, point1_ref, out_ref, mode_grad_ref, spread, point, held, grads, total, sems, sem,
 ):
-    head = head0_ref.shape[0]
-    point_copies = pieces(point0_ref, point, sems.at[0], (head, C))
-    point_copies |= pieces(point1_ref, point, sems.at[1], (C + head, XC), C)
+    point_copies = pieces(point0_ref, point, sems.at[0], (RESULT_HEADS[0], C))
+    point_copies |= pieces(point1_ref, point, sems.at[1], (C + RESULT_HEADS[1], XC), C)
     out_copies = pieces(held, out_ref, sems.at[2], RESULT_CUTS)
     for copy in point_copies.values():
         copy.start()
@@ -212,7 +211,8 @@
             both = spectral(g)
             for h in range(2):
                 plane, channel = divmod(g + h, C)
-                other = (head0_ref, head1_ref)[plane][channel] if channel < head else point[g + h]
+                head = (head0_ref, head1_ref)[plane]
+                other = head[channel] if channel < RESULT_HEADS[plane] else point[g + h]
                 held[g + h] = (both[:, N * h : N * (h + 1)] + other.astype(F32)).astype(BF)
         out_copies[low].start()
     for copy in (*out_copies.values(), mode_copy):
@@ -297,9 +297,13 @@
         copy(k).start()
     if not plane:
         head_copy.start()
-    bias[...] = lax.dot_general(
-        spread_ref[...].astype(F32), jnp.broadcast_to(bias_ref[...], (N, C)), (((1,), (1,)), ((), ())),
-        precision=lax.Precision.HIGHEST, preferred_element_type=F32,
+    high = bias_ref[...].astype(BF)
+    low = (bias_ref[...] - high.astype(F32)).astype(BF)
+    bias[...] = sum(
+        lax.dot_general(
+            spread_ref[...], jnp.broadcast_to(part, (N, C)), (((1,), (1,)), ((), ())), preferred_element_type=F32
+        )
+        for part in (high, low)
     )
     widen(weight_ref, spread_ref, wide, True, 1.0)
     for k in range(STEPS):
@@ -329,7 +333,7 @@
         copy(k).wait()
         point_rows(array, wide, None, out, k)
         out_copy(k).start()
-    head_ref[...] = out[:RESULT_HEAD]
+    head_ref[...] = out[: RESULT_HEADS[plane]]
     for k in range(STEPS):
         out_copy(k).wait()
 
@@ -492,7 +496,7 @@
 
 
 def pointwise_back(plane, weights, array):
-    kept = [pltpu.VMEM((RESULT_HEAD, N, N), BF)] + [WIDENED] * (not plane)
+    kept = [pltpu.VMEM((RESULT_HEADS[plane], N, N), BF)] + [WIDENED] * (not plane)
     return pl.pallas_call(
         functools.partial(point_back_kernel, plane),
         in_specs=[SMALL] * len(weights) + [LARGE],

time: 87.3 us -> 87 us (level)
  transfers between devices with their start and end apart: 7 -> 7, of which waited for: 4 -> 4; matrix products, arithmetic and copies ran while one was open for 0% -> 0% of each run, Pallas kernels for 19% -> 18%
where the time goes in v5:
time: 87 us; the launch traced here: 86.6 us
  Pallas kernels  31.6 us (36%)
  starting transfers between devices  30.7 us (35%)
  waiting for transfers between devices  23.3 us (27%)
  between operations  1.01 us (1%)
    all_to_all x4, starting transfers between devices, exchange(): lax.all_to_all(cut, 'space', split_axis=0, concat_axis=0, tiled=True)  26.9 us
    all_to_all x4, waiting for transfers between devices, exchange(): lax.all_to_all(cut, 'space', split_axis=0, concat_axis=0, tiled=True)  23.3 us
    pallas_call x2, Pallas kernels, pointwise(): pl.pallas_call(functools.partial(point_kernel, plane), in_specs=[SMALL] *...  7.99 us
    pallas_call x2, Pallas kernels, pointwise_back(): pl.pallas_call(functools.partial(point_back_kernel, plane), in_specs=[SMA...  7.69 us
    pallas_call x1, Pallas kernels, slopes(): pl.pallas_call(slope_kernel, in_specs=[SMALL] * 6 + [LARGE] * 3, out_spec...  5.67 us
    pallas_call x1, Pallas kernels, to_modes(): pl.pallas_call(to_modes_kernel, in_specs=[LARGE] * 3, out_specs=LARGE, ou...  3.84 us
    ppermute x3, starting transfers between devices, over_samples(): lax.ppermute(both, 'dp', [(i, i ^ k) for i in range(4)])  3.74 us
    pallas_call x1, Pallas kernels, result(): pl.pallas_call(result_kernel, in_specs=[SMALL] * 9 + [LARGE] * 2, out_spe...  3.46 us
  transfers between devices with their start and end apart: 7, of which 4 were waited for; matrix products, arithmetic and copies ran while one was open for 0% of the time, Pallas kernels for 18%

profile of v5, /device:TPU:16, one launch (start us, length us, event | category | flops | bytes accessed | tf_op | source)
XLA Modules:
  0.0 86.6 jit_solution(14452792520808721654)
XLA Ops:
  0.6 0.0 copy-start.1
  0.7 3.8 %to_modes.1 = bf16[256,128]{1,0:T(8,128)(2,1)} custom-call(bf16[128,128,128]{2,1,0:T(8,128)(2,1)} %bitcast.21, bf16[64,256]{1,0:T(8,128)(2,1)} %constant.14.clone.forward_y_ref, bf16[16,128]{1,0:T(8,128)(2,1)} %constant.18.clone.forward_z_ref.table_z_ref), custom_call_target="tpu_custom_call" | custom-call | flops 268435456 | bytes 4194304 | tf_op jit(solution)/shard_map/to_modes/pallas_call | solution.py:431
  4.5 12.7 %all-to-all-start = ((bf16[64,4,128]{2,1,0:T(4,128)(2,1)}), bf16[64,4,128]{2,1,0:T(4,128)(2,1)S(1)}, u32[]{:S(2)}, u32[]{:S(2)}) async-start(bf16[64,4,128]{2,1,0:T(4,128)(2,1)} %bitcast.26), calls=%async_computation | async-start | bytes 131072 | tf_op jit(solution)/shard_map/all_to_all | solution.py:536
  17.2 0.0 copy-done.1
  17.2 0.0 copy-done.4
  17.2 0.0 copy-start
  17.2 0.0 copy-start.2
  17.2 0.0 copy-start.3
  17.3 4.2 %pointwise.4 = (bf16[64,128,128]{2,1,0:T(8,128)(2,1)}, bf16[16,128,128]{2,1,0:T(8,128)(2,1)S(1)}, bf16[16,128,128]{2,1,0:T(8,128)(2,1)S(1)}) custom-call(bf16[64,64]{1,0:T(8,128)(2,1)S(1)} %copy-done.4, bf16[512,64]{1,0:T(8,128)(2,1)S(1)} %copy-done.1, f32[1,64]{1,0:T(1,128)S(1)} %bitcast.19, bf16[128,128,128]{2,1,0:T(8,128)(2,1)} %bitcast.24, ...), custom_call_target="tpu_custom_call" | custom-call | flops 1073741824 | bytes 4194304 | tf_op jit(solution)/shard_map/pointwise/pallas_call | solution.py:488
  21.5 6.5 %all-to-all-done = bf16[64,4,128]{2,1,0:T(4,128)(2,1)S(1)} async-done(((bf16[64,4,128]{2,1,0:T(4,128)(2,1)}), bf16[64,4,128]{2,1,0:T(4,128)(2,1)S(1)}, u32[]{:S(2)}, u32[]{:S(2)}) %all-to-all-start) | async-done | bytes 65568 | tf_op jit(solution)/shard_map/all_to_all | solution.py:536
  28.0 1.4 %mix.1 = (bf16[256,128]{1,0:T(8,128)(2,1)}, bf16[64,128]{1,0:T(8,128)(2,1)S(1)}) custom-call(bf16[256,128]{1,0:T(8,128)(2,1)S(1)} %bitcast.18, bf16[2,128,256]{2,1,0:T(8,128)(2,1)S(1)} %copy-done.3, bf16[2,256,128]{2,1,0:T(8,128)(2,1)S(1)} %copy-done.2, bf16[4,1024,64]{2,1,0:T(8,128)(2,1)S(1)} %bitcast.13), custom_call_target="tpu_custom_call" | custom-call | flops 134217728 | bytes 2097152 | tf_op jit(solution)/shard_map/mix/pallas_call | solution.py:511
  29.4 4.8 %all-to-all-start.1 = ((bf16[64,4,128]{2,1,0:T(4,128)(2,1)}), bf16[64,4,128]{2,1,0:T(4,128)(2,1)S(1)}, u32[]{:S(2)}, u32[]{:S(2)}) async-start(bf16[64,4,128]{2,1,0:T(4,128)(2,1)} %bitcast.6), calls=%async_computation.1 | async-start | bytes 131072 | tf_op jit(solution)/shard_map/all_to_all | solution.py:536
  34.2 0.0 copy-start.5
  34.2 0.0 copy-start.6
  34.2 0.0 copy-start.7
  34.2 3.8 %pointwise.5.point1_ref = bf16[64,128,128]{2,1,0:T(8,128)(2,1)} custom-call(bf16[64,64]{1,0:T(8,128)(2,1)S(1)} %copy-done.4, bf16[512,64]{1,0:T(8,128)(2,1)S(1)} %copy-done.1, f32[1,64]{1,0:T(1,128)S(1)} %bitcast.20, bf16[128,128,128]{2,1,0:T(8,128)(2,1)} %bitcast.23), custom_call_target="tpu_custom_call" | custom-call | flops 1073741824 | bytes 4194304 | tf_op jit(solution)/shard_map/pointwise/pallas_call | solution.py:488
  38.0 7.0 %all-to-all-done.1 = bf16[64,4,128]{2,1,0:T(4,128)(2,1)S(1)} async-done(((bf16[64,4,128]{2,1,0:T(4,128)(2,1)}), bf16[64,4,128]{2,1,0:T(4,128)(2,1)S(1)}, u32[]{:S(2)}, u32[]{:S(2)}) %all-to-all-start.1) | async-done | bytes 65568 | tf_op jit(solution)/shard_map/all_to_all | solution.py:536
  45.0 5.7 %slopes.1 = (bf16[128,128,128]{2,1,0:T(8,128)(2,1)}, bf16[256,128]{1,0:T(8,128)(2,1)}) custom-call(bf16[256,128]{1,0:T(8,128)(2,1)S(1)} %bitcast.16, bf16[16,128]{1,0:T(8,128)(2,1)S(1)} %copy-done.6, bf16[128,32]{1,0:T(8,128)(2,1)S(1)} %copy-done.5, bf16[64,256]{1,0:T(8,128)(2,1)S(1)} %copy-done.7, ...), custom_call_target="tpu_custom_call" | custom-call | flops 536870912 | bytes 12582912 | tf_op jit(solution)/shard_map/slopes/pallas_call | solution.py:447
  50.7 4.8 %all-to-all-start.2 = ((bf16[64,4,128]{2,1,0:T(4,128)(2,1)}), bf16[64,4,128]{2,1,0:T(4,128)(2,1)S(1)}, u32[]{:S(2)}, u32[]{:S(2)}) async-start(bf16[64,4,128]{2,1,0:T(4,128)(2,1)} %bitcast.27), calls=%async_computation.2 | async-start | bytes 131072 | tf_op jit(solution)/shard_map/all_to_all | solution.py:536
  55.5 3.8 %pointwise.6 = (bf16[64,128,128]{2,1,0:T(8,128)(2,1)}, bf16[32,128,128]{2,1,0:T(8,128)(2,1)S(1)}, bf16[512,512]{1,0:T(8,128)(2,1)S(1)}) custom-call(bf16[64,64]{1,0:T(8,128)(2,1)S(1)} %copy-done.4, bf16[512,64]{1,0:T(8,128)(2,1)S(1)} %copy-done.1, bf16[128,128,128]{2,1,0:T(8,128)(2,1)} %get-tuple-element.48.refs_2_.refs_1_), custom_call_target="tpu_custom_call" | custom-call | flops 1073741824 | bytes 4194304 | tf_op jit(solution)/shard_map/pointwise/pallas_call | solution.py:500
  59.3 6.7 %all-to-all-done.2 = bf16[64,4,128]{2,1,0:T(4,128)(2,1)S(1)} async-done(((bf16[64,4,128]{2,1,0:T(4,128)(2,1)}), bf16[64,4,128]{2,1,0:T(4,128)(2,1)S(1)}, u32[]{:S(2)}, u32[]{:S(2)}) %all-to-all-start.2) | async-done | bytes 65568 | tf_op jit(solution)/shard_map/all_to_all | solution.py:536
  66.1 1.5 %mix_back.1 = (bf16[256,128]{1,0:T(8,128)(2,1)}, bf16[64,128]{1,0:T(8,128)(2,1)S(1)}) custom-call(bf16[256,128]{1,0:T(8,128)(2,1)S(1)} %bitcast.17, bf16[2,128,256]{2,1,0:T(8,128)(2,1)S(1)} %copy-done.3, bf16[2,256,128]{2,1,0:T(8,128)(2,1)S(1)} %copy-done.2, bf16[4,1024,64]{2,1,0:T(8,128)(2,1)S(1)} %bitcast.14, ...), custom_call_target="tpu_custom_call" | custom-call | flops 134217728 | bytes 2097152 | tf_op jit(solution)/shard_map/mix_back/pallas_call | solution.py:523
  67.6 4.6 %all-to-all-start.3 = ((bf16[64,4,128]{2,1,0:T(4,128)(2,1)}), bf16[64,4,128]{2,1,0:T(4,128)(2,1)S(1)}, u32[]{:S(2)}, u32[]{:S(2)}) async-start(bf16[64,4,128]{2,1,0:T(4,128)(2,1)} %bitcast.10), calls=%async_computation.3 | async-start | bytes 131072 | tf_op jit(solution)/shard_map/all_to_all | solution.py:536
  72.2 0.1 collective-permute-start.2
  72.3 0.7 collective-permute-start.1
  73.1 2.9 %collective-permute-start = (bf16[64,128]{1,0:T(8,128)(2,1)S(1)}, bf16[64,128]{1,0:T(8,128)(2,1)S(1)}, u32[]{:S(2)}, u32[]{:S(2)}) collective-permute-start(bf16[64,128]{1,0:T(8,128)(2,1)S(1)} %get-tuple-element.45.both0_ref), channel_id=1, source_target_pairs={{0,128},{64,192},{128,0},{192,64},{1,129},{65,193},{129,1},{193,65... | collective-permute-start | bytes 49160 | tf_op jit(solution)/shard_map/ppermute | solution.py:540
  76.0 3.9 %pointwise.7 = (bf16[64,128,128]{2,1,0:T(8,128)(2,1)}, bf16[48,128,128]{2,1,0:T(8,128)(2,1)S(1)}) custom-call(bf16[512,512]{1,0:T(8,128)(2,1)S(1)} %get-tuple-element.47.refs_0_, bf16[128,128,128]{2,1,0:T(8,128)(2,1)} %get-tuple-element.48.refs_2_.refs_1_), custom_call_target="tpu_custom_call" | custom-call | flops 1073741824 | bytes 4194304 | tf_op jit(solution)/shard_map/pointwise/pallas_call | solution.py:500
  79.8 0.0 collective-permute-done.2.both3_ref
  79.8 0.0 collective-permute-done.1.both2_ref
  79.8 0.0 collective-permute-done.both1_ref
  79.9 3.1 %all-to-all-done.3 = bf16[64,4,128]{2,1,0:T(4,128)(2,1)S(1)} async-done(((bf16[64,4,128]{2,1,0:T(4,128)(2,1)}), bf16[64,4,128]{2,1,0:T(4,128)(2,1)S(1)}, u32[]{:S(2)}, u32[]{:S(2)}) %all-to-all-start.3) | async-done | bytes 65568 | tf_op jit(solution)/shard_map/all_to_all | solution.py:536
  83.0 3.5 %result.1 = (bf16[128,128,128]{2,1,0:T(8,128)(2,1)}, f32[4,4,64,64]{3,2,1,0:T(8,128)}) custom-call(bf16[256,128]{1,0:T(8,128)(2,1)S(1)} %bitcast.15, bf16[16,128]{1,0:T(8,128)(2,1)S(1)} %copy-done.6, bf16[128,32]{1,0:T(8,128)(2,1)S(1)} %copy-done.5, bf16[64,128]{1,0:T(8,128)(2,1)S(1)} %get-tuple-element.45.both0_ref, ...), custom_call_target="tpu_custom_call" | custom-call | flops 268435456 | bytes 8388608 | tf_op jit(solution)/shard_map/result/pallas_call | solution.py:464
  (9 shorter events, 0.0 us)
Async XLA Ops:
  0.6 16.6 %copy-start.1 = (bf16[512,64]{1,0:T(8,128)(2,1)S(1)}, bf16[512,64]{1,0:T(8,128)(2,1)}, u32[]{:S(2)}) copy-start(bf16[512,64]{1,0:T(8,128)(2,1)} %constant.16.clone.spread_ref.refs_1_) | copy-start | bytes 196612
  0.6 16.6 %copy-start.4 = (bf16[64,64]{1,0:T(8,128)(2,1)S(1)}, bf16[64,64]{1,0:T(8,128)(2,1)}, u32[]{:S(2)}) copy-start(bf16[64,64]{1,0:T(8,128)(2,1)} %refs_0_.1) | copy-start | bytes 24580
  0.7 16.6 %copy-start.8 = (f32[64]{0:T(128)S(1)}, f32[64]{0:T(128)}, u32[]{:S(2)}) copy-start(f32[64]{0:T(128)} %param.16) | copy-start | bytes 772
  4.5 23.4 %all-to-all-start = ((bf16[64,4,128]{2,1,0:T(4,128)(2,1)}), bf16[64,4,128]{2,1,0:T(4,128)(2,1)S(1)}, u32[]{:S(2)}, u32[]{:S(2)}) async-start(bf16[64,4,128]{2,1,0:T(4,128)(2,1)} %bitcast.26), calls=%async_computation | async-start | bytes 131072 | tf_op jit(solution)/shard_map/all_to_all | solution.py:536
  17.2 10.7 %copy-start = (bf16[4,16,64,64]{3,2,1,0:T(8,128)(2,1)S(1)}, bf16[4,16,64,64]{3,2,1,0:T(8,128)(2,1)}, u32[]{:S(2)}) copy-start(bf16[4,16,64,64]{3,2,1,0:T(8,128)(2,1)} %param.14) | copy-start | bytes 1572868
  17.2 10.7 %copy-start.2 = (bf16[2,256,128]{2,1,0:T(8,128)(2,1)S(1)}, bf16[2,256,128]{2,1,0:T(8,128)(2,1)}, u32[]{:S(2)}) copy-start(bf16[2,256,128]{2,1,0:T(8,128)(2,1)} %constant.20.clone.back_x_ref) | copy-start | bytes 393220
  17.2 10.7 %copy-start.3 = (bf16[2,128,256]{2,1,0:T(8,128)(2,1)S(1)}, bf16[2,128,256]{2,1,0:T(8,128)(2,1)}, u32[]{:S(2)}) copy-start(bf16[2,128,256]{2,1,0:T(8,128)(2,1)} %constant.19.clone.along_x_ref) | copy-start | bytes 393220
  29.4 15.6 %all-to-all-start.1 = ((bf16[64,4,128]{2,1,0:T(4,128)(2,1)}), bf16[64,4,128]{2,1,0:T(4,128)(2,1)S(1)}, u32[]{:S(2)}, u32[]{:S(2)}) async-start(bf16[64,4,128]{2,1,0:T(4,128)(2,1)} %bitcast.6), calls=%async_computation.1 | async-start | bytes 131072 | tf_op jit(solution)/shard_map/all_to_all | solution.py:536
  34.2 10.8 %copy-start.5 = (bf16[128,32]{1,0:T(8,128)(2,1)S(1)}, bf16[128,32]{1,0:T(8,128)(2,1)}, u32[]{:S(2)}) copy-start(bf16[128,32]{1,0:T(8,128)(2,1)} %constant.17.clone.back_y_ref) | copy-start | bytes 24580
  34.2 10.8 %copy-start.6 = (bf16[16,128]{1,0:T(8,128)(2,1)S(1)}, bf16[16,128]{1,0:T(8,128)(2,1)}, u32[]{:S(2)}) copy-start(bf16[16,128]{1,0:T(8,128)(2,1)} %constant.18.clone.forward_z_ref.table_z_ref) | copy-start | bytes 12292
  34.2 10.8 %copy-start.7 = (bf16[64,256]{1,0:T(8,128)(2,1)S(1)}, bf16[64,256]{1,0:T(8,128)(2,1)}, u32[]{:S(2)}) copy-start(bf16[64,256]{1,0:T(8,128)(2,1)} %constant.15.clone.forward_y_ref) | copy-start | bytes 98308
  50.7 15.4 %all-to-all-start.2 = ((bf16[64,4,128]{2,1,0:T(4,128)(2,1)}), bf16[64,4,128]{2,1,0:T(4,128)(2,1)S(1)}, u32[]{:S(2)}, u32[]{:S(2)}) async-start(bf16[64,4,128]{2,1,0:T(4,128)(2,1)} %bitcast.27), calls=%async_computation.2 | async-start | bytes 131072 | tf_op jit(solution)/shard_map/all_to_all | solution.py:536
  67.6 15.4 %all-to-all-start.3 = ((bf16[64,4,128]{2,1,0:T(4,128)(2,1)}), bf16[64,4,128]{2,1,0:T(4,128)(2,1)S(1)}, u32[]{:S(2)}, u32[]{:S(2)}) async-start(bf16[64,4,128]{2,1,0:T(4,128)(2,1)} %bitcast.10), calls=%async_computation.3 | async-start | bytes 131072 | tf_op jit(solution)/shard_map/all_to_all | solution.py:536
  72.2 7.6 %collective-permute-start.2 = (bf16[64,128]{1,0:T(8,128)(2,1)S(1)}, bf16[64,128]{1,0:T(8,128)(2,1)S(1)}, u32[]{:S(2)}, u32[]{:S(2)}) collective-permute-start(bf16[64,128]{1,0:T(8,128)(2,1)S(1)} %get-tuple-element.45.both0_ref), channel_id=1, source_target_pairs={{0,64},{64,0},{128,192},{192,128},{1,65},{65,1},{129,193},{193,129... | collective-permute-start | bytes 49160 | tf_op jit(solution)/shard_map/ppermute | solution.py:540
  72.3 7.5 %collective-permute-start.1 = (bf16[64,128]{1,0:T(8,128)(2,1)S(1)}, bf16[64,128]{1,0:T(8,128)(2,1)S(1)}, u32[]{:S(2)}, u32[]{:S(2)}) collective-permute-start(bf16[64,128]{1,0:T(8,128)(2,1)S(1)} %get-tuple-element.45.both0_ref), channel_id=1, source_target_pairs={{0,192},{64,128},{128,64},{192,0},{1,193},{65,129},{129,65},{193,1... | collective-permute-start | bytes 49160 | tf_op jit(solution)/shard_map/ppermute | solution.py:540
  73.1 6.8 %collective-permute-start = (bf16[64,128]{1,0:T(8,128)(2,1)S(1)}, bf16[64,128]{1,0:T(8,128)(2,1)S(1)}, u32[]{:S(2)}, u32[]{:S(2)}) collective-permute-start(bf16[64,128]{1,0:T(8,128)(2,1)S(1)} %get-tuple-element.45.both0_ref), channel_id=1, source_target_pairs={{0,128},{64,192},{128,0},{192,64},{1,129},{65,193},{129,1},{193,65... | collective-permute-start | bytes 49160 | tf_op jit(solution)/shard_map/ppermute | solution.py:540

commit v6 on v5

--- a/solution.py
+++ b/solution.py
@@ -42,7 +42,7 @@
 def tables():
     base = basis(N, M)
     table_z = base.astype(BF)
-    forward_y = np.concatenate([np.kron(np.eye(2, dtype=np.float32), part.astype(np.float32).T) for part in split(base)])
+    forward_y = np.kron(np.eye(2, dtype=np.float32), base.T)
     back_y = np.concatenate(split(base), axis=1)
     by_plane = base.reshape(GROUPS, XL, M)
     along_x = np.einsum("sxm,pq->xpmsq", by_plane, np.eye(OWN, dtype=np.float32)).reshape(XL * OWN * M, GROUPS * OWN)
@@ -61,8 +61,7 @@
     block = jnp.concatenate(
         [jnp.concatenate(group[0:2], axis=0), jnp.concatenate(group[2:4], axis=0)], axis=1
     )
-    both = jnp.dot(forward_y, block, preferred_element_type=F32)
-    modes = both[: 2 * M] + both[2 * M :]
+    modes = jnp.dot(forward_y, block, preferred_element_type=F32)
     scratch[pl.ds(row, 2 * M), :] = modes[:, :N]
     scratch[pl.ds(row + 2 * M, 2 * M), :] = modes[:, N:]
 

time: 87 us -> 86.9 us (level)
  no operation moved by 1% of the time
where the time goes in v6:
time: 86.9 us; the launch traced here: 86.5 us
  Pallas kernels  31.5 us (36%)
  starting transfers between devices  30.7 us (35%)
  waiting for transfers between devices  23.3 us (27%)
  between operations  1.01 us (1%)
    all_to_all x4, starting transfers between devices, exchange(): lax.all_to_all(cut, 'space', split_axis=0, concat_axis=0, tiled=True)  26.9 us
    all_to_all x4, waiting for transfers between devices, exchange(): lax.all_to_all(cut, 'space', split_axis=0, concat_axis=0, tiled=True)  23.3 us
    pallas_call x2, Pallas kernels, pointwise(): pl.pallas_call(functools.partial(point_kernel, plane), in_specs=[SMALL] *...  7.98 us
    pallas_call x2, Pallas kernels, pointwise_back(): pl.pallas_call(functools.partial(point_back_kernel, plane), in_specs=[SMA...  7.69 us
    pallas_call x1, Pallas kernels, slopes(): pl.pallas_call(slope_kernel, in_specs=[SMALL] * 6 + [LARGE] * 3, out_spec...  5.65 us
    pallas_call x1, Pallas kernels, to_modes(): pl.pallas_call(to_modes_kernel, in_specs=[LARGE] * 3, out_specs=LARGE, ou...  3.81 us
    ppermute x3, starting transfers between devices, over_samples(): lax.ppermute(both, 'dp', [(i, i ^ k) for i in range(4)])  3.74 us
    pallas_call x1, Pallas kernels, result(): pl.pallas_call(result_kernel, in_specs=[SMALL] * 9 + [LARGE] * 2, out_spe...  3.46 us
  transfers between devices with their start and end apart: 7, of which 4 were waited for; matrix products, arithmetic and copies ran while one was open for 0% of the time, Pallas kernels for 18%

profile of v6, /device:TPU:16, one launch (start us, length us, event | category | flops | bytes accessed | tf_op | source)
XLA Modules:
  0.0 86.5 jit_solution(15217383215416485527)
XLA Ops:
  0.6 0.0 copy-start.1
  0.7 3.8 %to_modes.1 = bf16[256,128]{1,0:T(8,128)(2,1)} custom-call(bf16[128,128,128]{2,1,0:T(8,128)(2,1)} %bitcast.21, bf16[32,256]{1,0:T(8,128)(2,1)} %constant.14.clone.forward_y_ref, bf16[16,128]{1,0:T(8,128)(2,1)} %constant.18.clone.forward_z_ref.table_z_ref), custom_call_target="tpu_custom_call" | custom-call | flops 268435456 | bytes 4194304 | tf_op jit(solution)/shard_map/to_modes/pallas_call | solution.py:430
  4.5 12.7 %all-to-all-start = ((bf16[64,4,128]{2,1,0:T(4,128)(2,1)}), bf16[64,4,128]{2,1,0:T(4,128)(2,1)S(1)}, u32[]{:S(2)}, u32[]{:S(2)}) async-start(bf16[64,4,128]{2,1,0:T(4,128)(2,1)} %bitcast.26), calls=%async_computation | async-start | bytes 131072 | tf_op jit(solution)/shard_map/all_to_all | solution.py:535
  17.2 0.0 copy-done.1
  17.2 0.0 copy-done.4
  17.2 0.0 copy-start
  17.2 0.0 copy-start.2
  17.2 0.0 copy-start.3
  17.2 4.2 %pointwise.4 = (bf16[64,128,128]{2,1,0:T(8,128)(2,1)}, bf16[16,128,128]{2,1,0:T(8,128)(2,1)S(1)}, bf16[16,128,128]{2,1,0:T(8,128)(2,1)S(1)}) custom-call(bf16[64,64]{1,0:T(8,128)(2,1)S(1)} %copy-done.4, bf16[512,64]{1,0:T(8,128)(2,1)S(1)} %copy-done.1, f32[1,64]{1,0:T(1,128)S(1)} %bitcast.19, bf16[128,128,128]{2,1,0:T(8,128)(2,1)} %bitcast.24, ...), custom_call_target="tpu_custom_call" | custom-call | flops 1073741824 | bytes 4194304 | tf_op jit(solution)/shard_map/pointwise/pallas_call | solution.py:487
  21.4 6.5 %all-to-all-done = bf16[64,4,128]{2,1,0:T(4,128)(2,1)S(1)} async-done(((bf16[64,4,128]{2,1,0:T(4,128)(2,1)}), bf16[64,4,128]{2,1,0:T(4,128)(2,1)S(1)}, u32[]{:S(2)}, u32[]{:S(2)}) %all-to-all-start) | async-done | bytes 65568 | tf_op jit(solution)/shard_map/all_to_all | solution.py:535
  27.9 1.4 %mix.1 = (bf16[256,128]{1,0:T(8,128)(2,1)}, bf16[64,128]{1,0:T(8,128)(2,1)S(1)}) custom-call(bf16[256,128]{1,0:T(8,128)(2,1)S(1)} %bitcast.18, bf16[2,128,256]{2,1,0:T(8,128)(2,1)S(1)} %copy-done.3, bf16[2,256,128]{2,1,0:T(8,128)(2,1)S(1)} %copy-done.2, bf16[4,1024,64]{2,1,0:T(8,128)(2,1)S(1)} %bitcast.13), custom_call_target="tpu_custom_call" | custom-call | flops 134217728 | bytes 2097152 | tf_op jit(solution)/shard_map/mix/pallas_call | solution.py:510
  29.3 4.8 %all-to-all-start.1 = ((bf16[64,4,128]{2,1,0:T(4,128)(2,1)}), bf16[64,4,128]{2,1,0:T(4,128)(2,1)S(1)}, u32[]{:S(2)}, u32[]{:S(2)}) async-start(bf16[64,4,128]{2,1,0:T(4,128)(2,1)} %bitcast.6), calls=%async_computation.1 | async-start | bytes 131072 | tf_op jit(solution)/shard_map/all_to_all | solution.py:535
  34.2 0.0 copy-start.5
  34.2 0.0 copy-start.6
  34.2 0.0 copy-start.7
  34.2 3.8 %pointwise.5.point1_ref = bf16[64,128,128]{2,1,0:T(8,128)(2,1)} custom-call(bf16[64,64]{1,0:T(8,128)(2,1)S(1)} %copy-done.4, bf16[512,64]{1,0:T(8,128)(2,1)S(1)} %copy-done.1, f32[1,64]{1,0:T(1,128)S(1)} %bitcast.20, bf16[128,128,128]{2,1,0:T(8,128)(2,1)} %bitcast.23), custom_call_target="tpu_custom_call" | custom-call | flops 1073741824 | bytes 4194304 | tf_op jit(solution)/shard_map/pointwise/pallas_call | solution.py:487
  38.0 7.0 %all-to-all-done.1 = bf16[64,4,128]{2,1,0:T(4,128)(2,1)S(1)} async-done(((bf16[64,4,128]{2,1,0:T(4,128)(2,1)}), bf16[64,4,128]{2,1,0:T(4,128)(2,1)S(1)}, u32[]{:S(2)}, u32[]{:S(2)}) %all-to-all-start.1) | async-done | bytes 65568 | tf_op jit(solution)/shard_map/all_to_all | solution.py:535
  45.0 5.6 %slopes.1 = (bf16[128,128,128]{2,1,0:T(8,128)(2,1)}, bf16[256,128]{1,0:T(8,128)(2,1)}) custom-call(bf16[256,128]{1,0:T(8,128)(2,1)S(1)} %bitcast.16, bf16[16,128]{1,0:T(8,128)(2,1)S(1)} %copy-done.6, bf16[128,32]{1,0:T(8,128)(2,1)S(1)} %copy-done.5, bf16[32,256]{1,0:T(8,128)(2,1)S(1)} %copy-done.7, ...), custom_call_target="tpu_custom_call" | custom-call | flops 536870912 | bytes 12582912 | tf_op jit(solution)/shard_map/slopes/pallas_call | solution.py:446
  50.6 4.8 %all-to-all-start.2 = ((bf16[64,4,128]{2,1,0:T(4,128)(2,1)}), bf16[64,4,128]{2,1,0:T(4,128)(2,1)S(1)}, u32[]{:S(2)}, u32[]{:S(2)}) async-start(bf16[64,4,128]{2,1,0:T(4,128)(2,1)} %bitcast.27), calls=%async_computation.2 | async-start | bytes 131072 | tf_op jit(solution)/shard_map/all_to_all | solution.py:535
  55.4 3.8 %pointwise.6 = (bf16[64,128,128]{2,1,0:T(8,128)(2,1)}, bf16[32,128,128]{2,1,0:T(8,128)(2,1)S(1)}, bf16[512,512]{1,0:T(8,128)(2,1)S(1)}) custom-call(bf16[64,64]{1,0:T(8,128)(2,1)S(1)} %copy-done.4, bf16[512,64]{1,0:T(8,128)(2,1)S(1)} %copy-done.1, bf16[128,128,128]{2,1,0:T(8,128)(2,1)} %get-tuple-element.48.refs_2_.refs_1_), custom_call_target="tpu_custom_call" | custom-call | flops 1073741824 | bytes 4194304 | tf_op jit(solution)/shard_map/pointwise/pallas_call | solution.py:499
  59.3 6.7 %all-to-all-done.2 = bf16[64,4,128]{2,1,0:T(4,128)(2,1)S(1)} async-done(((bf16[64,4,128]{2,1,0:T(4,128)(2,1)}), bf16[64,4,128]{2,1,0:T(4,128)(2,1)S(1)}, u32[]{:S(2)}, u32[]{:S(2)}) %all-to-all-start.2) | async-done | bytes 65568 | tf_op jit(solution)/shard_map/all_to_all | solution.py:535
  66.0 1.5 %mix_back.1 = (bf16[256,128]{1,0:T(8,128)(2,1)}, bf16[64,128]{1,0:T(8,128)(2,1)S(1)}) custom-call(bf16[256,128]{1,0:T(8,128)(2,1)S(1)} %bitcast.17, bf16[2,128,256]{2,1,0:T(8,128)(2,1)S(1)} %copy-done.3, bf16[2,256,128]{2,1,0:T(8,128)(2,1)S(1)} %copy-done.2, bf16[4,1024,64]{2,1,0:T(8,128)(2,1)S(1)} %bitcast.14, ...), custom_call_target="tpu_custom_call" | custom-call | flops 134217728 | bytes 2097152 | tf_op jit(solution)/shard_map/mix_back/pallas_call | solution.py:522
  67.5 4.6 %all-to-all-start.3 = ((bf16[64,4,128]{2,1,0:T(4,128)(2,1)}), bf16[64,4,128]{2,1,0:T(4,128)(2,1)S(1)}, u32[]{:S(2)}, u32[]{:S(2)}) async-start(bf16[64,4,128]{2,1,0:T(4,128)(2,1)} %bitcast.10), calls=%async_computation.3 | async-start | bytes 131072 | tf_op jit(solution)/shard_map/all_to_all | solution.py:535
  72.2 0.1 collective-permute-start.2
  72.3 0.8 collective-permute-start.1
  73.0 2.9 %collective-permute-start = (bf16[64,128]{1,0:T(8,128)(2,1)S(1)}, bf16[64,128]{1,0:T(8,128)(2,1)S(1)}, u32[]{:S(2)}, u32[]{:S(2)}) collective-permute-start(bf16[64,128]{1,0:T(8,128)(2,1)S(1)} %get-tuple-element.45.both0_ref), channel_id=1, source_target_pairs={{0,128},{64,192},{128,0},{192,64},{1,129},{65,193},{129,1},{193,65... | collective-permute-start | bytes 49160 | tf_op jit(solution)/shard_map/ppermute | solution.py:539
  75.9 3.9 %pointwise.7 = (bf16[64,128,128]{2,1,0:T(8,128)(2,1)}, bf16[48,128,128]{2,1,0:T(8,128)(2,1)S(1)}) custom-call(bf16[512,512]{1,0:T(8,128)(2,1)S(1)} %get-tuple-element.47.refs_0_, bf16[128,128,128]{2,1,0:T(8,128)(2,1)} %get-tuple-element.48.refs_2_.refs_1_), custom_call_target="tpu_custom_call" | custom-call | flops 1073741824 | bytes 4194304 | tf_op jit(solution)/shard_map/pointwise/pallas_call | solution.py:499
  79.8 0.0 collective-permute-done.2.both3_ref
  79.8 0.0 collective-permute-done.1.both2_ref
  79.8 0.0 collective-permute-done.both1_ref
  79.8 3.1 %all-to-all-done.3 = bf16[64,4,128]{2,1,0:T(4,128)(2,1)S(1)} async-done(((bf16[64,4,128]{2,1,0:T(4,128)(2,1)}), bf16[64,4,128]{2,1,0:T(4,128)(2,1)S(1)}, u32[]{:S(2)}, u32[]{:S(2)}) %all-to-all-start.3) | async-done | bytes 65568 | tf_op jit(solution)/shard_map/all_to_all | solution.py:535
  82.9 3.5 %result.1 = (bf16[128,128,128]{2,1,0:T(8,128)(2,1)}, f32[4,4,64,64]{3,2,1,0:T(8,128)}) custom-call(bf16[256,128]{1,0:T(8,128)(2,1)S(1)} %bitcast.15, bf16[16,128]{1,0:T(8,128)(2,1)S(1)} %copy-done.6, bf16[128,32]{1,0:T(8,128)(2,1)S(1)} %copy-done.5, bf16[64,128]{1,0:T(8,128)(2,1)S(1)} %get-tuple-element.45.both0_ref, ...), custom_call_target="tpu_custom_call" | custom-call | flops 268435456 | bytes 8388608 | tf_op jit(solution)/shard_map/result/pallas_call | solution.py:463
  (9 shorter events, 0.0 us)
Async XLA Ops:
  0.6 16.5 %copy-start.1 = (bf16[512,64]{1,0:T(8,128)(2,1)S(1)}, bf16[512,64]{1,0:T(8,128)(2,1)}, u32[]{:S(2)}) copy-start(bf16[512,64]{1,0:T(8,128)(2,1)} %constant.16.clone.spread_ref.refs_1_) | copy-start | bytes 196612
  0.6 16.5 %copy-start.4 = (bf16[64,64]{1,0:T(8,128)(2,1)S(1)}, bf16[64,64]{1,0:T(8,128)(2,1)}, u32[]{:S(2)}) copy-start(bf16[64,64]{1,0:T(8,128)(2,1)} %refs_0_.1) | copy-start | bytes 24580
  0.7 16.5 %copy-start.8 = (f32[64]{0:T(128)S(1)}, f32[64]{0:T(128)}, u32[]{:S(2)}) copy-start(f32[64]{0:T(128)} %param.16) | copy-start | bytes 772
  4.5 23.4 %all-to-all-start = ((bf16[64,4,128]{2,1,0:T(4,128)(2,1)}), bf16[64,4,128]{2,1,0:T(4,128)(2,1)S(1)}, u32[]{:S(2)}, u32[]{:S(2)}) async-start(bf16[64,4,128]{2,1,0:T(4,128)(2,1)} %bitcast.26), calls=%async_computation | async-start | bytes 131072 | tf_op jit(solution)/shard_map/all_to_all | solution.py:535
  17.2 10.7 %copy-start = (bf16[4,16,64,64]{3,2,1,0:T(8,128)(2,1)S(1)}, bf16[4,16,64,64]{3,2,1,0:T(8,128)(2,1)}, u32[]{:S(2)}) copy-start(bf16[4,16,64,64]{3,2,1,0:T(8,128)(2,1)} %param.14) | copy-start | bytes 1572868
  17.2 10.7 %copy-start.2 = (bf16[2,256,128]{2,1,0:T(8,128)(2,1)S(1)}, bf16[2,256,128]{2,1,0:T(8,128)(2,1)}, u32[]{:S(2)}) copy-start(bf16[2,256,128]{2,1,0:T(8,128)(2,1)} %constant.20.clone.back_x_ref) | copy-start | bytes 393220
  17.2 10.7 %copy-start.3 = (bf16[2,128,256]{2,1,0:T(8,128)(2,1)S(1)}, bf16[2,128,256]{2,1,0:T(8,128)(2,1)}, u32[]{:S(2)}) copy-start(bf16[2,128,256]{2,1,0:T(8,128)(2,1)} %constant.19.clone.along_x_ref) | copy-start | bytes 393220
  29.3 15.6 %all-to-all-start.1 = ((bf16[64,4,128]{2,1,0:T(4,128)(2,1)}), bf16[64,4,128]{2,1,0:T(4,128)(2,1)S(1)}, u32[]{:S(2)}, u32[]{:S(2)}) async-start(bf16[64,4,128]{2,1,0:T(4,128)(2,1)} %bitcast.6), calls=%async_computation.1 | async-start | bytes 131072 | tf_op jit(solution)/shard_map/all_to_all | solution.py:535
  34.2 10.8 %copy-start.5 = (bf16[128,32]{1,0:T(8,128)(2,1)S(1)}, bf16[128,32]{1,0:T(8,128)(2,1)}, u32[]{:S(2)}) copy-start(bf16[128,32]{1,0:T(8,128)(2,1)} %constant.17.clone.back_y_ref) | copy-start | bytes 24580
  34.2 10.8 %copy-start.6 = (bf16[16,128]{1,0:T(8,128)(2,1)S(1)}, bf16[16,128]{1,0:T(8,128)(2,1)}, u32[]{:S(2)}) copy-start(bf16[16,128]{1,0:T(8,128)(2,1)} %constant.18.clone.forward_z_ref.table_z_ref) | copy-start | bytes 12292
  34.2 10.8 %copy-start.7 = (bf16[32,256]{1,0:T(8,128)(2,1)S(1)}, bf16[32,256]{1,0:T(8,128)(2,1)}, u32[]{:S(2)}) copy-start(bf16[32,256]{1,0:T(8,128)(2,1)} %constant.15.clone.forward_y_ref) | copy-start | bytes 49156
  50.6 15.4 %all-to-all-start.2 = ((bf16[64,4,128]{2,1,0:T(4,128)(2,1)}), bf16[64,4,128]{2,1,0:T(4,128)(2,1)S(1)}, u32[]{:S(2)}, u32[]{:S(2)}) async-start(bf16[64,4,128]{2,1,0:T(4,128)(2,1)} %bitcast.27), calls=%async_computation.2 | async-start | bytes 131072 | tf_op jit(solution)/shard_map/all_to_all | solution.py:535
  67.5 15.4 %all-to-all-start.3 = ((bf16[64,4,128]{2,1,0:T(4,128)(2,1)}), bf16[64,4,128]{2,1,0:T(4,128)(2,1)S(1)}, u32[]{:S(2)}, u32[]{:S(2)}) async-start(bf16[64,4,128]{2,1,0:T(4,128)(2,1)} %bitcast.10), calls=%async_computation.3 | async-start | bytes 131072 | tf_op jit(solution)/shard_map/all_to_all | solution.py:535
  72.2 7.6 %collective-permute-start.2 = (bf16[64,128]{1,0:T(8,128)(2,1)S(1)}, bf16[64,128]{1,0:T(8,128)(2,1)S(1)}, u32[]{:S(2)}, u32[]{:S(2)}) collective-permute-start(bf16[64,128]{1,0:T(8,128)(2,1)S(1)} %get-tuple-element.45.both0_ref), channel_id=1, source_target_pairs={{0,64},{64,0},{128,192},{192,128},{1,65},{65,1},{129,193},{193,129... | collective-permute-start | bytes 49160 | tf_op jit(solution)/shard_map/ppermute | solution.py:539
  72.3 7.5 %collective-permute-start.1 = (bf16[64,128]{1,0:T(8,128)(2,1)S(1)}, bf16[64,128]{1,0:T(8,128)(2,1)S(1)}, u32[]{:S(2)}, u32[]{:S(2)}) collective-permute-start(bf16[64,128]{1,0:T(8,128)(2,1)S(1)} %get-tuple-element.45.both0_ref), channel_id=1, source_target_pairs={{0,192},{64,128},{128,64},{192,0},{1,193},{65,129},{129,65},{193,1... | collective-permute-start | bytes 49160 | tf_op jit(solution)/shard_map/ppermute | solution.py:539
  73.0 6.8 %collective-permute-start = (bf16[64,128]{1,0:T(8,128)(2,1)S(1)}, bf16[64,128]{1,0:T(8,128)(2,1)S(1)}, u32[]{:S(2)}, u32[]{:S(2)}) collective-permute-start(bf16[64,128]{1,0:T(8,128)(2,1)S(1)} %get-tuple-element.45.both0_ref), channel_id=1, source_target_pairs={{0,128},{64,192},{128,0},{192,64},{1,129},{65,193},{129,1},{193,65... | collective-permute-start | bytes 49160 | tf_op jit(solution)/shard_map/ppermute | solution.py:539

commit v7 on v6

--- a/solution.py
+++ b/solution.py
@@ -53,7 +53,7 @@
         back_y=back_y.astype(BF),
         forward_z=np.ascontiguousarray(table_z.T),
         along_x=np.stack(split(along_x)),
-        back_x=np.stack(split(np.ascontiguousarray(along_x.T))),
+        back_x=np.ascontiguousarray(along_x.T).astype(BF),
     )
 
 
@@ -350,9 +350,7 @@
     lane = lax.broadcasted_iota(jnp.int32, (OWN * M, XC), 1)
     stacked = jnp.concatenate([jnp.where(lane < C, twice, 0.0), jnp.where(lane < C, 0.0, twice)], axis=0)
     stacked = stacked.astype(BF)
-    return jnp.dot(back_x[0], stacked, preferred_element_type=F32) + jnp.dot(
-        back_x[1], stacked, preferred_element_type=F32
-    )
+    return jnp.dot(back_x, stacked, preferred_element_type=F32)
 
 
 def mix_kernel(received_ref, along_x_ref, back_x_ref, weight_ref, out_ref, spectrum_ref):

time: 86.9 us -> 86.8 us (level)
  no operation moved by 1% of the time
where the time goes in v7:
time: 86.8 us; the launch traced here: 86.4 us
  Pallas kernels  31.4 us (36%)
  starting transfers between devices  30.7 us (35%)
  waiting for transfers between devices  23.3 us (27%)
  between operations  1.01 us (1%)
    all_to_all x4, starting transfers between devices, exchange(): lax.all_to_all(cut, 'space', split_axis=0, concat_axis=0, tiled=True)  26.9 us
    all_to_all x4, waiting for transfers between devices, exchange(): lax.all_to_all(cut, 'space', split_axis=0, concat_axis=0, tiled=True)  23.3 us
    pallas_call x2, Pallas kernels, pointwise(): pl.pallas_call(functools.partial(point_kernel, plane), in_specs=[SMALL] *...  7.98 us
    pallas_call x2, Pallas kernels, pointwise_back(): pl.pallas_call(functools.partial(point_back_kernel, plane), in_specs=[SMA...  7.69 us
    pallas_call x1, Pallas kernels, slopes(): pl.pallas_call(slope_kernel, in_specs=[SMALL] * 6 + [LARGE] * 3, out_spec...  5.65 us
    pallas_call x1, Pallas kernels, to_modes(): pl.pallas_call(to_modes_kernel, in_specs=[LARGE] * 3, out_specs=LARGE, ou...  3.81 us
    ppermute x3, starting transfers between devices, over_samples(): lax.ppermute(both, 'dp', [(i, i ^ k) for i in range(4)])  3.74 us
    pallas_call x1, Pallas kernels, result(): pl.pallas_call(result_kernel, in_specs=[SMALL] * 9 + [LARGE] * 2, out_spe...  3.46 us
  transfers between devices with their start and end apart: 7, of which 4 were waited for; matrix products, arithmetic and copies ran while one was open for 0% of the time, Pallas kernels for 18%

profile of v7, /device:TPU:16, one launch (start us, length us, event | category | flops | bytes accessed | tf_op | source)
XLA Modules:
  0.0 86.4 jit_solution(9088074815064162282)
XLA Ops:
  0.6 0.0 copy-start.1
  0.7 3.8 %to_modes.1 = bf16[256,128]{1,0:T(8,128)(2,1)} custom-call(bf16[128,128,128]{2,1,0:T(8,128)(2,1)} %bitcast.21, bf16[32,256]{1,0:T(8,128)(2,1)} %constant.14.clone.forward_y_ref, bf16[16,128]{1,0:T(8,128)(2,1)} %constant.18.clone.forward_z_ref.table_z_ref), custom_call_target="tpu_custom_call" | custom-call | flops 268435456 | bytes 4194304 | tf_op jit(solution)/shard_map/to_modes/pallas_call | solution.py:428
  4.5 12.7 %all-to-all-start = ((bf16[64,4,128]{2,1,0:T(4,128)(2,1)}), bf16[64,4,128]{2,1,0:T(4,128)(2,1)S(1)}, u32[]{:S(2)}, u32[]{:S(2)}) async-start(bf16[64,4,128]{2,1,0:T(4,128)(2,1)} %bitcast.26), calls=%async_computation | async-start | bytes 131072 | tf_op jit(solution)/shard_map/all_to_all | solution.py:533
  17.2 0.0 copy-done.1
  17.2 0.0 copy-done.4
  17.2 0.0 copy-start
  17.2 0.0 copy-start.2
  17.2 0.0 copy-start.3
  17.2 4.2 %pointwise.4 = (bf16[64,128,128]{2,1,0:T(8,128)(2,1)}, bf16[16,128,128]{2,1,0:T(8,128)(2,1)S(1)}, bf16[16,128,128]{2,1,0:T(8,128)(2,1)S(1)}) custom-call(bf16[64,64]{1,0:T(8,128)(2,1)S(1)} %copy-done.4, bf16[512,64]{1,0:T(8,128)(2,1)S(1)} %copy-done.1, f32[1,64]{1,0:T(1,128)S(1)} %bitcast.19, bf16[128,128,128]{2,1,0:T(8,128)(2,1)} %bitcast.24, ...), custom_call_target="tpu_custom_call" | custom-call | flops 1073741824 | bytes 4194304 | tf_op jit(solution)/shard_map/pointwise/pallas_call | solution.py:485
  21.4 6.5 %all-to-all-done = bf16[64,4,128]{2,1,0:T(4,128)(2,1)S(1)} async-done(((bf16[64,4,128]{2,1,0:T(4,128)(2,1)}), bf16[64,4,128]{2,1,0:T(4,128)(2,1)S(1)}, u32[]{:S(2)}, u32[]{:S(2)}) %all-to-all-start) | async-done | bytes 65568 | tf_op jit(solution)/shard_map/all_to_all | solution.py:533
  27.9 1.3 %mix.1 = (bf16[256,128]{1,0:T(8,128)(2,1)}, bf16[64,128]{1,0:T(8,128)(2,1)S(1)}) custom-call(bf16[256,128]{1,0:T(8,128)(2,1)S(1)} %bitcast.17, bf16[2,128,256]{2,1,0:T(8,128)(2,1)S(1)} %copy-done.2, bf16[256,128]{1,0:T(8,128)(2,1)S(1)} %copy-done.3, bf16[4,1024,64]{2,1,0:T(8,128)(2,1)S(1)} %bitcast.13), custom_call_target="tpu_custom_call" | custom-call | flops 134217728 | bytes 2097152 | tf_op jit(solution)/shard_map/mix/pallas_call | solution.py:508
  29.3 4.8 %all-to-all-start.1 = ((bf16[64,4,128]{2,1,0:T(4,128)(2,1)}), bf16[64,4,128]{2,1,0:T(4,128)(2,1)S(1)}, u32[]{:S(2)}, u32[]{:S(2)}) async-start(bf16[64,4,128]{2,1,0:T(4,128)(2,1)} %bitcast.6), calls=%async_computation.1 | async-start | bytes 131072 | tf_op jit(solution)/shard_map/all_to_all | solution.py:533
  34.1 0.0 copy-start.5
  34.1 0.0 copy-start.6
  34.1 0.0 copy-start.7
  34.2 3.8 %pointwise.5.point1_ref = bf16[64,128,128]{2,1,0:T(8,128)(2,1)} custom-call(bf16[64,64]{1,0:T(8,128)(2,1)S(1)} %copy-done.4, bf16[512,64]{1,0:T(8,128)(2,1)S(1)} %copy-done.1, f32[1,64]{1,0:T(1,128)S(1)} %bitcast.20, bf16[128,128,128]{2,1,0:T(8,128)(2,1)} %bitcast.23), custom_call_target="tpu_custom_call" | custom-call | flops 1073741824 | bytes 4194304 | tf_op jit(solution)/shard_map/pointwise/pallas_call | solution.py:485
  37.9 7.0 %all-to-all-done.1 = bf16[64,4,128]{2,1,0:T(4,128)(2,1)S(1)} async-done(((bf16[64,4,128]{2,1,0:T(4,128)(2,1)}), bf16[64,4,128]{2,1,0:T(4,128)(2,1)S(1)}, u32[]{:S(2)}, u32[]{:S(2)}) %all-to-all-start.1) | async-done | bytes 65568 | tf_op jit(solution)/shard_map/all_to_all | solution.py:533
  44.9 5.6 %slopes.1 = (bf16[128,128,128]{2,1,0:T(8,128)(2,1)}, bf16[256,128]{1,0:T(8,128)(2,1)}) custom-call(bf16[256,128]{1,0:T(8,128)(2,1)S(1)} %bitcast.16, bf16[16,128]{1,0:T(8,128)(2,1)S(1)} %copy-done.6, bf16[128,32]{1,0:T(8,128)(2,1)S(1)} %copy-done.5, bf16[32,256]{1,0:T(8,128)(2,1)S(1)} %copy-done.7, ...), custom_call_target="tpu_custom_call" | custom-call | flops 536870912 | bytes 12582912 | tf_op jit(solution)/shard_map/slopes/pallas_call | solution.py:444
  50.6 4.8 %all-to-all-start.2 = ((bf16[64,4,128]{2,1,0:T(4,128)(2,1)}), bf16[64,4,128]{2,1,0:T(4,128)(2,1)S(1)}, u32[]{:S(2)}, u32[]{:S(2)}) async-start(bf16[64,4,128]{2,1,0:T(4,128)(2,1)} %bitcast.27), calls=%async_computation.2 | async-start | bytes 131072 | tf_op jit(solution)/shard_map/all_to_all | solution.py:533
  55.4 3.8 %pointwise.6 = (bf16[64,128,128]{2,1,0:T(8,128)(2,1)}, bf16[32,128,128]{2,1,0:T(8,128)(2,1)S(1)}, bf16[512,512]{1,0:T(8,128)(2,1)S(1)}) custom-call(bf16[64,64]{1,0:T(8,128)(2,1)S(1)} %copy-done.4, bf16[512,64]{1,0:T(8,128)(2,1)S(1)} %copy-done.1, bf16[128,128,128]{2,1,0:T(8,128)(2,1)} %get-tuple-element.48.refs_2_.refs_1_), custom_call_target="tpu_custom_call" | custom-call | flops 1073741824 | bytes 4194304 | tf_op jit(solution)/shard_map/pointwise/pallas_call | solution.py:497
  59.2 6.7 %all-to-all-done.2 = bf16[64,4,128]{2,1,0:T(4,128)(2,1)S(1)} async-done(((bf16[64,4,128]{2,1,0:T(4,128)(2,1)}), bf16[64,4,128]{2,1,0:T(4,128)(2,1)S(1)}, u32[]{:S(2)}, u32[]{:S(2)}) %all-to-all-start.2) | async-done | bytes 65568 | tf_op jit(solution)/shard_map/all_to_all | solution.py:533
  66.0 1.4 %mix_back.1 = (bf16[256,128]{1,0:T(8,128)(2,1)}, bf16[64,128]{1,0:T(8,128)(2,1)S(1)}) custom-call(bf16[256,128]{1,0:T(8,128)(2,1)S(1)} %bitcast.18, bf16[2,128,256]{2,1,0:T(8,128)(2,1)S(1)} %copy-done.2, bf16[256,128]{1,0:T(8,128)(2,1)S(1)} %copy-done.3, bf16[4,1024,64]{2,1,0:T(8,128)(2,1)S(1)} %bitcast.14, bf16[64,128]{1,0:T(8,128)(2,1)S(1)} %get-tuple-element.42.spectrum_ref), custom_call_target="tpu_custom_call" | custom-call | flops 134217728 | bytes 2097152 | tf_op jit(solution)/shard_map/mix_back/pallas_call | solution.py:520
  67.4 4.6 %all-to-all-start.3 = ((bf16[64,4,128]{2,1,0:T(4,128)(2,1)}), bf16[64,4,128]{2,1,0:T(4,128)(2,1)S(1)}, u32[]{:S(2)}, u32[]{:S(2)}) async-start(bf16[64,4,128]{2,1,0:T(4,128)(2,1)} %bitcast.10), calls=%async_computation.3 | async-start | bytes 131072 | tf_op jit(solution)/shard_map/all_to_all | solution.py:533
  72.0 0.1 collective-permute-start.2
  72.1 0.8 collective-permute-start.1
  72.9 2.9 %collective-permute-start = (bf16[64,128]{1,0:T(8,128)(2,1)S(1)}, bf16[64,128]{1,0:T(8,128)(2,1)S(1)}, u32[]{:S(2)}, u32[]{:S(2)}) collective-permute-start(bf16[64,128]{1,0:T(8,128)(2,1)S(1)} %get-tuple-element.45.both0_ref), channel_id=1, source_target_pairs={{0,128},{64,192},{128,0},{192,64},{1,129},{65,193},{129,1},{193,65... | collective-permute-start | bytes 49160 | tf_op jit(solution)/shard_map/ppermute | solution.py:537
  75.8 3.9 %pointwise.7 = (bf16[64,128,128]{2,1,0:T(8,128)(2,1)}, bf16[48,128,128]{2,1,0:T(8,128)(2,1)S(1)}) custom-call(bf16[512,512]{1,0:T(8,128)(2,1)S(1)} %get-tuple-element.47.refs_0_, bf16[128,128,128]{2,1,0:T(8,128)(2,1)} %get-tuple-element.48.refs_2_.refs_1_), custom_call_target="tpu_custom_call" | custom-call | flops 1073741824 | bytes 4194304 | tf_op jit(solution)/shard_map/pointwise/pallas_call | solution.py:497
  79.7 0.0 collective-permute-done.2.both3_ref
  79.7 0.0 collective-permute-done.1.both2_ref
  79.7 0.0 collective-permute-done.both1_ref
  79.7 3.1 %all-to-all-done.3 = bf16[64,4,128]{2,1,0:T(4,128)(2,1)S(1)} async-done(((bf16[64,4,128]{2,1,0:T(4,128)(2,1)}), bf16[64,4,128]{2,1,0:T(4,128)(2,1)S(1)}, u32[]{:S(2)}, u32[]{:S(2)}) %all-to-all-start.3) | async-done | bytes 65568 | tf_op jit(solution)/shard_map/all_to_all | solution.py:533
  82.8 3.5 %result.1 = (bf16[128,128,128]{2,1,0:T(8,128)(2,1)}, f32[4,4,64,64]{3,2,1,0:T(8,128)}) custom-call(bf16[256,128]{1,0:T(8,128)(2,1)S(1)} %bitcast.15, bf16[16,128]{1,0:T(8,128)(2,1)S(1)} %copy-done.6, bf16[128,32]{1,0:T(8,128)(2,1)S(1)} %copy-done.5, bf16[64,128]{1,0:T(8,128)(2,1)S(1)} %get-tuple-element.45.both0_ref, ...), custom_call_target="tpu_custom_call" | custom-call | flops 268435456 | bytes 8388608 | tf_op jit(solution)/shard_map/result/pallas_call | solution.py:461
  (9 shorter events, 0.0 us)
Async XLA Ops:
  0.6 16.5 %copy-start.1 = (bf16[512,64]{1,0:T(8,128)(2,1)S(1)}, bf16[512,64]{1,0:T(8,128)(2,1)}, u32[]{:S(2)}) copy-start(bf16[512,64]{1,0:T(8,128)(2,1)} %constant.16.clone.spread_ref.refs_1_) | copy-start | bytes 196612
  0.6 16.5 %copy-start.4 = (bf16[64,64]{1,0:T(8,128)(2,1)S(1)}, bf16[64,64]{1,0:T(8,128)(2,1)}, u32[]{:S(2)}) copy-start(bf16[64,64]{1,0:T(8,128)(2,1)} %refs_0_.1) | copy-start | bytes 24580
  0.7 16.5 %copy-start.8 = (f32[64]{0:T(128)S(1)}, f32[64]{0:T(128)}, u32[]{:S(2)}) copy-start(f32[64]{0:T(128)} %param.16) | copy-start | bytes 772
  4.5 23.4 %all-to-all-start = ((bf16[64,4,128]{2,1,0:T(4,128)(2,1)}), bf16[64,4,128]{2,1,0:T(4,128)(2,1)S(1)}, u32[]{:S(2)}, u32[]{:S(2)}) async-start(bf16[64,4,128]{2,1,0:T(4,128)(2,1)} %bitcast.26), calls=%async_computation | async-start | bytes 131072 | tf_op jit(solution)/shard_map/all_to_all | solution.py:533
  17.2 10.7 %copy-start = (bf16[4,16,64,64]{3,2,1,0:T(8,128)(2,1)S(1)}, bf16[4,16,64,64]{3,2,1,0:T(8,128)(2,1)}, u32[]{:S(2)}) copy-start(bf16[4,16,64,64]{3,2,1,0:T(8,128)(2,1)} %param.14) | copy-start | bytes 1572868
  17.2 10.7 %copy-start.2 = (bf16[2,128,256]{2,1,0:T(8,128)(2,1)S(1)}, bf16[2,128,256]{2,1,0:T(8,128)(2,1)}, u32[]{:S(2)}) copy-start(bf16[2,128,256]{2,1,0:T(8,128)(2,1)} %constant.19.clone.along_x_ref) | copy-start | bytes 393220
  17.2 10.7 %copy-start.3 = (bf16[256,128]{1,0:T(8,128)(2,1)S(1)}, bf16[256,128]{1,0:T(8,128)(2,1)}, u32[]{:S(2)}) copy-start(bf16[256,128]{1,0:T(8,128)(2,1)} %constant.20.clone.back_x_ref) | copy-start | bytes 196612
  29.3 15.6 %all-to-all-start.1 = ((bf16[64,4,128]{2,1,0:T(4,128)(2,1)}), bf16[64,4,128]{2,1,0:T(4,128)(2,1)S(1)}, u32[]{:S(2)}, u32[]{:S(2)}) async-start(bf16[64,4,128]{2,1,0:T(4,128)(2,1)} %bitcast.6), calls=%async_computation.1 | async-start | bytes 131072 | tf_op jit(solution)/shard_map/all_to_all | solution.py:533
  34.1 10.8 %copy-start.5 = (bf16[128,32]{1,0:T(8,128)(2,1)S(1)}, bf16[128,32]{1,0:T(8,128)(2,1)}, u32[]{:S(2)}) copy-start(bf16[128,32]{1,0:T(8,128)(2,1)} %constant.17.clone.back_y_ref) | copy-start | bytes 24580
  34.1 10.8 %copy-start.6 = (bf16[16,128]{1,0:T(8,128)(2,1)S(1)}, bf16[16,128]{1,0:T(8,128)(2,1)}, u32[]{:S(2)}) copy-start(bf16[16,128]{1,0:T(8,128)(2,1)} %constant.18.clone.forward_z_ref.table_z_ref) | copy-start | bytes 12292
  34.1 10.8 %copy-start.7 = (bf16[32,256]{1,0:T(8,128)(2,1)S(1)}, bf16[32,256]{1,0:T(8,128)(2,1)}, u32[]{:S(2)}) copy-start(bf16[32,256]{1,0:T(8,128)(2,1)} %constant.15.clone.forward_y_ref) | copy-start | bytes 49156
  50.6 15.4 %all-to-all-start.2 = ((bf16[64,4,128]{2,1,0:T(4,128)(2,1)}), bf16[64,4,128]{2,1,0:T(4,128)(2,1)S(1)}, u32[]{:S(2)}, u32[]{:S(2)}) async-start(bf16[64,4,128]{2,1,0:T(4,128)(2,1)} %bitcast.27), calls=%async_computation.2 | async-start | bytes 131072 | tf_op jit(solution)/shard_map/all_to_all | solution.py:533
  67.4 15.4 %all-to-all-start.3 = ((bf16[64,4,128]{2,1,0:T(4,128)(2,1)}), bf16[64,4,128]{2,1,0:T(4,128)(2,1)S(1)}, u32[]{:S(2)}, u32[]{:S(2)}) async-start(bf16[64,4,128]{2,1,0:T(4,128)(2,1)} %bitcast.10), calls=%async_computation.3 | async-start | bytes 131072 | tf_op jit(solution)/shard_map/all_to_all | solution.py:533
  72.0 7.6 %collective-permute-start.2 = (bf16[64,128]{1,0:T(8,128)(2,1)S(1)}, bf16[64,128]{1,0:T(8,128)(2,1)S(1)}, u32[]{:S(2)}, u32[]{:S(2)}) collective-permute-start(bf16[64,128]{1,0:T(8,128)(2,1)S(1)} %get-tuple-element.45.both0_ref), channel_id=1, source_target_pairs={{0,64},{64,0},{128,192},{192,128},{1,65},{65,1},{129,193},{193,129... | collective-permute-start | bytes 49160 | tf_op jit(solution)/shard_map/ppermute | solution.py:537
  72.1 7.5 %collective-permute-start.1 = (bf16[64,128]{1,0:T(8,128)(2,1)S(1)}, bf16[64,128]{1,0:T(8,128)(2,1)S(1)}, u32[]{:S(2)}, u32[]{:S(2)}) collective-permute-start(bf16[64,128]{1,0:T(8,128)(2,1)S(1)} %get-tuple-element.45.both0_ref), channel_id=1, source_target_pairs={{0,192},{64,128},{128,64},{192,0},{1,193},{65,129},{129,65},{193,1... | collective-permute-start | bytes 49160 | tf_op jit(solution)/shard_map/ppermute | solution.py:537
  72.9 6.8 %collective-permute-start = (bf16[64,128]{1,0:T(8,128)(2,1)S(1)}, bf16[64,128]{1,0:T(8,128)(2,1)S(1)}, u32[]{:S(2)}, u32[]{:S(2)}) collective-permute-start(bf16[64,128]{1,0:T(8,128)(2,1)S(1)} %get-tuple-element.45.both0_ref), channel_id=1, source_target_pairs={{0,128},{64,192},{128,0},{192,64},{1,129},{65,193},{129,1},{193,65... | collective-permute-start | bytes 49160 | tf_op jit(solution)/shard_map/ppermute | solution.py:537
